TPU v7x, 32 devices: a whole 2x2x4 slice. The times are simulated.
32 devices in a mesh: seq: 4 (over x, core), grp: 4 (over z), head: 2 (over y).
Axes of the slice: x: 2, y: 2, z: 4, core: 2. Of those that a mesh axis runs over, the one named last changes fastest.
Arguments:
- query_feat: bfloat16 [4, 4, 512, 6144], P('grp', 'seq', None, 'head'), may hold values from -6 to 6
- key_feat: bfloat16 [4, 4, 512, 6144], P('grp', 'seq', None, 'head'), may hold values from -6 to 6
- value_feat: bfloat16 [4, 4, 512, 6144], P('grp', 'seq', None, 'head'), may hold values from -6 to 6
- norm_gain: float32 [6144], P('head'), may hold values from 0.5 to 1.5
Outputs:
- attended: bfloat16 [4, 4, 512, 6144], P('grp', 'seq', None, 'head')
All inputs are finite; a program needn't handle non-finite values.
Results may differ from a plain program's by a relative error of at most 0.0049.
Values sent between devices are 32-bit elements; how exact they have to be, the bound alone decides.
No kernel may reach another device: no remote copies, remote signals or barrier semaphores. Data moves between devices by JAX's collectives and lax.ppermute only.
A program may use at most 128 MiB of HBM per device.

v0:
```python
import jax
import jax.numpy as jnp
from jax import lax
from jax.sharding import PartitionSpec as P

DH = 128
BLK = 512


def carried_in(shard, axis, combine, identity):
    count, position = (lax.axis_size(axis), lax.axis_index(axis))
    everything = lax.all_gather(shard, axis)
    start = jnp.broadcast_to(jnp.asarray(identity, shard.dtype), shard.shape)

    def hop(k, before):
        reached = k < position
        new = combine(before, everything[k])
        return jnp.where(reached, new, before)

    return lax.fori_loop(0, count, hop, start)


def add_states(earlier, later):
    return earlier + later


def per_device(query_feat, key_feat, value_feat, norm_gain):
    tokens_here = query_feat.shape[2]
    width = query_feat.shape[3]
    heads_here = width // DH
    nblocks = tokens_here // BLK

    def split(array):
        return array.reshape(nblocks, BLK, heads_here, DH)

    queries = split(query_feat)
    keys_all = split(key_feat)
    values = split(value_feat)
    block_sums = jnp.einsum("bthd,bthe->bhde", keys_all, values, preferred_element_type=jnp.float32)
    local_total = jnp.sum(block_sums, axis=0)
    running = jnp.cumsum(block_sums, axis=0)
    earlier_blocks = jnp.concatenate([jnp.zeros_like(block_sums), running[:-1]], axis=0)
    zero_state = jnp.zeros_like(local_total)
    gathered = lax.all_gather(local_total[None], "seq", axis=0, tiled=True)
    position = lax.axis_index("seq")
    lower = (lax.broadcasted_iota(jnp.int32, (gathered.shape[0],), 0) < position).astype(
        jnp.float32
    )
    within = jnp.einsum("j,jhde->hde", lower, gathered, precision=lax.Precision.HIGHEST)
    group_total = jnp.sum(gathered, axis=0)
    before = carried_in(group_total, "grp", add_states, zero_state)
    incoming = before + within
    starts = (incoming[None] + earlier_blocks).astype(jnp.bfloat16)
    rows = lax.broadcasted_iota(jnp.int32, (BLK, BLK), 0)
    columns = lax.broadcasted_iota(jnp.int32, (BLK, BLK), 1)
    causal = rows >= columns
    scores = jnp.einsum("bthd,bshd->bhts", queries, keys_all, preferred_element_type=jnp.float32)
    weights = jnp.where(causal[None, None], scores, 0.0).astype(jnp.bfloat16)
    mixed = jnp.einsum("bhts,bshe->bthe", weights, values, preferred_element_type=jnp.float32)
    mixed = mixed + jnp.einsum(
        "bthd,bhde->bthe", queries, starts, preferred_element_type=jnp.float32
    )
    meansq = jnp.mean(mixed * mixed, axis=-1, keepdims=True)
    gain = norm_gain.reshape(heads_here, DH)
    result = (mixed * lax.rsqrt(meansq + 1e-05) * gain).astype(jnp.bfloat16)
    return result.reshape(query_feat.shape)


def solution(mesh):
    placed = (
        P("grp", "seq", None, "head"),
        P("grp", "seq", None, "head"),
        P("grp", "seq", None, "head"),
        P("head"),
    )
    return jax.shard_map(
        per_device,
        mesh=mesh,
        in_specs=placed,
        out_specs=P("grp", "seq", None, "head"),
        check_vma=False,
    )
```

profile of v0, /device:TPU:0, one launch (start us, length us, event | category | flops | bytes accessed | tf_op | source)
XLA Modules:
  0.0 211.4 jit_solution(12137355321183506053)
XLA Ops:
  6.5 3.2 %copy.21 = bf16[1,1,512,3072]{2,3,1,0:T(8,128)(2,1)S(1)} copy(bf16[1,1,512,3072]{3,2,1,0:T(8,128)(2,1)} %param.7) | data formatting | bytes 6291456 | tf_op jit(solution)/shard_map/reshape.2
  9.7 3.9 %copy.23 = bf16[64,8,24,128]{3,2,1,0:T(8,128)(2,1)S(1)} copy(bf16[64,8,24,128]{3,1,2,0:T(8,128)(2,1)} %bitcast.56) | data formatting | bytes 6291456
  13.6 1.6 copy-done.1
  15.3 2.2 %fusion.15 = f32[24,128,128]{2,1,0:T(8,128)} fusion(bf16[512,24,128]{0,2,1:T(8,128)(2,1)S(1)} %bitcast.47, bf16[512,24,128]{2,1,0:T(8,128)(2,1)S(1)} %bitcast.49), kind=kOutput, calls=%fused_computation.18 | convolution fusion | flops 402653184 | bytes 7864320 | tf_op jit(solution)/shard_map/bthd,bthe->bhde/dot_general | solution.py:39
  17.5 0.0 all-gather.5.cloned.1.call-update
  17.5 0.0 all-gather.7.cloned.1.call-start
  17.6 49.2 %all-gather.5.cloned.1.call-done = f32[96,128,128]{2,1,0:T(8,128)} async-done(((f32[24,128,128]{2,1,0:T(8,128)}), f32[96,128,128]{2,1,0:T(8,128)}) %all-gather.5.cloned.1.call-update) | async-done | bytes 6291472 | tf_op jit(solution)/shard_map/all_gather | solution.py:44
  66.7 4.7 %reduce_sum.16 = f32[24,128,128]{2,1,0:T(8,128)} reduce(f32[4,24,128,128]{3,2,1,0:T(8,128)} %bitcast.45, f32[]{:T(128)} %constant.36.clone.1), dimensions={0}, to_apply=%region_0.0 | reduce | flops 1179648 | bytes 7864324 | tf_op jit(solution)/shard_map/reduce_sum | solution.py:50
  71.5 0.0 all-gather.7.cloned.1.call-update
  71.5 4.4 %copy.22 = bf16[64,8,24,128]{3,2,1,0:T(8,128)(2,1)} copy(bf16[64,8,24,128]{3,1,2,0:T(8,128)(2,1)} %bitcast.57) | data formatting | bytes 6291456
  75.9 0.1 iota_compare_fusion
  76.0 13.5 %fusion = f32[24,512,128]{1,2,0:T(8,128)} fusion(pred[512,512]{1,0:T(8,128)(4,1)S(1)} %iota_compare_fusion, bf16[512,24,128]{0,2,1:T(8,128)(2,1)} %bitcast.48, bf16[512,24,128]{2,1,0:T(8,128)(2,1)} %bitcast.52, bf16[512,24,128]{2,1,0:T(8,128)(2,1)} %bitcast.50), kind=kOutput, calls=%fused_computation.2 | convolution fusion | flops 3233808384 | bytes 15990784 | tf_op jit(solution)/shard_map/bhts,bshe->bthe/dot_general | solution.py:59
  89.5 12.7 %fusion.8 = f32[1,24,128,128]{3,0,2,1:T(1,128)S(1)} fusion(f32[4,24,128,128]{3,2,1,0:T(8,128)} %bitcast.46, s32[]{:T(128)S(6)} %axis_index.28), kind=kOutput, calls=%fused_computation.12 | convolution fusion | flops 18874372 | bytes 7864324 | tf_op jit(solution)/shard_map/j,jhde->hde/dot_general | solution.py:49
  102.2 84.8 %all-gather.7.cloned.1.call-done = f32[96,128,128]{2,1,0:T(8,128)} async-done(((f32[24,128,128]{2,1,0:T(8,128)}), f32[96,128,128]{2,1,0:T(8,128)}) %all-gather.7.cloned.1.call-update) | async-done | bytes 6291472 | tf_op jit(solution)/shard_map/all_gather | solution.py:12
  187.0 7.9 %while.14 = (s32[]{:T(128)}, f32[24,128,128]{2,1,0:T(8,128)S(1)}, s32[]{:T(128)}, f32[4,24,128,128]{3,2,1,0:T(8,128)}, s32[]{:T(128)}, /*index=5*/s32[]{:T(128)}) while((s32[]{:T(128)}, f32[24,128,128]{2,1,0:T(8,128)S(1)}, s32[]{:T(128)}, f32[4,24,128,128]{3,2,1,0:T(8,128)}, s32[]{:T(128)}, /*index=5*/s32[]{:T(128)}) %tuple.40), condition=%wide.region_2.3_spmd.clone, body=%wide.region_1.0_spmd.clone.sunk | while | flops 1179652 | bytes 4718693 | solution.py:20
  187.0 1.9 add_select_fusion.2
  189.0 2.0 add_select_fusion.2
  190.9 2.0 add_select_fusion.2
  192.9 2.0 add_select_fusion.2
  194.9 0.0 copy-start.2
  194.9 5.5 %fusion.5 = (f32[512,24]{0,1:T(8,128)S(1)}, f32[24,128,512]{2,1,0:T(8,128)S(1)}) fusion(f32[24,512,128]{1,2,0:T(8,128)} %fusion, bf16[512,24,128]{2,1,0:T(8,128)(2,1)} %bitcast.53, f32[24,128,128]{2,1,0:T(8,128)S(1)} %get-tuple-element.84, f32[24,128,128]{2,1,0:T(8,128)S(1)} %bitcast.55), kind=kOutput, calls=%fused_computation.8 | convolution fusion | flops 408145920 | bytes 18923520 | tf_op jit(solution)/shard_map/bthd,bhde->bthe/dot_general | solution.py:60
  200.4 0.1 slice-done.1
  200.5 1.0 fusion.7
  201.5 3.0 %copy.16 = bf16[1,1,512,3072]{3,2,1,0:T(8,128)(2,1)} copy(bf16[1,1,512,3072]{2,3,1,0:T(8,128)(2,1)S(1)} %bitcast.51) | data formatting | bytes 6291456 | tf_op jit(solution)/shard_map/reshape | solution.py:66
  (11 shorter events, 0.0 us)
Async XLA Ops:
  6.5 60.2 %all-gather.5.cloned.1.call-start = ((), (), s32[]{:S(2)}) async-start(), calls=%async_computation | async-start | bytes 7864320 | tf_op jit(solution)/shard_map/all_gather | solution.py:44
  9.7 3.9 %copy-start = (bf16[1,1,512,3072]{2,3,1,0:T(8,128)(2,1)}, bf16[1,1,512,3072]{2,3,1,0:T(8,128)(2,1)S(1)}, u32[]{:S(2)}) copy-start(bf16[1,1,512,3072]{2,3,1,0:T(8,128)(2,1)S(1)} %copy.21) | copy-start | bytes 9437188
  13.6 1.7 copy-start.1
  17.5 169.5 %all-gather.7.cloned.1.call-start = ((), (), s32[]{:S(2)}) async-start(), calls=%async_computation.1 | async-start | bytes 7864320 | tf_op jit(solution)/shard_map/all_gather | solution.py:12
  194.9 5.5 %slice-start = ((s8[6291456]{0:T(1024)(128)(4,1)}), s8[4194304]{0:T(1024)(128)(4,1)S(1)}, s32[]{:S(2)}) async-start(s8[6291456]{0:T(1024)(128)(4,1)} %bitcast.43), calls=%async_computation.2 | async-start | bytes 8388608
  194.9 5.6 %slice-start.1 = ((s8[6291456]{0:T(1024)(128)(4,1)}), s8[2097152]{0:T(1024)(128)(4,1)S(1)}, s32[]{:S(2)}) async-start(s8[6291456]{0:T(1024)(128)(4,1)} %bitcast.43), calls=%async_computation.3 | async-start | bytes 4194304
  194.9 5.6 %copy-start.2 = (f32[3072]{0:T(1024)S(1)}, f32[3072]{0:T(1024)}, u32[]{:S(2)}) copy-start(f32[3072]{0:T(1024)} %param.9) | copy-start | bytes 36868
Sparse Core Ops, SparseCore 0:
  17.6 49.0 all-gather.4
  71.6 115.3 all-gather.6
where the time goes:
time: 212 us; the launch traced here: 211 us
  waiting for transfers between devices  134 us (63%)
  matrix products  33.9 us (16%)
  local copies, waits for them, and re-layouts  16.2 us (8%)
  other arithmetic  13.6 us (6%)
  between operations  13.5 us (6%)
    all_gather x1, waiting for transfers between devices, carried_in(): everything = lax.all_gather(shard, axis)  84.8 us
    all_gather x1, waiting for transfers between devices, per_device(): gathered = lax.all_gather(local_total[None], 'seq', axis=0, tiled=True)  49.2 us
    dot_general x1, matrix products, per_device(): jnp.einsum('bhts,bshe->bthe', weights, values, preferred_element_type=jnp...  13.5 us
    dot_general x1, matrix products, per_device(): jnp.einsum('j,jhde->hde', lower, gathered, precision=lax.Precision.HIGHEST)  12.7 us
    unnamed x12, local copies, waits for them, and re-layouts  10 us
    select_n x4, other arithmetic, hop(): return jnp.where(reached, new, before)  7.8 us
    dot_general x1, matrix products, per_device(): jnp.einsum('bthd,bhde->bthe', queries, starts, preferred_element_type=jnp...  5.47 us
    reduce_sum x1, other arithmetic, per_device(): group_total = jnp.sum(gathered, axis=0)  4.72 us
  transfers between devices with their start and end apart: 2, of which 2 were waited for; matrix products, arithmetic and copies ran while one was open for 15% of the time, Pallas kernels for 0%

commit v1 on v0

v1 whole, which is shorter than its diff:
```python
import functools

import jax
import jax.numpy as jnp
from jax import lax
from jax.experimental import pallas as pl
from jax.experimental.pallas import tpu as pltpu
from jax.sharding import PartitionSpec as P

DH = 128
BLK = 512
TILE = 256
CHUNKS = 2
F32 = jnp.float32
BF16 = jnp.bfloat16
VMEM_LIMIT = 48 * 1024 * 1024


def params():
    return pltpu.CompilerParams(vmem_limit_bytes=VMEM_LIMIT)


def head_cols(i):
    return slice(i * DH, (i + 1) * DH)


def kvsum_block(heads, k_ref, v_ref, write):
    for i in range(heads):
        total = lax.dot_general(
            k_ref[:, head_cols(i)],
            v_ref[:, head_cols(i)],
            (((0,), (0,)), ((), ())),
            preferred_element_type=F32,
        )
        write(i, total)


def kvsum_kernel(heads, where_ref, k_ref, v_ref, keep_ref, send_ref):
    step = pl.program_id(0)

    @pl.when(step < 2)
    def _():
        def write(i, total):
            keep_ref[0, head_cols(i), :] = total

        kvsum_block(heads, k_ref, v_ref, write)

    @pl.when(step >= 2)
    def _():
        def write(i, total):
            send_ref[0, head_cols(i), :] = total

        kvsum_block(heads, k_ref, v_ref, write)


def slot_block(chunk, step, where):
    half = (step // 2) ^ where[0]
    quarter = (step % 2) ^ where[1]
    return chunk * 4 + half * 2 + quarter


def kvsum_chunk(where, k, v, chunk, heads):
    tokens = k.shape[0]
    width = heads * DH

    def columns(step, where_ref):
        return (0, slot_block(chunk, step, where_ref))

    return pl.pallas_call(
        functools.partial(kvsum_kernel, heads),
        grid_spec=pltpu.PrefetchScalarGridSpec(
            num_scalar_prefetch=1,
            grid=(4,),
            in_specs=[pl.BlockSpec((tokens, width), columns)] * 2,
            out_specs=[
                pl.BlockSpec((1, width, DH), lambda s, w: (jnp.minimum(s, 1), 0, 0)),
                pl.BlockSpec((1, width, DH), lambda s, w: (jnp.maximum(s - 2, 0), 0, 0)),
            ],
        ),
        out_shape=[jax.ShapeDtypeStruct((2, width, DH), F32)] * 2,
        compiler_params=params(),
        cost_estimate=pl.CostEstimate(
            flops=8 * heads * tokens * DH * DH,
            bytes_accessed=16 * tokens * width + 16 * width * DH,
            transcendentals=0,
        ),
        name="kvsum",
    )(where, k, v)


def local_kernel(heads, q_ref, k_ref, v_ref, mixed_ref):
    rows = lax.broadcasted_iota(jnp.int32, (TILE, TILE), 0)
    cols = lax.broadcasted_iota(jnp.int32, (TILE, TILE), 1)
    causal = rows >= cols
    for i in range(heads):
        c = head_cols(i)
        for t in range(BLK // TILE):
            at = slice(t * TILE, (t + 1) * TILE)
            total = None
            for s in range(t + 1):
                seen = slice(s * TILE, (s + 1) * TILE)
                scores = lax.dot_general(
                    q_ref[at, c], k_ref[seen, c], (((1,), (1,)), ((), ())), preferred_element_type=F32
                )
                if s == t:
                    scores = jnp.where(causal, scores, 0.0)
                part = jnp.dot(scores.astype(BF16), v_ref[seen, c], preferred_element_type=F32)
                total = part if total is None else total + part
            mixed_ref[at, c] = total


def local_chunk(q, k, v, chunk, count, heads):
    tokens = q.shape[0]
    nblocks = tokens // BLK
    steps = count // heads
    width = heads * DH
    spec = pl.BlockSpec((BLK, width), lambda b, s: (b, chunk * steps + s))
    return pl.pallas_call(
        functools.partial(local_kernel, heads),
        grid=(nblocks, steps),
        in_specs=[spec] * 3,
        out_specs=pl.BlockSpec((BLK, width), lambda b, s: (b, s)),
        out_shape=jax.ShapeDtypeStruct((tokens, count * DH), F32),
        compiler_params=params(),
        cost_estimate=pl.CostEstimate(
            flops=3 * count * tokens * BLK * DH,
            bytes_accessed=10 * tokens * count * DH,
            transcendentals=0,
        ),
        name="local_attention",
    )(q, k, v)


def finish_head(q, state, mixed, gain):
    mixed = mixed + jnp.dot(q, state.astype(BF16), preferred_element_type=F32)
    meansq = jnp.mean(mixed * mixed, axis=-1, keepdims=True)
    return (mixed * lax.rsqrt(meansq + 1e-05) * gain).astype(BF16)


def finish_kernel(heads, first, where_ref, q_ref, mixed_ref, gain_ref, own_ref, add_ref, other_ref, *rest):
    out_ref = rest[-1]
    step = pl.program_id(0)
    scale = where_ref[0].astype(F32)

    def run(state_of):
        for i in range(heads):
            c = head_cols(i)
            out_ref[:, c] = finish_head(q_ref[:, c], state_of(c), mixed_ref[:, c], gain_ref[:, c])

    @pl.when(step < 2)
    def _():
        run(lambda c: own_ref[0, c, :] + scale * add_ref[0, c, :])

    @pl.when(step >= 2)
    def _():
        run(lambda c: other_ref[0, c, :])


def finish_chunk(where, q, mixed, gain, own, add, other, out, chunk, heads):
    tokens, total = q.shape
    width = heads * DH

    def columns(step, where_ref):
        return (0, slot_block(chunk, step, where_ref))

    def local_columns(step, where_ref):
        return (0, slot_block(0, step, where_ref))

    kept = pl.BlockSpec((1, width, DH), lambda s, w: (jnp.minimum(s, 1), 0, 0))
    in_specs = [
        pl.BlockSpec((tokens, width), columns),
        pl.BlockSpec((tokens, width), local_columns),
        pl.BlockSpec((1, width), columns),
        kept,
        kept,
        pl.BlockSpec((1, width, DH), lambda s, w: (jnp.maximum(s - 2, 0), 0, 0)),
    ]
    operands = [q, mixed, gain, own, add, other]
    aliases = {}
    if out is not None:
        in_specs.append(pl.BlockSpec(memory_space=pl.ANY))
        operands.append(out)
        aliases = {7: 0}
    return pl.pallas_call(
        functools.partial(finish_kernel, heads, out is None),
        grid_spec=pltpu.PrefetchScalarGridSpec(
            num_scalar_prefetch=1,
            grid=(4,),
            in_specs=in_specs,
            out_specs=pl.BlockSpec((tokens, width), columns),
        ),
        out_shape=jax.ShapeDtypeStruct((tokens, total), BF16),
        input_output_aliases=aliases,
        compiler_params=params(),
        cost_estimate=pl.CostEstimate(
            flops=8 * heads * tokens * DH * DH,
            bytes_accessed=32 * tokens * width,
            transcendentals=0,
        ),
        name="finish",
    )(where, *operands)


def fast_path(q, k, v, gain, groups, heads_here):
    chunks = range(CHUNKS)
    heads = heads_here // (4 * CHUNKS)
    position = lax.axis_index("seq")
    core, chip = position % 2, position // 2
    where = jnp.stack([core, chip]).astype(jnp.int32)
    second_core, second_chip = core.astype(F32), chip.astype(F32)
    other_core = [(0, 1), (1, 0), (2, 3), (3, 2)]
    other_chip = [(0, 2), (2, 0), (1, 3), (3, 1)]

    kept, sent = zip(*[kvsum_chunk(where, k, v, j, heads) for j in chunks])
    from_core = [lax.ppermute(s, "seq", other_core) for s in sent]
    sums = [a + b for a, b in zip(kept, from_core)]
    here = [s[0] for s in sums]
    there = [s[1] for s in sums]
    mixed = [None] * CHUNKS

    there[-1], held = lax.optimization_barrier((there[-1], q))
    first_mixed = local_chunk(held, k, v, 0, 4 * heads, heads)
    from_chip = [lax.ppermute(s, "seq", other_chip) for s in there]
    from_chip[0], mixed[0] = lax.optimization_barrier((from_chip[0], first_mixed))
    group_total = [a + b for a, b in zip(here, from_chip)]
    group_total[-1], held = lax.optimization_barrier((group_total[-1], q))
    later_mixed = [local_chunk(held, k, v, j, 4 * heads, heads) for j in chunks[1:]]

    arrived = [[] for _ in chunks]
    passing = group_total
    for hop in range(groups - 1):
        received = [lax.ppermute(p, "grp", [(hop, hop + 1)]) for p in passing]
        if hop == 0:
            received[0], mixed[1:] = lax.optimization_barrier((received[0], later_mixed))
        for j in chunks:
            arrived[j].append(received[j])
        passing = [r + g for r, g in zip(received, group_total)]
    before = [sum(a) if a else jnp.zeros_like(g) for a, g in zip(arrived, group_total)]

    back = [b + (1.0 - second_chip) * h for b, h in zip(before, here)]
    from_chip_back = [lax.ppermute(b, "seq", other_chip) for b in back]
    mine = [
        jnp.stack([b + second_chip * c, r])
        for b, c, r in zip(before, from_chip, from_chip_back)
    ]
    back = [m + (1.0 - second_core) * a for m, a in zip(mine, kept)]
    from_core_back = [lax.ppermute(b, "seq", other_core) for b in back]

    out = None
    for j in chunks:
        out = finish_chunk(
            where, q, mixed[j], gain, mine[j], from_core[j], from_core_back[j], out, j, heads
        )
    return out


def general_states(k, v, heads_here, nblocks, groups):
    def split(array):
        return array.reshape(nblocks, BLK, heads_here, DH)

    block_sums = jnp.einsum("bthd,bthe->bhde", split(k), split(v), preferred_element_type=F32)
    total = jnp.sum(block_sums, axis=0)
    earlier = jnp.concatenate([jnp.zeros_like(total)[None], jnp.cumsum(block_sums, axis=0)[:-1]])
    gathered = lax.all_gather(total, "seq")
    position = lax.axis_index("seq")
    lower = lax.broadcasted_iota(jnp.int32, (gathered.shape[0], 1, 1, 1), 0) < position
    within = jnp.sum(jnp.where(lower, gathered, 0.0), axis=0)
    group_total = jnp.sum(gathered, axis=0)
    before = jnp.zeros_like(total)
    passing = group_total
    for hop in range(groups - 1):
        received = lax.ppermute(passing, "grp", [(hop, hop + 1)])
        before = before + received
        passing = received + group_total
    return (before + within)[None] + earlier


def general_path(q, k, v, gain, groups, heads_here):
    tokens = q.shape[0]
    nblocks = tokens // BLK
    states = general_states(k, v, heads_here, nblocks, groups).astype(BF16)
    mixed = local_chunk(q, k, v, 0, heads_here, 1).reshape(nblocks, BLK, heads_here, DH)
    queries = q.reshape(nblocks, BLK, heads_here, DH)
    mixed = mixed + jnp.einsum("bthd,bhde->bthe", queries, states, preferred_element_type=F32)
    meansq = jnp.mean(mixed * mixed, axis=-1, keepdims=True)
    result = mixed * lax.rsqrt(meansq + 1e-05) * gain.reshape(heads_here, DH)
    return result.astype(BF16).reshape(q.shape)


def per_device(groups, shards, query_feat, key_feat, value_feat, norm_gain):
    shape = query_feat.shape
    tokens, width = shape[2:]
    heads_here = width // DH
    q, k, v = (a.reshape(tokens, width) for a in (query_feat, key_feat, value_feat))
    gain = norm_gain.reshape(1, width)
    fits = shards == 4 and tokens == BLK and heads_here % (4 * CHUNKS) == 0
    path = fast_path if fits else general_path
    return path(q, k, v, gain, groups, heads_here).reshape(shape)


def solution(mesh):
    placed = P("grp", "seq", None, "head")
    return jax.shard_map(
        functools.partial(per_device, mesh.shape["grp"], mesh.shape["seq"]),
        mesh=mesh,
        in_specs=(placed, placed, placed, P("head")),
        out_specs=placed,
        check_vma=False,
    )
```

time: 212 us -> 71.2 us (0.34)
  the two profiles are of different devices: /device:TPU:0 before, /device:TPU:25 now
where the time goes in v1:
time: 71.2 us; the launch traced here: 70.7 us
  Pallas kernels  31.3 us (44%)
  starting transfers between devices  18.1 us (25%)
  waiting for transfers between devices  12.8 us (18%)
  local copies, waits for them, and re-layouts  5.22 us (7%)
  other arithmetic  2.99 us (4%)
    pallas_call x2, Pallas kernels, local_chunk(): pl.pallas_call(functools.partial(local_kernel, heads), grid=(nblocks, ste...  13.1 us
    ppermute x6, waiting for transfers between devices, fast_path(): received = [lax.ppermute(p, 'grp', [(hop, hop + 1)]) for p in passing]  12.1 us
    pallas_call x2, Pallas kernels, finish_chunk(): pl.pallas_call(functools.partial(finish_kernel, heads, out is None), grid...  10.8 us
    ppermute x2, starting transfers between devices, fast_path(): from_core_back = [lax.ppermute(b, 'seq', other_core) for b in back]  9.11 us
    pallas_call x2, Pallas kernels, kvsum_chunk(): pl.pallas_call(functools.partial(kvsum_kernel, heads), grid_spec=pltpu.Pr...  7.49 us
    ppermute x6, starting transfers between devices, fast_path(): received = [lax.ppermute(p, 'grp', [(hop, hop + 1)]) for p in passing]  5.52 us
    unnamed x12, local copies, waits for them, and re-layouts  5.19 us
    ppermute x2, starting transfers between devices, fast_path(): from_chip = [lax.ppermute(s, 'seq', other_chip) for s in there]  2.55 us
  transfers between devices with their start and end apart: 14, of which 4 were waited for; matrix products, arithmetic and copies ran while one was open for 4% of the time, Pallas kernels for 31%

profile of v1, /device:TPU:25, one launch (start us, length us, event | category | flops | bytes accessed | tf_op | source)
XLA Modules:
  0.0 70.7 jit_solution(4119247819034318264)
XLA Ops:
  0.1 1.9 %copy-done = bf16[1,1,512,3072]{3,2,1,0:T(8,128)(2,1)S(1)} copy-done((bf16[1,1,512,3072]{3,2,1,0:T(8,128)(2,1)S(1)}, bf16[1,1,512,3072]{3,2,1,0:T(8,128)(2,1)}, u32[]{:S(2)}) %copy-start) | copy-done | bytes 3145752
  2.0 3.7 %kvsum.2 = (f32[2,384,128]{2,1,0:T(8,128)S(1)}, f32[2,384,128]{2,1,0:T(8,128)S(1)}) custom-call(s32[2]{0:T(128)S(1)} %pad_add_fusion.where_ref, bf16[512,3072]{1,0:T(8,128)(2,1)S(1)} %bitcast.31, bf16[512,3072]{1,0:T(8,128)(2,1)} %bitcast.39), custom_call_target="tpu_custom_call" | custom-call | flops 201326592 | bytes 3932160 | tf_op jit(solution)/shard_map/kvsum/pallas_call | solution.py:69
  5.7 0.7 %collective-permute-start = (f32[2,384,128]{2,1,0:T(8,128)S(1)}, f32[2,384,128]{2,1,0:T(8,128)S(1)}, u32[]{:S(2)}, u32[]{:S(2)}) collective-permute-start(f32[2,384,128]{2,1,0:T(8,128)S(1)} %get-tuple-element.18), channel_id=1, source_target_pairs={{0,8},{8,0},{16,24},{24,16},{1,9},{9,1},{17,25},{25,17},{2,10},{10... | collective-permute-start | bytes 1179656 | tf_op jit(solution)/shard_map/ppermute | solution.py:215
  6.5 3.7 %kvsum.3 = (f32[2,384,128]{2,1,0:T(8,128)S(1)}, f32[2,384,128]{2,1,0:T(8,128)S(1)}) custom-call(s32[2]{0:T(128)S(1)} %pad_add_fusion.where_ref, bf16[512,3072]{1,0:T(8,128)(2,1)S(1)} %bitcast.32, bf16[512,3072]{1,0:T(8,128)(2,1)} %bitcast.40), custom_call_target="tpu_custom_call" | custom-call | flops 201326592 | bytes 3932160 | tf_op jit(solution)/shard_map/kvsum/pallas_call | solution.py:69
  10.4 1.3 %collective-permute-start.1 = (f32[384,128]{1,0:T(8,128)S(1)}, f32[384,128]{1,0:T(8,128)S(1)}, u32[]{:S(2)}, u32[]{:S(2)}) collective-permute-start(f32[384,128]{1,0:T(8,128)S(1)} %slice_bitcast_fusion.2), channel_id=1, source_target_pairs={{0,16},{16,0},{8,24},{24,8},{1,17},{17,1},{9,25},{25,9},{2,18},{18... | collective-permute-start | bytes 589832 | tf_op jit(solution)/shard_map/ppermute | solution.py:223
  12.1 1.3 %collective-permute-start.4 = (f32[384,128]{1,0:T(8,128)S(1)}, f32[384,128]{1,0:T(8,128)S(1)}, u32[]{:S(2)}, u32[]{:S(2)}) collective-permute-start(f32[384,128]{1,0:T(8,128)S(1)} %slice_bitcast_fusion.1), channel_id=1, source_target_pairs={{0,16},{16,0},{8,24},{24,8},{1,17},{17,1},{9,25},{25,9},{2,18},{18... | collective-permute-start | bytes 589832 | tf_op jit(solution)/shard_map/ppermute | solution.py:223
  13.3 6.5 %local_attention.2.mixed_ref = f32[512,1536]{1,0:T(8,128)S(1)} custom-call(bf16[512,3072]{1,0:T(8,128)(2,1)} %bitcast.33, bf16[512,3072]{1,0:T(8,128)(2,1)} %bitcast.29, bf16[512,3072]{1,0:T(8,128)(2,1)} %bitcast.41), custom_call_target="tpu_custom_call" | custom-call | flops 1207959552 | bytes 7864320 | tf_op jit(solution)/shard_map/local_attention/pallas_call | solution.py:118
  19.9 1.7 %copy-done.2 = f32[512,1536]{1,0:T(8,128)} copy-done((f32[512,1536]{1,0:T(8,128)}, f32[512,1536]{1,0:T(8,128)S(1)}, u32[]{:S(2)}) %copy-start.2) | copy-done | bytes 3145752
  21.6 0.7 collective-permute-start.3
  22.3 0.7 collective-permute-start.5
  23.0 6.6 %local_attention.3.mixed_ref = f32[512,1536]{1,0:T(8,128)S(1)} custom-call(bf16[512,3072]{1,0:T(8,128)(2,1)} %bitcast.34, bf16[512,3072]{1,0:T(8,128)(2,1)} %bitcast.30, bf16[512,3072]{1,0:T(8,128)(2,1)} %bitcast.42), custom_call_target="tpu_custom_call" | custom-call | flops 1207959552 | bytes 7864320 | tf_op jit(solution)/shard_map/local_attention/pallas_call | solution.py:118
  29.6 1.6 %copy-done.3 = f32[512,1536]{1,0:T(8,128)} copy-done((f32[512,1536]{1,0:T(8,128)}, f32[512,1536]{1,0:T(8,128)S(1)}, u32[]{:S(2)}) %copy-start.3) | copy-done | bytes 3145752
  31.2 0.7 collective-permute-start.10
  31.9 0.7 add.64
  33.3 0.8 %add.73 = f32[384,128]{1,0:T(8,128)} add(f32[384,128]{1,0:T(8,128)S(1)} %collective-permute-done.10, f32[384,128]{1,0:T(8,128)S(1)} %fusion) | non-fusion elementwise | flops 49152 | bytes 589824 | tf_op jit(solution)/shard_map/add | solution.py:237
  34.1 1.3 %collective-permute-start.11 = (f32[384,128]{1,0:T(8,128)}, f32[384,128]{1,0:T(8,128)}, u32[]{:S(2)}, u32[]{:S(2)}) collective-permute-start(f32[384,128]{1,0:T(8,128)} %add.73), channel_id=1, source_target_pairs={{4,6},{5,7},{12,14},{13,15},{20,22},{21,23},{28,30},{29,31}} | collective-permute-start | bytes 589832 | tf_op jit(solution)/shard_map/ppermute | solution.py:232
  35.5 1.6 %collective-permute-start.7 = (f32[384,128]{1,0:T(8,128)S(1)}, f32[384,128]{1,0:T(8,128)S(1)}, u32[]{:S(2)}, u32[]{:S(2)}) collective-permute-start(f32[384,128]{1,0:T(8,128)S(1)} %add.66), channel_id=1, source_target_pairs={{4,6},{5,7},{12,14},{13,15},{20,22},{21,23},{28,30},{29,31}} | collective-permute-start | bytes 589832 | tf_op jit(solution)/shard_map/ppermute | solution.py:232
  37.0 7.7 %collective-permute-done.11 = f32[384,128]{1,0:T(8,128)} collective-permute-done((f32[384,128]{1,0:T(8,128)}, f32[384,128]{1,0:T(8,128)}, u32[]{:S(2)}, u32[]{:S(2)}) %collective-permute-start.11) | collective-permute-done | bytes 196640 | tf_op jit(solution)/shard_map/ppermute | solution.py:232
  44.8 1.1 %add_bitcast_fusion = (f32[1,384,128]{2,1,0:T(8,128)S(1)}, f32[384,128]{1,0:T(8,128)S(1)}) fusion(f32[384,128]{1,0:T(8,128)S(1)} %collective-permute-done.1, f32[]{:T(128)S(6)} %convert_element_type.6, f32[384,128]{1,0:T(8,128)} %collective-permute-done.11, f32[384,128]{1,0:T(8,128)S(1)} %collective-permute-done.3, f32[384,128]{1,0:T(8,128)} %copy-done.5, ...), kind=kLoop, calls=%fused_computation.9 | loop fusion | flops 294912 | bytes 1376264 | tf_op jit(solution)/shard_map/stack | solution.py:243
  45.9 4.4 %collective-permute-done.7 = f32[384,128]{1,0:T(8,128)S(1)} collective-permute-done((f32[384,128]{1,0:T(8,128)S(1)}, f32[384,128]{1,0:T(8,128)S(1)}, u32[]{:S(2)}, u32[]{:S(2)}) %collective-permute-start.7) | collective-permute-done | bytes 196640 | tf_op jit(solution)/shard_map/ppermute | solution.py:232
  50.8 7.1 %collective-permute-start.13 = (f32[2,384,128]{2,1,0:T(8,128)S(1)}, f32[2,384,128]{2,1,0:T(8,128)S(1)}, u32[]{:S(2)}, u32[]{:S(2)}) collective-permute-start(f32[2,384,128]{2,1,0:T(8,128)S(1)} %get-tuple-element.33), channel_id=1, source_target_pairs={{0,8},{8,0},{16,24},{24,16},{1,9},{9,1},{17,25},{25,17},{2,10},{10... | collective-permute-start | bytes 1179656 | tf_op jit(solution)/shard_map/ppermute | solution.py:247
  57.9 2.0 %collective-permute-start.9 = (f32[2,384,128]{2,1,0:T(8,128)S(1)}, f32[2,384,128]{2,1,0:T(8,128)S(1)}, u32[]{:S(2)}, u32[]{:S(2)}) collective-permute-start(f32[2,384,128]{2,1,0:T(8,128)S(1)} %get-tuple-element.35), channel_id=1, source_target_pairs={{0,8},{8,0},{16,24},{24,16},{1,9},{9,1},{17,25},{25,17},{2,10},{10... | collective-permute-start | bytes 1179656 | tf_op jit(solution)/shard_map/ppermute | solution.py:247
  60.0 5.4 %finish.2.rest_0_ = bf16[512,3072]{1,0:T(8,128)(2,1)} custom-call(s32[2]{0:T(128)S(1)} %pad_add_fusion.where_ref, bf16[512,3072]{1,0:T(8,128)(2,1)S(1)} %bitcast.35, f32[512,1536]{1,0:T(8,128)} %copy-done.2, f32[1,3072]{1,0:T(1,128)S(1)} %bitcast.37, f32[2,384,128]{2,1,0:T(8,128)S(1)} %get-tuple-element.34.own_ref, ...), custom_call_target="tpu_custom_call" | custom-call | flops 201326592 | bytes 6291456 | tf_op jit(solution)/shard_map/finish/pallas_call | solution.py:184
  65.4 5.4 %finish.3 = bf16[512,3072]{1,0:T(8,128)(2,1)} custom-call(s32[2]{0:T(128)S(1)} %pad_add_fusion.where_ref, bf16[512,3072]{1,0:T(8,128)(2,1)S(1)} %bitcast.36, f32[512,1536]{1,0:T(8,128)} %copy-done.3, f32[1,3072]{1,0:T(1,128)S(1)} %bitcast.38, f32[2,384,128]{2,1,0:T(8,128)S(1)} %get-tuple-element.36.own_ref, ...), custom_call_target="tpu_custom_call", output_to_operand_aliasing={{}: (7, {})} | custom-call | flops 201326592 | bytes 6291456 | tf_op jit(solution)/shard_map/finish/pallas_call | solution.py:184
  (37 shorter events, 2.0 us)
Async XLA Ops:
  0.1 1.9 %copy-start = (bf16[1,1,512,3072]{3,2,1,0:T(8,128)(2,1)S(1)}, bf16[1,1,512,3072]{3,2,1,0:T(8,128)(2,1)}, u32[]{:S(2)}) copy-start(bf16[1,1,512,3072]{3,2,1,0:T(8,128)(2,1)} %param.5) | copy-start | bytes 9437188
  5.7 4.6 %collective-permute-start = (f32[2,384,128]{2,1,0:T(8,128)S(1)}, f32[2,384,128]{2,1,0:T(8,128)S(1)}, u32[]{:S(2)}, u32[]{:S(2)}) collective-permute-start(f32[2,384,128]{2,1,0:T(8,128)S(1)} %get-tuple-element.18), channel_id=1, source_target_pairs={{0,8},{8,0},{16,24},{24,16},{1,9},{9,1},{17,25},{25,17},{2,10},{10... | collective-permute-start | bytes 1179656 | tf_op jit(solution)/shard_map/ppermute | solution.py:215
  10.2 1.8 %collective-permute-start.2 = (f32[2,384,128]{2,1,0:T(8,128)S(1)}, f32[2,384,128]{2,1,0:T(8,128)S(1)}, u32[]{:S(2)}, u32[]{:S(2)}) collective-permute-start(f32[2,384,128]{2,1,0:T(8,128)S(1)} %get-tuple-element.20), channel_id=1, source_target_pairs={{0,8},{8,0},{16,24},{24,16},{1,9},{9,1},{17,25},{25,17},{2,10},{10... | collective-permute-start | bytes 1179656 | tf_op jit(solution)/shard_map/ppermute | solution.py:215
  10.4 11.2 %collective-permute-start.1 = (f32[384,128]{1,0:T(8,128)S(1)}, f32[384,128]{1,0:T(8,128)S(1)}, u32[]{:S(2)}, u32[]{:S(2)}) collective-permute-start(f32[384,128]{1,0:T(8,128)S(1)} %slice_bitcast_fusion.2), channel_id=1, source_target_pairs={{0,16},{16,0},{8,24},{24,8},{1,17},{17,1},{9,25},{25,9},{2,18},{18... | collective-permute-start | bytes 589832 | tf_op jit(solution)/shard_map/ppermute | solution.py:223
  12.1 10.2 %collective-permute-start.4 = (f32[384,128]{1,0:T(8,128)S(1)}, f32[384,128]{1,0:T(8,128)S(1)}, u32[]{:S(2)}, u32[]{:S(2)}) collective-permute-start(f32[384,128]{1,0:T(8,128)S(1)} %slice_bitcast_fusion.1), channel_id=1, source_target_pairs={{0,16},{16,0},{8,24},{24,8},{1,17},{17,1},{9,25},{25,9},{2,18},{18... | collective-permute-start | bytes 589832 | tf_op jit(solution)/shard_map/ppermute | solution.py:223
  19.9 1.7 %copy-start.2 = (f32[512,1536]{1,0:T(8,128)}, f32[512,1536]{1,0:T(8,128)S(1)}, u32[]{:S(2)}) copy-start(f32[512,1536]{1,0:T(8,128)S(1)} %local_attention.2.mixed_ref) | copy-start | bytes 9437188
  21.6 9.6 %collective-permute-start.3 = (f32[384,128]{1,0:T(8,128)S(1)}, f32[384,128]{1,0:T(8,128)S(1)}, u32[]{:S(2)}, u32[]{:S(2)}) collective-permute-start(f32[384,128]{1,0:T(8,128)S(1)} %fusion), channel_id=1, source_target_pairs={{0,2},{1,3},{8,10},{9,11},{16,18},{17,19},{24,26},{25,27}} | collective-permute-start | bytes 589832 | tf_op jit(solution)/shard_map/ppermute | solution.py:232
  22.3 9.6 %collective-permute-start.5 = (f32[384,128]{1,0:T(8,128)S(1)}, f32[384,128]{1,0:T(8,128)S(1)}, u32[]{:S(2)}, u32[]{:S(2)}) collective-permute-start(f32[384,128]{1,0:T(8,128)S(1)} %fusion.1), channel_id=1, source_target_pairs={{0,2},{1,3},{8,10},{9,11},{16,18},{17,19},{24,26},{25,27}} | collective-permute-start | bytes 589832 | tf_op jit(solution)/shard_map/ppermute | solution.py:232
  29.6 1.6 %copy-start.3 = (f32[512,1536]{1,0:T(8,128)}, f32[512,1536]{1,0:T(8,128)S(1)}, u32[]{:S(2)}) copy-start(f32[512,1536]{1,0:T(8,128)S(1)} %local_attention.3.mixed_ref) | copy-start | bytes 9437188
  31.2 2.1 %collective-permute-start.10 = (f32[384,128]{1,0:T(8,128)S(1)}, f32[384,128]{1,0:T(8,128)S(1)}, u32[]{:S(2)}, u32[]{:S(2)}) collective-permute-start(f32[384,128]{1,0:T(8,128)S(1)} %add.71), channel_id=1, source_target_pairs={{2,4},{3,5},{10,12},{11,13},{18,20},{19,21},{26,28},{27,29}} | collective-permute-start | bytes 589832 | tf_op jit(solution)/shard_map/ppermute | solution.py:232
  32.6 2.8 %collective-permute-start.6 = (f32[384,128]{1,0:T(8,128)}, f32[384,128]{1,0:T(8,128)S(1)}, u32[]{:S(2)}, u32[]{:S(2)}) collective-permute-start(f32[384,128]{1,0:T(8,128)} %add.64), channel_id=1, source_target_pairs={{2,4},{3,5},{10,12},{11,13},{18,20},{19,21},{26,28},{27,29}} | collective-permute-start | bytes 589832 | tf_op jit(solution)/shard_map/ppermute | solution.py:232
  33.3 0.8 %copy-start.5 = (f32[384,128]{1,0:T(8,128)}, f32[384,128]{1,0:T(8,128)S(1)}, u32[]{:S(2)}) copy-start(f32[384,128]{1,0:T(8,128)S(1)} %collective-permute-done.10) | copy-start | bytes 589828
  34.1 10.7 %collective-permute-start.11 = (f32[384,128]{1,0:T(8,128)}, f32[384,128]{1,0:T(8,128)}, u32[]{:S(2)}, u32[]{:S(2)}) collective-permute-start(f32[384,128]{1,0:T(8,128)} %add.73), channel_id=1, source_target_pairs={{4,6},{5,7},{12,14},{13,15},{20,22},{21,23},{28,30},{29,31}} | collective-permute-start | bytes 589832 | tf_op jit(solution)/shard_map/ppermute | solution.py:232
  35.4 24.6 %copy-start.1 = (bf16[1,1,512,3072]{3,2,1,0:T(8,128)(2,1)S(1)}, bf16[1,1,512,3072]{3,2,1,0:T(8,128)(2,1)}, u32[]{:S(2)}) copy-start(bf16[1,1,512,3072]{3,2,1,0:T(8,128)(2,1)} %param.4) | copy-start | bytes 9437188
  35.4 24.6 %copy-start.4 = (f32[3072]{0:T(1024)S(1)}, f32[3072]{0:T(1024)}, u32[]{:S(2)}) copy-start(f32[3072]{0:T(1024)} %param.7) | copy-start | bytes 36868
  35.5 14.8 %collective-permute-start.7 = (f32[384,128]{1,0:T(8,128)S(1)}, f32[384,128]{1,0:T(8,128)S(1)}, u32[]{:S(2)}, u32[]{:S(2)}) collective-permute-start(f32[384,128]{1,0:T(8,128)S(1)} %add.66), channel_id=1, source_target_pairs={{4,6},{5,7},{12,14},{13,15},{20,22},{21,23},{28,30},{29,31}} | collective-permute-start | bytes 589832 | tf_op jit(solution)/shard_map/ppermute | solution.py:232
  45.9 4.9 %collective-permute-start.12 = (f32[384,128]{1,0:T(8,128)S(1)}, f32[384,128]{1,0:T(8,128)S(1)}, u32[]{:S(2)}, u32[]{:S(2)}) collective-permute-start(f32[384,128]{1,0:T(8,128)S(1)} %get-tuple-element.30), channel_id=1, source_target_pairs={{0,16},{16,0},{8,24},{24,8},{1,17},{17,1},{9,25},{25,9},{2,18},{18... | collective-permute-start | bytes 589832 | tf_op jit(solution)/shard_map/ppermute | solution.py:241
  50.4 7.5 %collective-permute-start.8 = (f32[384,128]{1,0:T(8,128)S(1)}, f32[384,128]{1,0:T(8,128)S(1)}, u32[]{:S(2)}, u32[]{:S(2)}) collective-permute-start(f32[384,128]{1,0:T(8,128)S(1)} %get-tuple-element.32), channel_id=1, source_target_pairs={{0,16},{16,0},{8,24},{24,8},{1,17},{17,1},{9,25},{25,9},{2,18},{18... | collective-permute-start | bytes 589832 | tf_op jit(solution)/shard_map/ppermute | solution.py:241
  50.8 9.2 %collective-permute-start.13 = (f32[2,384,128]{2,1,0:T(8,128)S(1)}, f32[2,384,128]{2,1,0:T(8,128)S(1)}, u32[]{:S(2)}, u32[]{:S(2)}) collective-permute-start(f32[2,384,128]{2,1,0:T(8,128)S(1)} %get-tuple-element.33), channel_id=1, source_target_pairs={{0,8},{8,0},{16,24},{24,16},{1,9},{9,1},{17,25},{25,17},{2,10},{10... | collective-permute-start | bytes 1179656 | tf_op jit(solution)/shard_map/ppermute | solution.py:247
  57.9 7.4 %collective-permute-start.9 = (f32[2,384,128]{2,1,0:T(8,128)S(1)}, f32[2,384,128]{2,1,0:T(8,128)S(1)}, u32[]{:S(2)}, u32[]{:S(2)}) collective-permute-start(f32[2,384,128]{2,1,0:T(8,128)S(1)} %get-tuple-element.35), channel_id=1, source_target_pairs={{0,8},{8,0},{16,24},{24,16},{1,9},{9,1},{17,25},{25,17},{2,10},{10... | collective-permute-start | bytes 1179656 | tf_op jit(solution)/shard_map/ppermute | solution.py:247

commit v2 on v0

v2 whole, which is shorter than its diff:
```python
import functools

import jax
import jax.numpy as jnp
from jax import lax
from jax.experimental import pallas as pl
from jax.experimental.pallas import tpu as pltpu
from jax.sharding import PartitionSpec as P

DH = 128
BLK = 512
TILE = 256
CHUNKS = 2
EARLY = 3
SMALL = pl.CostEstimate(flops=1000, bytes_accessed=0, transcendentals=0)
F32 = jnp.float32
BF16 = jnp.bfloat16
VMEM_LIMIT = 8 * 1024 * 1024


def params():
    return pltpu.CompilerParams(vmem_limit_bytes=VMEM_LIMIT)


def in_hbm(array):
    return pltpu.with_memory_space_constraint(array, pltpu.HBM)


def in_vmem(array):
    return pltpu.with_memory_space_constraint(array, pltpu.VMEM)


def head_cols(i):
    return slice(i * DH, (i + 1) * DH)


def slot_column(slot, width, core, chip):
    half = (slot // 2) ^ core
    quarter = (slot % 2) ^ chip
    return pl.multiple_of((half * 2 + quarter) * width, DH)


class Slots:
    def __init__(self, where_ref, width):
        self.core, self.chip, self.width = where_ref[0], where_ref[1], width

    def column(self, first, slot):
        return pl.multiple_of(first + slot_column(slot, self.width, self.core, self.chip), DH)

    def load(self, first, slot, source, target, sem):
        copy = pltpu.make_async_copy(
            source.at[:, pl.ds(self.column(first, slot), self.width)], target, sem
        )
        copy.start()
        return copy


def specs(*spaces):
    return [pl.BlockSpec(memory_space=s) for s in spaces]


SLOT_ORDER = (3, 2, 0, 1)
KVSUM_OUTS = 6


def kvsum_kernel(width, where_ref, k_hbm, v_hbm, q_hbm, *refs):
    *refs, q_ref, sems = refs
    slots = Slots(where_ref, width)
    outs = [refs[KVSUM_OUTS * j : KVSUM_OUTS * (j + 1)] for j in range(CHUNKS)]
    loads = []
    for slot in SLOT_ORDER:
        for j in range(CHUNKS):
            k_ref, v_ref = outs[j][4:]
            first = 4 * width * j
            loads.append(
                (
                    slot,
                    j,
                    slots.load(first, slot, k_hbm, k_ref.at[slot], sems.at[0, j, slot]),
                    slots.load(first, slot, v_hbm, v_ref.at[slot], sems.at[1, j, slot]),
                )
            )
    q_load = slots.load(0, 0, q_hbm, q_ref, sems.at[2, 0, 0])
    for slot, j, *copies in loads:
        for copy in copies:
            copy.wait()
        lead, rest, own, other, k_ref, v_ref = outs[j]
        for i in range(width // DH):
            c = head_cols(i)
            total = lax.dot_general(
                k_ref[slot, :, c],
                v_ref[slot, :, c],
                (((0,), (0,)), ((), ())),
                preferred_element_type=F32,
            )
            if slot == 3:
                lead[c, :] = total
            else:
                rest[(slot + 1) % 3, c, :] = total
            if slot < 2:
                (own, other)[slot][c, :] = total
    q_load.wait()


def kvsum(where, q, k, v, width):
    tokens = k.shape[0]
    one = pltpu.VMEM((width, DH), F32)
    part = pltpu.VMEM((4, tokens, width), BF16)
    outs = [one, pltpu.VMEM((3, width, DH), F32), one, one, part, part] * CHUNKS
    outs.append(pltpu.VMEM((tokens, width), BF16))
    results = pl.pallas_call(
        functools.partial(kvsum_kernel, width),
        in_specs=specs(pltpu.SMEM, *[pltpu.HBM] * 3),
        out_specs=specs(*[pltpu.VMEM] * len(outs)),
        out_shape=outs,
        scratch_shapes=[pltpu.SemaphoreType.DMA((3, CHUNKS, 4))],
        compiler_params=params(),
        cost_estimate=SMALL,
        name="kvsum",
    )(where, in_hbm(k), in_hbm(v), in_hbm(q))
    return [results[KVSUM_OUTS * j : KVSUM_OUTS * (j + 1)] for j in range(CHUNKS)], results[-1]


def local_scores(q_ref, k_ref, c):
    rows = lax.broadcasted_iota(jnp.int32, (TILE, TILE), 0)
    cols = lax.broadcasted_iota(jnp.int32, (TILE, TILE), 1)
    causal = rows >= cols
    tiles = []
    for t in range(BLK // TILE):
        scores = lax.dot_general(
            q_ref[t * TILE : (t + 1) * TILE, c],
            k_ref[: (t + 1) * TILE, c],
            (((1,), (1,)), ((), ())),
            preferred_element_type=F32,
        )
        last = jnp.where(causal, scores[:, t * TILE :], 0.0).astype(BF16)
        if t > 0:
            last = jnp.concatenate([scores[:, : t * TILE].astype(BF16), last], axis=1)
        tiles.append(last)
    return tiles


def local_mix(tiles, v_ref, out_ref, c):
    for t, scores in enumerate(tiles):
        out_ref[t * TILE : (t + 1) * TILE, c] = jnp.dot(
            scores, v_ref[: (t + 1) * TILE, c], preferred_element_type=F32
        )


def local_heads(items):
    held = None
    for q_ref, k_ref, v_ref, out_ref, c in items:
        tiles = local_scores(q_ref, k_ref, c)
        if held is not None:
            local_mix(*held)
        held = (tiles, v_ref, out_ref, c)
    local_mix(*held)


def local_kernel(heads, q_ref, k_ref, v_ref, mixed_ref):
    local_heads([(q_ref, k_ref, v_ref, mixed_ref, head_cols(i)) for i in range(heads)])


def local_blocks(q, k, v, heads):
    tokens, width = q.shape
    spec = pl.BlockSpec((BLK, heads * DH), lambda b, s: (b, s))
    return pl.pallas_call(
        functools.partial(local_kernel, heads),
        grid=(tokens // BLK, width // (heads * DH)),
        in_specs=[spec] * 3,
        out_specs=spec,
        out_shape=jax.ShapeDtypeStruct((tokens, width), F32),
        compiler_params=params(),
        name="local_attention",
    )(q, k, v)


def local_slots_kernel(width, places, where_ref, q_hbm, *refs):
    count = len(places)
    if q_hbm is None:
        q_refs, loads = dict(zip(places, refs)), {}
        refs = refs[count:]
    else:
        every = [(j, n) for j in range(CHUNKS) for n in range(4)]
        *refs, sems = refs
        q_refs = dict(zip(every, [refs[0], *refs[-len(every) + 1 :]]))
        refs = refs[1:]
        slots = Slots(where_ref, width)
        loads = {
            (j, n): slots.load(4 * width * j, n, q_hbm, q_refs[j, n], sems.at[j, n])
            for j, n in every[1:]
        }
    k_refs, v_refs, out_refs = refs[:CHUNKS], refs[CHUNKS : 2 * CHUNKS], refs[2 * CHUNKS :]

    def items():
        for place, out_ref in zip(places, out_refs):
            j, n = place
            if place in loads:
                loads.pop(place).wait()
            for i in range(width // DH):
                yield q_refs[place], k_refs[j].at[n], v_refs[j].at[n], out_ref, head_cols(i)

    local_heads(items())
    for copy in loads.values():
        copy.wait()


def local_slots(where, q, q_lead, q_slots, k_parts, v_parts, width, places):
    tokens = k_parts[0].shape[1]
    first = q_lead is not None
    every = 4 * CHUNKS
    kernel = functools.partial(local_slots_kernel, width, places)
    if not first:
        kernel = lambda where_ref, *refs: local_slots_kernel(width, places, where_ref, None, *refs)
    queries = [q_lead] if first else [q_slots[p] for p in places]
    outs = [pltpu.VMEM((tokens, width), F32)] * len(places)
    outs += [pltpu.VMEM((tokens, width), BF16)] * ((every - 1) * first)
    results = pl.pallas_call(
        kernel,
        in_specs=specs(
            pltpu.SMEM, *[pltpu.HBM] * first, *[pltpu.VMEM] * (len(queries) + 2 * CHUNKS)
        ),
        out_specs=specs(*[pltpu.VMEM] * len(outs)),
        out_shape=outs,
        scratch_shapes=[pltpu.SemaphoreType.DMA((CHUNKS, 4))] * first,
        compiler_params=params(),
        cost_estimate=SMALL,
        name="local_attention",
    )(where, *([in_hbm(q)] if first else []), *[in_vmem(a) for a in (*queries, *k_parts, *v_parts)])
    return results[: len(places)], results[len(places) :]


def finish_kernel(first, width, where_ref, gain_ref, *refs):
    q_refs, mixed_refs = refs[:4], refs[4:8]
    own_near, own_far, lead_ref, rest_ref, far_near, far_far = refs[8:14]
    out_hbm, out_ref, sems = refs[-3:]
    slots = Slots(where_ref, width)
    second = slots.core.astype(F32)
    states = (own_near, own_far, far_near, far_far)
    from_core = (rest_ref.at[0], lead_ref, rest_ref.at[1], rest_ref.at[2])
    stores = []
    for n in range(4):
        column = slots.column(first, n)
        for i in range(width // DH):
            c = head_cols(i)
            state = states[n][c, :] + second * from_core[n][c, :]
            mixed = mixed_refs[n][:, c] + jnp.dot(
                q_refs[n][:, c], state.astype(BF16), preferred_element_type=F32
            )
            meansq = jnp.mean(mixed * mixed, axis=-1, keepdims=True)
            gain = gain_ref[:, pl.ds(pl.multiple_of(column + i * DH, DH), DH)]
            out_ref[n, :, c] = (mixed * lax.rsqrt(meansq + 1e-05) * gain).astype(BF16)
        store = pltpu.make_async_copy(out_ref.at[n], out_hbm.at[:, pl.ds(column, width)], sems.at[n])
        store.start()
        stores.append(store)
    for store in stores:
        store.wait()


def finish(where, gain, queries, mixed, states, out, first, width):
    tokens = queries[0].shape[0]
    earlier = [] if out is None else [out]
    operands = [where, gain, *[in_vmem(a) for a in (*queries, *mixed)], *states]
    return pl.pallas_call(
        functools.partial(finish_kernel, first, width),
        in_specs=specs(pltpu.SMEM, *[pltpu.VMEM] * (len(operands) - 1), *[pltpu.HBM] * len(earlier)),
        out_specs=specs(pltpu.HBM)[0],
        out_shape=jax.ShapeDtypeStruct((tokens, gain.shape[1]), BF16),
        scratch_shapes=[pltpu.VMEM((4, tokens, width), BF16), pltpu.SemaphoreType.DMA((4,))],
        input_output_aliases={len(operands): 0} if earlier else {},
        compiler_params=params(),
        cost_estimate=SMALL,
        name="finish",
    )(*operands, *earlier)


def combine(compute, count, where, *operands):
    shape = operands[0].shape

    def kernel(where_ref, *refs):
        ins, outs = refs[: len(operands)], refs[len(operands) :]
        core, chip = where_ref[0].astype(F32), where_ref[1].astype(F32)
        results = compute(core, chip, *[r[...] for r in ins])
        for ref, value in zip(outs, results):
            ref[...] = value

    return pl.pallas_call(
        kernel,
        in_specs=specs(pltpu.SMEM, *[pltpu.VMEM] * len(operands)),
        out_specs=specs(*[pltpu.VMEM] * count),
        out_shape=[jax.ShapeDtypeStruct(shape, F32)] * count,
        compiler_params=params(),
        cost_estimate=SMALL,
        name="combine",
    )(where, *operands)


def tie(*values):
    return lax.optimization_barrier(values)


def fast_path(q, k, v, gain, groups, heads_here):
    chunks = range(CHUNKS)
    width = heads_here // (4 * CHUNKS) * DH
    position = lax.axis_index("seq")
    core, chip = position % 2, position // 2
    where = jnp.stack([core, chip]).astype(jnp.int32)
    other_core = [(0, 1), (1, 0), (2, 3), (3, 2)]
    other_chip = [(0, 2), (2, 0), (1, 3), (3, 1)]

    sums, q_lead = kvsum(where, q, k, v, width)
    lead = [lax.ppermute(s[0], "seq", other_core) for s in sums]
    there = [s[3] + r for s, r in zip(sums, lead)]
    rest = [lax.ppermute(s[1], "seq", other_core) for s in sums]
    k_parts, v_parts = [s[4] for s in sums], [s[5] for s in sums]
    every = [(j, n) for j in chunks for n in range(4)]
    there[0], held = tie(there[0], where)
    early, q_slots = local_slots(held, q, q_lead, None, k_parts, v_parts, width, every[:EARLY])
    q_slots = dict(zip(every, [q_lead, *q_slots]))
    *later_there, early = tie(*there[1:], early)
    there[1:] = later_there
    from_chip = [lax.ppermute(t, "seq", other_chip) for t in there]
    here = [s[2] + r[0] for s, r in zip(sums, rest)]
    first_total, held = tie(here[0] + from_chip[0], where)
    late, _ = local_slots(held, None, None, q_slots, k_parts, v_parts, width, every[EARLY:])
    *later_chip, late = tie(*from_chip[1:], late)
    from_chip[1:] = later_chip
    group_total = [first_total] + [h + r for h, r in zip(here[1:], from_chip[1:])]
    local = dict(zip(every, [*early, *late]))

    arrived = [[] for _ in chunks]
    passing = group_total
    for hop in range(groups - 1):
        received = [lax.ppermute(p, "grp", [(hop, hop + 1)]) for p in passing]
        for j in chunks:
            arrived[j].append(received[j])
        passing = [r + g for r, g in zip(received, group_total)]

    def turn(core, chip, here, from_chip, *arrived):
        before = sum(arrived[1:], arrived[0])
        return before + (1.0 - chip) * here, before + chip * from_chip

    turned = [combine(turn, 2, where, here[j], from_chip[j], *arrived[j]) for j in chunks]
    from_chip_back = [lax.ppermute(back, "seq", other_chip) for back, _ in turned]
    near_back = [lax.ppermute(own, "seq", other_core) for _, own in turned]
    out = None
    for j in chunks:
        if out is not None:
            from_chip_back[j], out = tie(from_chip_back[j], out)
        far_back = lax.ppermute(from_chip_back[j], "seq", other_core)
        states = (turned[j][1], from_chip_back[j], lead[j], rest[j], near_back[j], far_back)
        queries = [q_slots[j, n] for n in range(4)]
        mixed = [local[j, n] for n in range(4)]
        out = finish(where, gain, queries, mixed, states, out, j * 4 * width, width)
    return out


def general_states(k, v, heads_here, nblocks, groups):
    def split(array):
        return array.reshape(nblocks, BLK, heads_here, DH)

    block_sums = jnp.einsum("bthd,bthe->bhde", split(k), split(v), preferred_element_type=F32)
    total = jnp.sum(block_sums, axis=0)
    earlier = jnp.concatenate([jnp.zeros_like(total)[None], jnp.cumsum(block_sums, axis=0)[:-1]])
    gathered = lax.all_gather(total, "seq")
    position = lax.axis_index("seq")
    lower = lax.broadcasted_iota(jnp.int32, (gathered.shape[0], 1, 1, 1), 0) < position
    within = jnp.sum(jnp.where(lower, gathered, 0.0), axis=0)
    group_total = jnp.sum(gathered, axis=0)
    before = jnp.zeros_like(total)
    passing = group_total
    for hop in range(groups - 1):
        received = lax.ppermute(passing, "grp", [(hop, hop + 1)])
        before = before + received
        passing = received + group_total
    return (before + within)[None] + earlier


def general_path(q, k, v, gain, groups, heads_here):
    tokens = q.shape[0]
    nblocks = tokens // BLK
    states = general_states(k, v, heads_here, nblocks, groups).astype(BF16)
    mixed = local_blocks(q, k, v, 1).reshape(nblocks, BLK, heads_here, DH)
    queries = q.reshape(nblocks, BLK, heads_here, DH)
    mixed = mixed + jnp.einsum("bthd,bhde->bthe", queries, states, preferred_element_type=F32)
    meansq = jnp.mean(mixed * mixed, axis=-1, keepdims=True)
    result = mixed * lax.rsqrt(meansq + 1e-05) * gain.reshape(heads_here, DH)
    return result.astype(BF16).reshape(q.shape)


def per_device(groups, shards, query_feat, key_feat, value_feat, norm_gain):
    shape = query_feat.shape
    tokens, width = shape[2:]
    heads_here = width // DH
    q, k, v = (a.reshape(tokens, width) for a in (query_feat, key_feat, value_feat))
    gain = norm_gain.reshape(1, width)
    fits = shards == 4 and groups > 1 and tokens == BLK and heads_here % (4 * CHUNKS) == 0
    path = fast_path if fits else general_path
    return path(q, k, v, gain, groups, heads_here).reshape(shape)


def solution(mesh):
    placed = P("grp", "seq", None, "head")
    return jax.shard_map(
        functools.partial(per_device, mesh.shape["grp"], mesh.shape["seq"]),
        mesh=mesh,
        in_specs=(placed, placed, placed, P("head")),
        out_specs=placed,
        check_vma=False,
    )
```

time: 212 us -> 53.3 us (0.25)
  the two profiles are of different devices: /device:TPU:0 before, /device:TPU:25 now
where the time goes in v2:
time: 53.3 us; the launch traced here: 53.1 us
  starting transfers between devices  21.3 us (40%)
  Pallas kernels  18.2 us (34%)
  waiting for transfers between devices  13.1 us (25%)
    ppermute x6, waiting for transfers between devices, fast_path(): received = [lax.ppermute(p, 'grp', [(hop, hop + 1)]) for p in passing]  8.82 us
    pallas_call x2, Pallas kernels, local_slots(): pl.pallas_call(kernel, in_specs=specs(pltpu.SMEM, *[pltpu.HBM] * first, *...  7.59 us
    ppermute x2, starting transfers between devices, fast_path(): near_back = [lax.ppermute(own, 'seq', other_core) for _, own in turned]  6.71 us
    ppermute x2, starting transfers between devices, fast_path(): far_back = lax.ppermute(from_chip_back[j], 'seq', other_core)  5.3 us
    ppermute x6, starting transfers between devices, fast_path(): received = [lax.ppermute(p, 'grp', [(hop, hop + 1)]) for p in passing]  5.28 us
    pallas_call x2, Pallas kernels, finish(): pl.pallas_call(functools.partial(finish_kernel, first, width), in_specs=s...  5.01 us
    pallas_call x1, Pallas kernels, kvsum(): pl.pallas_call(functools.partial(kvsum_kernel, width), in_specs=specs(plt...  4.39 us
    ppermute x2, waiting for transfers between devices, fast_path(): from_chip = [lax.ppermute(t, 'seq', other_chip) for t in there]  1.71 us
  transfers between devices with their start and end apart: 18, of which 6 were waited for; matrix products, arithmetic and copies ran while one was open for 0% of the time, Pallas kernels for 21%

profile of v2, /device:TPU:25, one launch (start us, length us, event | category | flops | bytes accessed | tf_op | source)
XLA Modules:
  0.0 53.1 jit_solution(454479754010076712)
XLA Ops:
  0.1 4.4 %kvsum.1 = (f32[384,128]{1,0:T(8,128)S(1)}, f32[3,384,128]{2,1,0:T(8,128)S(1)}, f32[384,128]{1,0:T(8,128)S(1)}, f32[384,128]{1,0:T(8,128)S(1)}, bf16[4,512,384]{...) custom-call(s32[2]{0:T(128)S(1)} %pad_add_fusion.where_ref, ...), custom_call_target="tpu_custom_call" | custom-call | flops 1000 | tf_op jit(solution)/shard_map/kvsum/pallas_call | solution.py:111
  4.5 0.7 %collective-permute-start.3 = (f32[3,384,128]{2,1,0:T(8,128)S(1)}, f32[3,384,128]{2,1,0:T(8,128)S(1)}, u32[]{:S(2)}, u32[]{:S(2)}) collective-permute-start(f32[3,384,128]{2,1,0:T(8,128)S(1)} %get-tuple-element.72), channel_id=1, source_target_pairs={{0,8},{8,0},{16,24},{24,16},{1,9},{9,1},{17,25},{25,17},{2,10},{10... | collective-permute-start | bytes 1769480 | tf_op jit(solution)/shard_map/ppermute | solution.py:314
  5.7 1.4 %collective-permute-done.refs_10_ = f32[384,128]{1,0:T(8,128)S(1)} collective-permute-done((f32[384,128]{1,0:T(8,128)S(1)}, f32[384,128]{1,0:T(8,128)S(1)}, u32[]{:S(2)}, u32[]{:S(2)}) %collective-permute-start) | collective-permute-done | bytes 196640 | tf_op jit(solution)/shard_map/ppermute | solution.py:312
  7.1 1.3 %collective-permute-start.4 = (f32[384,128]{1,0:T(8,128)S(1)}, f32[384,128]{1,0:T(8,128)S(1)}, u32[]{:S(2)}, u32[]{:S(2)}) collective-permute-start(f32[384,128]{1,0:T(8,128)S(1)} %add.36), channel_id=1, source_target_pairs={{0,16},{16,0},{8,24},{24,8},{1,17},{17,1},{9,25},{25,9},{2,18},{18... | collective-permute-start | bytes 589832 | tf_op jit(solution)/shard_map/ppermute | solution.py:322
  8.4 0.7 %collective-permute-start.5 = (f32[3,384,128]{2,1,0:T(8,128)S(1)}, f32[3,384,128]{2,1,0:T(8,128)S(1)}, u32[]{:S(2)}, u32[]{:S(2)}) collective-permute-start(f32[3,384,128]{2,1,0:T(8,128)S(1)} %get-tuple-element.86), channel_id=1, source_target_pairs={{0,8},{8,0},{16,24},{24,16},{1,9},{9,1},{17,25},{25,17},{2,10},{10... | collective-permute-start | bytes 1769480 | tf_op jit(solution)/shard_map/ppermute | solution.py:314
  9.1 3.8 %local_attention.2 = (f32[512,384]{1,0:T(8,128)S(1)}, f32[512,384]{1,0:T(8,128)S(1)}, f32[512,384]{1,0:T(8,128)S(1)}, bf16[512,384]{1,0:T(8,128)(2,1)S(1)}, bf16...) custom-call(s32[2]{0:T(128)S(1)} %pad_add_fusion.where_ref, ...), custom_call_target="tpu_custom_call" | custom-call | flops 1000 | tf_op jit(solution)/shard_map/local_attention/pallas_call | solution.py:218
  13.4 0.7 %collective-permute-start.10 = (f32[384,128]{1,0:T(8,128)S(1)}, f32[384,128]{1,0:T(8,128)S(1)}, u32[]{:S(2)}, u32[]{:S(2)}) collective-permute-start(f32[384,128]{1,0:T(8,128)S(1)} %get-tuple-element.96), channel_id=1, source_target_pairs={{0,2},{1,3},{8,10},{9,11},{16,18},{17,19},{24,26},{25,27}} | collective-permute-start | bytes 589832 | tf_op jit(solution)/shard_map/ppermute | solution.py:334
  14.1 3.8 %local_attention.3 = (f32[512,384]{1,0:T(8,128)S(1)}, f32[512,384]{1,0:T(8,128)S(1)}, f32[512,384]{1,0:T(8,128)S(1)}, f32[512,384]{1,0:T(8,128)S(1)}, f32[512,384]{1,0:T(8,128)S(1)}) custom-call(s32[2]{0:T(128)S(1)} %pad_add_fusion.where_ref, bf16[512,384]{1,0:T(8,128)(2,1)S(1)} %get-tuple-element.75.refs_0_.refs_3_, ...), custom_call_target="tpu_custom_call" | custom-call | flops 1000 | tf_op jit(solution)/shard_map/local_attention/pallas_call | solution.py:218
  17.9 1.6 %collective-permute-done.2.refs_1_ = f32[384,128]{1,0:T(8,128)S(1)} collective-permute-done((f32[384,128]{1,0:T(8,128)S(1)}, f32[384,128]{1,0:T(8,128)S(1)}, u32[]{:S(2)}, u32[]{:S(2)}) %collective-permute-start.2) | collective-permute-done | bytes 196640 | tf_op jit(solution)/shard_map/ppermute | solution.py:322
  19.5 0.7 %collective-permute-start.11 = (f32[384,128]{1,0:T(8,128)S(1)}, f32[384,128]{1,0:T(8,128)S(1)}, u32[]{:S(2)}, u32[]{:S(2)}) collective-permute-start(f32[384,128]{1,0:T(8,128)S(1)} %add.44), channel_id=1, source_target_pairs={{2,4},{3,5},{10,12},{11,13},{18,20},{19,21},{26,28},{27,29}} | collective-permute-start | bytes 589832 | tf_op jit(solution)/shard_map/ppermute | solution.py:334
  20.3 0.7 %collective-permute-start.6 = (f32[384,128]{1,0:T(8,128)S(1)}, f32[384,128]{1,0:T(8,128)S(1)}, u32[]{:S(2)}, u32[]{:S(2)}) collective-permute-start(f32[384,128]{1,0:T(8,128)S(1)} %get-tuple-element.101), channel_id=1, source_target_pairs={{0,2},{1,3},{8,10},{9,11},{16,18},{17,19},{24,26},{25,27}} | collective-permute-start | bytes 589832 | tf_op jit(solution)/shard_map/ppermute | solution.py:334
  21.0 1.3 %collective-permute-start.12 = (f32[384,128]{1,0:T(8,128)S(1)}, f32[384,128]{1,0:T(8,128)S(1)}, u32[]{:S(2)}, u32[]{:S(2)}) collective-permute-start(f32[384,128]{1,0:T(8,128)S(1)} %add.45), channel_id=1, source_target_pairs={{4,6},{5,7},{12,14},{13,15},{20,22},{21,23},{28,30},{29,31}} | collective-permute-start | bytes 589832 | tf_op jit(solution)/shard_map/ppermute | solution.py:334
  22.3 0.7 %collective-permute-start.7 = (f32[384,128]{1,0:T(8,128)S(1)}, f32[384,128]{1,0:T(8,128)S(1)}, u32[]{:S(2)}, u32[]{:S(2)}) collective-permute-start(f32[384,128]{1,0:T(8,128)S(1)} %add.42), channel_id=1, source_target_pairs={{2,4},{3,5},{10,12},{11,13},{18,20},{19,21},{26,28},{27,29}} | collective-permute-start | bytes 589832 | tf_op jit(solution)/shard_map/ppermute | solution.py:334
  23.0 8.8 %collective-permute-done.12.refs_4_ = f32[384,128]{1,0:T(8,128)S(1)} collective-permute-done((f32[384,128]{1,0:T(8,128)S(1)}, f32[384,128]{1,0:T(8,128)S(1)}, u32[]{:S(2)}, u32[]{:S(2)}) %collective-permute-start.12) | collective-permute-done | bytes 196640 | tf_op jit(solution)/shard_map/ppermute | solution.py:334
  31.8 0.6 %combine.3 = (f32[384,128]{1,0:T(8,128)S(1)}, f32[384,128]{1,0:T(8,128)S(1)}) custom-call(s32[2]{0:T(128)S(1)} %pad_add_fusion.where_ref, f32[384,128]{1,0:T(8,128)S(1)} %get-tuple-element.104.refs_0_, f32[384,128]{1,0:T(8,128)S(1)} %collective-permute-done.4.refs_1_, f32[384,128]{1,0:T(8,128)S(1)} %collective-permute-done.10.refs_2_, ...), custom_call_target="tpu_custom_call" | custom-call | flops 1000 | tf_op jit(solution)/shard_map/combine/pallas_call | solution.py:287
  32.6 1.3 %collective-permute-start.8 = (f32[384,128]{1,0:T(8,128)S(1)}, f32[384,128]{1,0:T(8,128)S(1)}, u32[]{:S(2)}, u32[]{:S(2)}) collective-permute-start(f32[384,128]{1,0:T(8,128)S(1)} %add.43), channel_id=1, source_target_pairs={{4,6},{5,7},{12,14},{13,15},{20,22},{21,23},{28,30},{29,31}} | collective-permute-start | bytes 589832 | tf_op jit(solution)/shard_map/ppermute | solution.py:334
  33.9 3.1 %collective-permute-start.14 = (f32[384,128]{1,0:T(8,128)S(1)}, f32[384,128]{1,0:T(8,128)S(1)}, u32[]{:S(2)}, u32[]{:S(2)}) collective-permute-start(f32[384,128]{1,0:T(8,128)S(1)} %get-tuple-element.97.refs_8_), channel_id=1, source_target_pairs={{0,8},{8,0},{16,24},{24,16},{1,9},{9,1},{17,25},{25,17},{2,10},{10... | collective-permute-start | bytes 589832 | tf_op jit(solution)/shard_map/ppermute | solution.py:345
  37.0 3.6 %collective-permute-start.15 = (f32[384,128]{1,0:T(8,128)S(1)}, f32[384,128]{1,0:T(8,128)S(1)}, u32[]{:S(2)}, u32[]{:S(2)}) collective-permute-start(f32[384,128]{1,0:T(8,128)S(1)} %collective-permute-done.13.refs_9_), channel_id=1, source_target_pairs={{0,8},{8,0},{16,24},{24,16},{1,9},{9,1},{17,25},{25,17},{2,10},{10... | collective-permute-start | bytes 589832 | tf_op jit(solution)/shard_map/ppermute | solution.py:350
  40.6 0.6 %combine.2 = (f32[384,128]{1,0:T(8,128)S(1)}, f32[384,128]{1,0:T(8,128)S(1)}) custom-call(s32[2]{0:T(128)S(1)} %pad_add_fusion.where_ref, f32[384,128]{1,0:T(8,128)S(1)} %get-tuple-element.102.refs_0_, f32[384,128]{1,0:T(8,128)S(1)} %collective-permute-done.2.refs_1_, f32[384,128]{1,0:T(8,128)S(1)} %collective-permute-done.6.refs_2_, ...), custom_call_target="tpu_custom_call" | custom-call | flops 1000 | tf_op jit(solution)/shard_map/combine/pallas_call | solution.py:287
  41.6 3.6 %collective-permute-start.16 = (f32[384,128]{1,0:T(8,128)S(1)}, f32[384,128]{1,0:T(8,128)S(1)}, u32[]{:S(2)}, u32[]{:S(2)}) collective-permute-start(f32[384,128]{1,0:T(8,128)S(1)} %get-tuple-element.88.refs_8_), channel_id=1, source_target_pairs={{0,8},{8,0},{16,24},{24,16},{1,9},{9,1},{17,25},{25,17},{2,10},{10... | collective-permute-start | bytes 589832 | tf_op jit(solution)/shard_map/ppermute | solution.py:345
  45.2 2.5 %finish.2.refs_14_ = bf16[512,3072]{1,0:T(8,128)(2,1)} custom-call(s32[2]{0:T(128)S(1)} %pad_add_fusion.where_ref, f32[1,3072]{1,0:T(1,128)S(1)} %bitcast.17, bf16[512,384]{1,0:T(8,128)(2,1)S(1)} %get-tuple-element.56.refs_0_, bf16[512,384]{1,0:T(8,128)(2,1)S(1)} %get-tuple-element.90.refs_1_, bf16[512,384]{1,0:T(8,128)(2,1)S(1)} %get-tuple-element.91.refs_2_, ...), custom_call_target="tpu_custom_call" | custom-call | flops 1000 | tf_op jit(solution)/shard_map/finish/pallas_call | solution.py:264
  47.8 1.7 %collective-permute-start.17 = (f32[384,128]{1,0:T(8,128)S(1)}, f32[384,128]{1,0:T(8,128)S(1)}, u32[]{:S(2)}, u32[]{:S(2)}) collective-permute-start(f32[384,128]{1,0:T(8,128)S(1)} %collective-permute-done.9.refs_9_), channel_id=1, source_target_pairs={{0,8},{8,0},{16,24},{24,16},{1,9},{9,1},{17,25},{25,17},{2,10},{10... | collective-permute-start | bytes 589832 | tf_op jit(solution)/shard_map/ppermute | solution.py:350
  49.5 1.1 %collective-permute-done.17.refs_13_ = f32[384,128]{1,0:T(8,128)S(1)} collective-permute-done((f32[384,128]{1,0:T(8,128)S(1)}, f32[384,128]{1,0:T(8,128)S(1)}, u32[]{:S(2)}, u32[]{:S(2)}) %collective-permute-start.17) | collective-permute-done | bytes 196640 | tf_op jit(solution)/shard_map/ppermute | solution.py:350
  50.6 2.5 %finish.3 = bf16[512,3072]{1,0:T(8,128)(2,1)} custom-call(s32[2]{0:T(128)S(1)} %pad_add_fusion.where_ref, f32[1,3072]{1,0:T(1,128)S(1)} %bitcast.18, bf16[512,384]{1,0:T(8,128)(2,1)S(1)} %get-tuple-element.61.refs_1_.refs_0_, bf16[512,384]{1,0:T(8,128)(2,1)S(1)} %get-tuple-element.62.refs_2_.refs_1_, ...), custom_call_target="tpu_custom_call", output_to_operand_aliasing={{}: (16, {})} | custom-call | flops 1000 | tf_op jit(solution)/shard_map/finish/pallas_call | solution.py:264
  (30 shorter events, 1.8 us)
Async XLA Ops:
  4.5 8.9 %collective-permute-start.3 = (f32[3,384,128]{2,1,0:T(8,128)S(1)}, f32[3,384,128]{2,1,0:T(8,128)S(1)}, u32[]{:S(2)}, u32[]{:S(2)}) collective-permute-start(f32[3,384,128]{2,1,0:T(8,128)S(1)} %get-tuple-element.72), channel_id=1, source_target_pairs={{0,8},{8,0},{16,24},{24,16},{1,9},{9,1},{17,25},{25,17},{2,10},{10... | collective-permute-start | bytes 1769480 | tf_op jit(solution)/shard_map/ppermute | solution.py:314
  5.2 1.9 %collective-permute-start = (f32[384,128]{1,0:T(8,128)S(1)}, f32[384,128]{1,0:T(8,128)S(1)}, u32[]{:S(2)}, u32[]{:S(2)}) collective-permute-start(f32[384,128]{1,0:T(8,128)S(1)} %get-tuple-element.54), channel_id=1, source_target_pairs={{0,8},{8,0},{16,24},{24,16},{1,9},{9,1},{17,25},{25,17},{2,10},{10... | collective-permute-start | bytes 589832 | tf_op jit(solution)/shard_map/ppermute | solution.py:312
  5.3 7.6 %collective-permute-start.1 = (f32[384,128]{1,0:T(8,128)S(1)}, f32[384,128]{1,0:T(8,128)S(1)}, u32[]{:S(2)}, u32[]{:S(2)}) collective-permute-start(f32[384,128]{1,0:T(8,128)S(1)} %get-tuple-element.66), channel_id=1, source_target_pairs={{0,8},{8,0},{16,24},{24,16},{1,9},{9,1},{17,25},{25,17},{2,10},{10... | collective-permute-start | bytes 589832 | tf_op jit(solution)/shard_map/ppermute | solution.py:312
  7.1 6.2 %collective-permute-start.4 = (f32[384,128]{1,0:T(8,128)S(1)}, f32[384,128]{1,0:T(8,128)S(1)}, u32[]{:S(2)}, u32[]{:S(2)}) collective-permute-start(f32[384,128]{1,0:T(8,128)S(1)} %add.36), channel_id=1, source_target_pairs={{0,16},{16,0},{8,24},{24,8},{1,17},{17,1},{9,25},{25,9},{2,18},{18... | collective-permute-start | bytes 589832 | tf_op jit(solution)/shard_map/ppermute | solution.py:322
  8.4 11.8 %collective-permute-start.5 = (f32[3,384,128]{2,1,0:T(8,128)S(1)}, f32[3,384,128]{2,1,0:T(8,128)S(1)}, u32[]{:S(2)}, u32[]{:S(2)}) collective-permute-start(f32[3,384,128]{2,1,0:T(8,128)S(1)} %get-tuple-element.86), channel_id=1, source_target_pairs={{0,8},{8,0},{16,24},{24,16},{1,9},{9,1},{17,25},{25,17},{2,10},{10... | collective-permute-start | bytes 1769480 | tf_op jit(solution)/shard_map/ppermute | solution.py:314
  12.9 6.6 %collective-permute-start.2 = (f32[384,128]{1,0:T(8,128)S(1)}, f32[384,128]{1,0:T(8,128)S(1)}, u32[]{:S(2)}, u32[]{:S(2)}) collective-permute-start(f32[384,128]{1,0:T(8,128)S(1)} %add.37), channel_id=1, source_target_pairs={{0,16},{16,0},{8,24},{24,8},{1,17},{17,1},{9,25},{25,9},{2,18},{18... | collective-permute-start | bytes 589832 | tf_op jit(solution)/shard_map/ppermute | solution.py:322
  13.4 6.1 %collective-permute-start.10 = (f32[384,128]{1,0:T(8,128)S(1)}, f32[384,128]{1,0:T(8,128)S(1)}, u32[]{:S(2)}, u32[]{:S(2)}) collective-permute-start(f32[384,128]{1,0:T(8,128)S(1)} %get-tuple-element.96), channel_id=1, source_target_pairs={{0,2},{1,3},{8,10},{9,11},{16,18},{17,19},{24,26},{25,27}} | collective-permute-start | bytes 589832 | tf_op jit(solution)/shard_map/ppermute | solution.py:334
  17.9 27.4 %copy-start = (f32[3072]{0:T(1024)S(1)}, f32[3072]{0:T(1024)}, u32[]{:S(2)}) copy-start(f32[3072]{0:T(1024)} %param.7) | copy-start | bytes 36868
  19.5 1.4 %collective-permute-start.11 = (f32[384,128]{1,0:T(8,128)S(1)}, f32[384,128]{1,0:T(8,128)S(1)}, u32[]{:S(2)}, u32[]{:S(2)}) collective-permute-start(f32[384,128]{1,0:T(8,128)S(1)} %add.44), channel_id=1, source_target_pairs={{2,4},{3,5},{10,12},{11,13},{18,20},{19,21},{26,28},{27,29}} | collective-permute-start | bytes 589832 | tf_op jit(solution)/shard_map/ppermute | solution.py:334
  20.3 2.0 %collective-permute-start.6 = (f32[384,128]{1,0:T(8,128)S(1)}, f32[384,128]{1,0:T(8,128)S(1)}, u32[]{:S(2)}, u32[]{:S(2)}) collective-permute-start(f32[384,128]{1,0:T(8,128)S(1)} %get-tuple-element.101), channel_id=1, source_target_pairs={{0,2},{1,3},{8,10},{9,11},{16,18},{17,19},{24,26},{25,27}} | collective-permute-start | bytes 589832 | tf_op jit(solution)/shard_map/ppermute | solution.py:334
  21.0 10.8 %collective-permute-start.12 = (f32[384,128]{1,0:T(8,128)S(1)}, f32[384,128]{1,0:T(8,128)S(1)}, u32[]{:S(2)}, u32[]{:S(2)}) collective-permute-start(f32[384,128]{1,0:T(8,128)S(1)} %add.45), channel_id=1, source_target_pairs={{4,6},{5,7},{12,14},{13,15},{20,22},{21,23},{28,30},{29,31}} | collective-permute-start | bytes 589832 | tf_op jit(solution)/shard_map/ppermute | solution.py:334
  22.3 10.2 %collective-permute-start.7 = (f32[384,128]{1,0:T(8,128)S(1)}, f32[384,128]{1,0:T(8,128)S(1)}, u32[]{:S(2)}, u32[]{:S(2)}) collective-permute-start(f32[384,128]{1,0:T(8,128)S(1)} %add.42), channel_id=1, source_target_pairs={{2,4},{3,5},{10,12},{11,13},{18,20},{19,21},{26,28},{27,29}} | collective-permute-start | bytes 589832 | tf_op jit(solution)/shard_map/ppermute | solution.py:334
  32.4 4.6 %collective-permute-start.13 = (f32[384,128]{1,0:T(8,128)S(1)}, f32[384,128]{1,0:T(8,128)S(1)}, u32[]{:S(2)}, u32[]{:S(2)}) collective-permute-start(f32[384,128]{1,0:T(8,128)S(1)} %get-tuple-element.98), channel_id=1, source_target_pairs={{0,16},{16,0},{8,24},{24,8},{1,17},{17,1},{9,25},{25,9},{2,18},{18... | collective-permute-start | bytes 589832 | tf_op jit(solution)/shard_map/ppermute | solution.py:344
  32.6 8.1 %collective-permute-start.8 = (f32[384,128]{1,0:T(8,128)S(1)}, f32[384,128]{1,0:T(8,128)S(1)}, u32[]{:S(2)}, u32[]{:S(2)}) collective-permute-start(f32[384,128]{1,0:T(8,128)S(1)} %add.43), channel_id=1, source_target_pairs={{4,6},{5,7},{12,14},{13,15},{20,22},{21,23},{28,30},{29,31}} | collective-permute-start | bytes 589832 | tf_op jit(solution)/shard_map/ppermute | solution.py:334
  33.9 11.4 %collective-permute-start.14 = (f32[384,128]{1,0:T(8,128)S(1)}, f32[384,128]{1,0:T(8,128)S(1)}, u32[]{:S(2)}, u32[]{:S(2)}) collective-permute-start(f32[384,128]{1,0:T(8,128)S(1)} %get-tuple-element.97.refs_8_), channel_id=1, source_target_pairs={{0,8},{8,0},{16,24},{24,16},{1,9},{9,1},{17,25},{25,17},{2,10},{10... | collective-permute-start | bytes 589832 | tf_op jit(solution)/shard_map/ppermute | solution.py:345
  37.0 8.2 %collective-permute-start.15 = (f32[384,128]{1,0:T(8,128)S(1)}, f32[384,128]{1,0:T(8,128)S(1)}, u32[]{:S(2)}, u32[]{:S(2)}) collective-permute-start(f32[384,128]{1,0:T(8,128)S(1)} %collective-permute-done.13.refs_9_), channel_id=1, source_target_pairs={{0,8},{8,0},{16,24},{24,16},{1,9},{9,1},{17,25},{25,17},{2,10},{10... | collective-permute-start | bytes 589832 | tf_op jit(solution)/shard_map/ppermute | solution.py:350
  41.2 6.5 %collective-permute-start.9 = (f32[384,128]{1,0:T(8,128)S(1)}, f32[384,128]{1,0:T(8,128)S(1)}, u32[]{:S(2)}, u32[]{:S(2)}) collective-permute-start(f32[384,128]{1,0:T(8,128)S(1)} %get-tuple-element.89), channel_id=1, source_target_pairs={{0,16},{16,0},{8,24},{24,8},{1,17},{17,1},{9,25},{25,9},{2,18},{18... | collective-permute-start | bytes 589832 | tf_op jit(solution)/shard_map/ppermute | solution.py:344
  41.6 7.9 %collective-permute-start.16 = (f32[384,128]{1,0:T(8,128)S(1)}, f32[384,128]{1,0:T(8,128)S(1)}, u32[]{:S(2)}, u32[]{:S(2)}) collective-permute-start(f32[384,128]{1,0:T(8,128)S(1)} %get-tuple-element.88.refs_8_), channel_id=1, source_target_pairs={{0,8},{8,0},{16,24},{24,16},{1,9},{9,1},{17,25},{25,17},{2,10},{10... | collective-permute-start | bytes 589832 | tf_op jit(solution)/shard_map/ppermute | solution.py:345
  47.8 2.8 %collective-permute-start.17 = (f32[384,128]{1,0:T(8,128)S(1)}, f32[384,128]{1,0:T(8,128)S(1)}, u32[]{:S(2)}, u32[]{:S(2)}) collective-permute-start(f32[384,128]{1,0:T(8,128)S(1)} %collective-permute-done.9.refs_9_), channel_id=1, source_target_pairs={{0,8},{8,0},{16,24},{24,16},{1,9},{9,1},{17,25},{25,17},{2,10},{10... | collective-permute-start | bytes 589832 | tf_op jit(solution)/shard_map/ppermute | solution.py:350

commit v3 on v2

--- a/solution.py
+++ b/solution.py
@@ -12,7 +12,7 @@
 TILE = 256
 CHUNKS = 2
 EARLY = 3
-SMALL = pl.CostEstimate(flops=1000, bytes_accessed=0, transcendentals=0)
+NO_COST = pl.CostEstimate(flops=0, bytes_accessed=0, transcendentals=0)
 F32 = jnp.float32
 BF16 = jnp.bfloat16
 VMEM_LIMIT = 8 * 1024 * 1024
@@ -115,7 +115,7 @@
         out_shape=outs,
         scratch_shapes=[pltpu.SemaphoreType.DMA((3, CHUNKS, 4))],
         compiler_params=params(),
-        cost_estimate=SMALL,
+        cost_estimate=NO_COST,
         name="kvsum",
     )(where, in_hbm(k), in_hbm(v), in_hbm(q))
     return [results[KVSUM_OUTS * j : KVSUM_OUTS * (j + 1)] for j in range(CHUNKS)], results[-1]
@@ -224,7 +224,7 @@
         out_shape=outs,
         scratch_shapes=[pltpu.SemaphoreType.DMA((CHUNKS, 4))] * first,
         compiler_params=params(),
-        cost_estimate=SMALL,
+        cost_estimate=NO_COST,
         name="local_attention",
     )(where, *([in_hbm(q)] if first else []), *[in_vmem(a) for a in (*queries, *k_parts, *v_parts)])
     return results[: len(places)], results[len(places) :]
@@ -269,7 +269,7 @@
         scratch_shapes=[pltpu.VMEM((4, tokens, width), BF16), pltpu.SemaphoreType.DMA((4,))],
         input_output_aliases={len(operands): 0} if earlier else {},
         compiler_params=params(),
-        cost_estimate=SMALL,
+        cost_estimate=NO_COST,
         name="finish",
     )(*operands, *earlier)
 
@@ -290,9 +290,14 @@
         out_specs=specs(*[pltpu.VMEM] * count),
         out_shape=[jax.ShapeDtypeStruct(shape, F32)] * count,
         compiler_params=params(),
-        cost_estimate=SMALL,
+        cost_estimate=NO_COST,
         name="combine",
     )(where, *operands)
+
+
+def send(name, array, axis, pairs):
+    with jax.named_scope(name):
+        return lax.ppermute(array, axis, pairs)
 
 
 def tie(*values):
@@ -309,45 +314,54 @@
     other_chip = [(0, 2), (2, 0), (1, 3), (3, 1)]
 
     sums, q_lead = kvsum(where, q, k, v, width)
-    lead = [lax.ppermute(s[0], "seq", other_core) for s in sums]
+    lead = [send(f"lead{j}", s[0], "seq", other_core) for j, s in enumerate(sums)]
     there = [s[3] + r for s, r in zip(sums, lead)]
-    rest = [lax.ppermute(s[1], "seq", other_core) for s in sums]
+    rest = []
+    for j, s in enumerate(sums):
+        there[0], held = tie(there[0], s[1])
+        rest.append(send(f"rest{j}", held, "seq", other_core))
     k_parts, v_parts = [s[4] for s in sums], [s[5] for s in sums]
     every = [(j, n) for j in chunks for n in range(4)]
-    there[0], held = tie(there[0], where)
-    early, q_slots = local_slots(held, q, q_lead, None, k_parts, v_parts, width, every[:EARLY])
-    q_slots = dict(zip(every, [q_lead, *q_slots]))
-    *later_there, early = tie(*there[1:], early)
-    there[1:] = later_there
-    from_chip = [lax.ppermute(t, "seq", other_chip) for t in there]
+    local, q_slots = [], None
+    for j in chunks[:-1]:
+        there[j], held = tie(there[j], where)
+        places = every[len(local) : len(local) + EARLY]
+        if j == 0:
+            part, q_slots = local_slots(held, q, q_lead, None, k_parts, v_parts, width, places)
+            q_slots = dict(zip(every, [q_lead, *q_slots]))
+        else:
+            part, _ = local_slots(held, None, None, q_slots, k_parts, v_parts, width, places)
+        there[j + 1], part = tie(there[j + 1], part)
+        local += part
+    from_chip = [send(f"chip{j}", t, "seq", other_chip) for j, t in enumerate(there)]
     here = [s[2] + r[0] for s, r in zip(sums, rest)]
-    first_total, held = tie(here[0] + from_chip[0], where)
-    late, _ = local_slots(held, None, None, q_slots, k_parts, v_parts, width, every[EARLY:])
-    *later_chip, late = tie(*from_chip[1:], late)
-    from_chip[1:] = later_chip
-    group_total = [first_total] + [h + r for h, r in zip(here[1:], from_chip[1:])]
-    local = dict(zip(every, [*early, *late]))
+    group_total = [h + r for h, r in zip(here, from_chip)]
 
     arrived = [[] for _ in chunks]
     passing = group_total
     for hop in range(groups - 1):
-        received = [lax.ppermute(p, "grp", [(hop, hop + 1)]) for p in passing]
+        if hop == min(1, groups - 2):
+            passing[-1], held = tie(passing[-1], where)
+            late, _ = local_slots(held, None, None, q_slots, k_parts, v_parts, width, every[len(local) :])
+        received = [send(f"hop{hop}_{j}", p, "grp", [(hop, hop + 1)]) for j, p in enumerate(passing)]
+        if hop == min(1, groups - 2):
+            received[0], late = tie(received[0], late)
         for j in chunks:
             arrived[j].append(received[j])
         passing = [r + g for r, g in zip(received, group_total)]
 
+    local = dict(zip(every, [*local, *late]))
+
     def turn(core, chip, here, from_chip, *arrived):
         before = sum(arrived[1:], arrived[0])
         return before + (1.0 - chip) * here, before + chip * from_chip
 
     turned = [combine(turn, 2, where, here[j], from_chip[j], *arrived[j]) for j in chunks]
-    from_chip_back = [lax.ppermute(back, "seq", other_chip) for back, _ in turned]
-    near_back = [lax.ppermute(own, "seq", other_core) for _, own in turned]
+    from_chip_back = [send(f"chipback{j}", t[0], "seq", other_chip) for j, t in enumerate(turned)]
+    near_back = [send(f"near{j}", t[1], "seq", other_core) for j, t in enumerate(turned)]
     out = None
     for j in chunks:
-        if out is not None:
-            from_chip_back[j], out = tie(from_chip_back[j], out)
-        far_back = lax.ppermute(from_chip_back[j], "seq", other_core)
+        far_back = send(f"far{j}", from_chip_back[j], "seq", other_core)
         states = (turned[j][1], from_chip_back[j], lead[j], rest[j], near_back[j], far_back)
         queries = [q_slots[j, n] for n in range(4)]
         mixed = [local[j, n] for n in range(4)]

time: 53.3 us -> 50.3 us (0.944)
  starting transfers between devices: 21.3 us -> 18.1 us
    ppermute x18, starting transfers between devices: 21.3 us -> 18.1 us  [send(): return lax.ppermute(array, axis, pairs)]
  transfers between devices with their start and end apart: 18 -> 18, of which waited for: 6 -> 5; matrix products, arithmetic and copies ran while one was open for 0% -> 0% of each run, Pallas kernels for 21% -> 23%
where the time goes in v3:
time: 50.3 us; the launch traced here: 50 us
  Pallas kernels  18.2 us (36%)
  starting transfers between devices  18.1 us (36%)
  waiting for transfers between devices  13.1 us (26%)
    ppermute x18, starting transfers between devices, send(): return lax.ppermute(array, axis, pairs)  18.1 us
    ppermute x18, waiting for transfers between devices, send(): return lax.ppermute(array, axis, pairs)  13.1 us
    pallas_call x2, Pallas kernels, local_slots(): pl.pallas_call(kernel, in_specs=specs(pltpu.SMEM, *[pltpu.HBM] * first, *...  7.58 us
    pallas_call x2, Pallas kernels, finish(): pl.pallas_call(functools.partial(finish_kernel, first, width), in_specs=s...  5.03 us
    pallas_call x1, Pallas kernels, kvsum(): pl.pallas_call(functools.partial(kvsum_kernel, width), in_specs=specs(plt...  4.39 us
    pallas_call x2, Pallas kernels, combine(): pl.pallas_call(kernel, in_specs=specs(pltpu.SMEM, *[pltpu.VMEM] * len(ope...  1.2 us
  transfers between devices with their start and end apart: 18, of which 5 were waited for; matrix products, arithmetic and copies ran while one was open for 0% of the time, Pallas kernels for 23%

profile of v3, /device:TPU:25, one launch (start us, length us, event | category | flops | bytes accessed | tf_op | source)
XLA Modules:
  0.0 50.0 jit_solution(1303406624568140612)
XLA Ops:
  0.1 4.4 %kvsum.1 = (f32[384,128]{1,0:T(8,128)S(1)}, f32[3,384,128]{2,1,0:T(8,128)S(1)}, f32[384,128]{1,0:T(8,128)S(1)}, f32[384,128]{1,0:T(8,128)S(1)}, bf16[4,512,384]{...) custom-call(s32[2]{0:T(128)S(1)} %pad_add_fusion.where_ref, ...), custom_call_target="tpu_custom_call" | custom-call | tf_op jit(solution)/shard_map/kvsum/pallas_call | solution.py:111
  4.5 0.7 %collective-permute-start = (f32[384,128]{1,0:T(8,128)S(1)}, f32[384,128]{1,0:T(8,128)S(1)}, u32[]{:S(2)}, u32[]{:S(2)}) collective-permute-start(f32[384,128]{1,0:T(8,128)S(1)} %get-tuple-element.56), channel_id=1, source_target_pairs={{0,8},{8,0},{16,24},{24,16},{1,9},{9,1},{17,25},{25,17},{2,10},{10... | collective-permute-start | bytes 589832 | tf_op jit(solution)/shard_map/lead0/ppermute | solution.py:300
  5.2 1.1 %collective-permute-done.refs_10_ = f32[384,128]{1,0:T(8,128)S(1)} collective-permute-done((f32[384,128]{1,0:T(8,128)S(1)}, f32[384,128]{1,0:T(8,128)S(1)}, u32[]{:S(2)}, u32[]{:S(2)}) %collective-permute-start) | collective-permute-done | bytes 196640 | tf_op jit(solution)/shard_map/lead0/ppermute | solution.py:300
  7.3 1.2 %collective-permute-start.2 = (f32[384,128]{1,0:T(8,128)S(1)}, f32[384,128]{1,0:T(8,128)S(1)}, u32[]{:S(2)}, u32[]{:S(2)}) collective-permute-start(f32[384,128]{1,0:T(8,128)S(1)} %add.36), channel_id=1, source_target_pairs={{0,16},{16,0},{8,24},{24,8},{1,17},{17,1},{9,25},{25,9},{2,18},{18... | collective-permute-start | bytes 589832 | tf_op jit(solution)/shard_map/chip0/ppermute | solution.py:300
  8.5 3.8 %local_attention.2 = (f32[512,384]{1,0:T(8,128)S(1)}, f32[512,384]{1,0:T(8,128)S(1)}, f32[512,384]{1,0:T(8,128)S(1)}, bf16[512,384]{1,0:T(8,128)(2,1)S(1)}, bf16...) custom-call(s32[2]{0:T(128)S(1)} %pad_add_fusion.where_ref, ...), custom_call_target="tpu_custom_call" | custom-call | tf_op jit(solution)/shard_map/local_attention/pallas_call | solution.py:218
  12.6 1.0 %collective-permute-done.2.refs_1_ = f32[384,128]{1,0:T(8,128)S(1)} collective-permute-done((f32[384,128]{1,0:T(8,128)S(1)}, f32[384,128]{1,0:T(8,128)S(1)}, u32[]{:S(2)}, u32[]{:S(2)}) %collective-permute-start.2) | collective-permute-done | bytes 196640 | tf_op jit(solution)/shard_map/chip0/ppermute | solution.py:300
  13.7 0.7 %collective-permute-start.3 = (f32[384,128]{1,0:T(8,128)S(1)}, f32[384,128]{1,0:T(8,128)S(1)}, u32[]{:S(2)}, u32[]{:S(2)}) collective-permute-start(f32[384,128]{1,0:T(8,128)S(1)} %get-tuple-element.107), channel_id=1, source_target_pairs={{0,2},{1,3},{8,10},{9,11},{16,18},{17,19},{24,26},{25,27}} | collective-permute-start | bytes 589832 | tf_op jit(solution)/shard_map/hop0_0/ppermute | solution.py:300
  14.4 4.0 %collective-permute-done.7.refs_1_ = f32[384,128]{1,0:T(8,128)S(1)} collective-permute-done((f32[384,128]{1,0:T(8,128)S(1)}, f32[384,128]{1,0:T(8,128)S(1)}, u32[]{:S(2)}, u32[]{:S(2)}) %collective-permute-start.7) | collective-permute-done | bytes 196640 | tf_op jit(solution)/shard_map/chip1/ppermute | solution.py:300
  18.4 0.7 %collective-permute-start.8 = (f32[384,128]{1,0:T(8,128)S(1)}, f32[384,128]{1,0:T(8,128)S(1)}, u32[]{:S(2)}, u32[]{:S(2)}) collective-permute-start(f32[384,128]{1,0:T(8,128)S(1)} %get-tuple-element.105), channel_id=1, source_target_pairs={{0,2},{1,3},{8,10},{9,11},{16,18},{17,19},{24,26},{25,27}} | collective-permute-start | bytes 589832 | tf_op jit(solution)/shard_map/hop0_1/ppermute | solution.py:300
  19.1 0.7 %collective-permute-start.4 = (f32[384,128]{1,0:T(8,128)S(1)}, f32[384,128]{1,0:T(8,128)S(1)}, u32[]{:S(2)}, u32[]{:S(2)}) collective-permute-start(f32[384,128]{1,0:T(8,128)S(1)} %add.39), channel_id=1, source_target_pairs={{2,4},{3,5},{10,12},{11,13},{18,20},{19,21},{26,28},{27,29}} | collective-permute-start | bytes 589832 | tf_op jit(solution)/shard_map/hop1_0/ppermute | solution.py:300
  19.9 0.7 %collective-permute-start.9 = (f32[384,128]{1,0:T(8,128)S(1)}, f32[384,128]{1,0:T(8,128)S(1)}, u32[]{:S(2)}, u32[]{:S(2)}) collective-permute-start(f32[384,128]{1,0:T(8,128)S(1)} %add.43), channel_id=1, source_target_pairs={{2,4},{3,5},{10,12},{11,13},{18,20},{19,21},{26,28},{27,29}} | collective-permute-start | bytes 589832 | tf_op jit(solution)/shard_map/hop1_1/ppermute | solution.py:300
  20.5 3.8 %local_attention.3 = (f32[512,384]{1,0:T(8,128)S(1)}, f32[512,384]{1,0:T(8,128)S(1)}, f32[512,384]{1,0:T(8,128)S(1)}, f32[512,384]{1,0:T(8,128)S(1)}, f32[512,384]{1,0:T(8,128)S(1)}) custom-call(s32[2]{0:T(128)S(1)} %pad_add_fusion.where_ref, bf16[512,384]{1,0:T(8,128)(2,1)S(1)} %get-tuple-element.83.refs_0_.refs_3_, ...), custom_call_target="tpu_custom_call" | custom-call | tf_op jit(solution)/shard_map/local_attention/pallas_call | solution.py:218
  24.4 1.3 %collective-permute-start.14 = (f32[384,128]{1,0:T(8,128)S(1)}, f32[384,128]{1,0:T(8,128)S(1)}, u32[]{:S(2)}, u32[]{:S(2)}) collective-permute-start(f32[384,128]{1,0:T(8,128)S(1)} %add.45), channel_id=1, source_target_pairs={{4,6},{5,7},{12,14},{13,15},{20,22},{21,23},{28,30},{29,31}} | collective-permute-start | bytes 589832 | tf_op jit(solution)/shard_map/hop2_0/ppermute | solution.py:300
  25.8 1.3 %collective-permute-start.10 = (f32[384,128]{1,0:T(8,128)S(1)}, f32[384,128]{1,0:T(8,128)S(1)}, u32[]{:S(2)}, u32[]{:S(2)}) collective-permute-start(f32[384,128]{1,0:T(8,128)S(1)} %add.44), channel_id=1, source_target_pairs={{4,6},{5,7},{12,14},{13,15},{20,22},{21,23},{28,30},{29,31}} | collective-permute-start | bytes 589832 | tf_op jit(solution)/shard_map/hop2_1/ppermute | solution.py:300
  27.1 3.8 %collective-permute-done.14.refs_4_ = f32[384,128]{1,0:T(8,128)S(1)} collective-permute-done((f32[384,128]{1,0:T(8,128)S(1)}, f32[384,128]{1,0:T(8,128)S(1)}, u32[]{:S(2)}, u32[]{:S(2)}) %collective-permute-start.14) | collective-permute-done | bytes 196640 | tf_op jit(solution)/shard_map/hop2_0/ppermute | solution.py:300
  30.8 0.6 %combine.3 = (f32[384,128]{1,0:T(8,128)S(1)}, f32[384,128]{1,0:T(8,128)S(1)}) custom-call(s32[2]{0:T(128)S(1)} %pad_add_fusion.where_ref, f32[384,128]{1,0:T(8,128)S(1)} %get-tuple-element.108.refs_0_, f32[384,128]{1,0:T(8,128)S(1)} %collective-permute-done.2.refs_1_, f32[384,128]{1,0:T(8,128)S(1)} %collective-permute-done.3.refs_2_, ...), custom_call_target="tpu_custom_call" | custom-call | tf_op jit(solution)/shard_map/combine/pallas_call | solution.py:287
  32.0 3.2 %collective-permute-done.10.refs_4_ = f32[384,128]{1,0:T(8,128)S(1)} collective-permute-done((f32[384,128]{1,0:T(8,128)S(1)}, f32[384,128]{1,0:T(8,128)S(1)}, u32[]{:S(2)}, u32[]{:S(2)}) %collective-permute-start.10) | collective-permute-done | bytes 196640 | tf_op jit(solution)/shard_map/hop2_1/ppermute | solution.py:300
  35.2 0.6 %combine.2 = (f32[384,128]{1,0:T(8,128)S(1)}, f32[384,128]{1,0:T(8,128)S(1)}) custom-call(s32[2]{0:T(128)S(1)} %pad_add_fusion.where_ref, f32[384,128]{1,0:T(8,128)S(1)} %get-tuple-element.106.refs_0_, f32[384,128]{1,0:T(8,128)S(1)} %collective-permute-done.7.refs_1_, f32[384,128]{1,0:T(8,128)S(1)} %collective-permute-done.8.refs_2_, ...), custom_call_target="tpu_custom_call" | custom-call | tf_op jit(solution)/shard_map/combine/pallas_call | solution.py:287
  35.8 1.5 %collective-permute-start.11 = (f32[384,128]{1,0:T(8,128)S(1)}, f32[384,128]{1,0:T(8,128)S(1)}, u32[]{:S(2)}, u32[]{:S(2)}) collective-permute-start(f32[384,128]{1,0:T(8,128)S(1)} %get-tuple-element.95), channel_id=1, source_target_pairs={{0,16},{16,0},{8,24},{24,8},{1,17},{17,1},{9,25},{25,9},{2,18},{18... | collective-permute-start | bytes 589832 | tf_op jit(solution)/shard_map/chipback1/ppermute | solution.py:300
  37.2 3.1 %collective-permute-start.16 = (f32[384,128]{1,0:T(8,128)S(1)}, f32[384,128]{1,0:T(8,128)S(1)}, u32[]{:S(2)}, u32[]{:S(2)}) collective-permute-start(f32[384,128]{1,0:T(8,128)S(1)} %get-tuple-element.103.refs_8_), channel_id=1, source_target_pairs={{0,8},{8,0},{16,24},{24,16},{1,9},{9,1},{17,25},{25,17},{2,10},{10... | collective-permute-start | bytes 589832 | tf_op jit(solution)/shard_map/near0/ppermute | solution.py:300
  40.3 2.2 %collective-permute-start.17 = (f32[384,128]{1,0:T(8,128)S(1)}, f32[384,128]{1,0:T(8,128)S(1)}, u32[]{:S(2)}, u32[]{:S(2)}) collective-permute-start(f32[384,128]{1,0:T(8,128)S(1)} %collective-permute-done.15.refs_9_), channel_id=1, source_target_pairs={{0,8},{8,0},{16,24},{24,16},{1,9},{9,1},{17,25},{25,17},{2,10},{10... | collective-permute-start | bytes 589832 | tf_op jit(solution)/shard_map/far0/ppermute | solution.py:300
  42.5 2.4 %collective-permute-start.13 = (f32[384,128]{1,0:T(8,128)S(1)}, f32[384,128]{1,0:T(8,128)S(1)}, u32[]{:S(2)}, u32[]{:S(2)}) collective-permute-start(f32[384,128]{1,0:T(8,128)S(1)} %collective-permute-done.11.refs_9_), channel_id=1, source_target_pairs={{0,8},{8,0},{16,24},{24,16},{1,9},{9,1},{17,25},{25,17},{2,10},{10... | collective-permute-start | bytes 589832 | tf_op jit(solution)/shard_map/far1/ppermute | solution.py:300
  44.9 2.5 %finish.2.refs_14_ = bf16[512,3072]{1,0:T(8,128)(2,1)} custom-call(s32[2]{0:T(128)S(1)} %pad_add_fusion.where_ref, f32[1,3072]{1,0:T(1,128)S(1)} %bitcast.17, bf16[512,384]{1,0:T(8,128)(2,1)S(1)} %get-tuple-element.62.refs_0_, bf16[512,384]{1,0:T(8,128)(2,1)S(1)} %get-tuple-element.96.refs_1_, bf16[512,384]{1,0:T(8,128)(2,1)S(1)} %get-tuple-element.97.refs_2_, ...), custom_call_target="tpu_custom_call" | custom-call | tf_op jit(solution)/shard_map/finish/pallas_call | solution.py:264
  47.5 2.5 %finish.3 = bf16[512,3072]{1,0:T(8,128)(2,1)} custom-call(s32[2]{0:T(128)S(1)} %pad_add_fusion.where_ref, f32[1,3072]{1,0:T(1,128)S(1)} %bitcast.18, bf16[512,384]{1,0:T(8,128)(2,1)S(1)} %get-tuple-element.67.refs_1_.refs_0_, bf16[512,384]{1,0:T(8,128)(2,1)S(1)} %get-tuple-element.68.refs_2_.refs_1_, ...), custom_call_target="tpu_custom_call", output_to_operand_aliasing={{}: (16, {})} | custom-call | tf_op jit(solution)/shard_map/finish/pallas_call | solution.py:264
  (30 shorter events, 2.1 us)
Async XLA Ops:
  4.5 1.8 %collective-permute-start = (f32[384,128]{1,0:T(8,128)S(1)}, f32[384,128]{1,0:T(8,128)S(1)}, u32[]{:S(2)}, u32[]{:S(2)}) collective-permute-start(f32[384,128]{1,0:T(8,128)S(1)} %get-tuple-element.56), channel_id=1, source_target_pairs={{0,8},{8,0},{16,24},{24,16},{1,9},{9,1},{17,25},{25,17},{2,10},{10... | collective-permute-start | bytes 589832 | tf_op jit(solution)/shard_map/lead0/ppermute | solution.py:300
  6.3 7.3 %collective-permute-start.1 = (f32[3,384,128]{2,1,0:T(8,128)S(1)}, f32[3,384,128]{2,1,0:T(8,128)S(1)}, u32[]{:S(2)}, u32[]{:S(2)}) collective-permute-start(f32[3,384,128]{2,1,0:T(8,128)S(1)} %get-tuple-element.72), channel_id=1, source_target_pairs={{0,8},{8,0},{16,24},{24,16},{1,9},{9,1},{17,25},{25,17},{2,10},{10... | collective-permute-start | bytes 1769480 | tf_op jit(solution)/shard_map/rest0/ppermute | solution.py:300
  6.7 11.6 %collective-permute-start.5 = (f32[3,384,128]{2,1,0:T(8,128)S(1)}, f32[3,384,128]{2,1,0:T(8,128)S(1)}, u32[]{:S(2)}, u32[]{:S(2)}) collective-permute-start(f32[3,384,128]{2,1,0:T(8,128)S(1)} %get-tuple-element.75), channel_id=1, source_target_pairs={{0,8},{8,0},{16,24},{24,16},{1,9},{9,1},{17,25},{25,17},{2,10},{10... | collective-permute-start | bytes 1769480 | tf_op jit(solution)/shard_map/rest1/ppermute | solution.py:300
  6.9 5.4 %collective-permute-start.6 = (f32[384,128]{1,0:T(8,128)S(1)}, f32[384,128]{1,0:T(8,128)S(1)}, u32[]{:S(2)}, u32[]{:S(2)}) collective-permute-start(f32[384,128]{1,0:T(8,128)S(1)} %get-tuple-element.77), channel_id=1, source_target_pairs={{0,8},{8,0},{16,24},{24,16},{1,9},{9,1},{17,25},{25,17},{2,10},{10... | collective-permute-start | bytes 589832 | tf_op jit(solution)/shard_map/lead1/ppermute | solution.py:300
  7.3 6.4 %collective-permute-start.2 = (f32[384,128]{1,0:T(8,128)S(1)}, f32[384,128]{1,0:T(8,128)S(1)}, u32[]{:S(2)}, u32[]{:S(2)}) collective-permute-start(f32[384,128]{1,0:T(8,128)S(1)} %add.36), channel_id=1, source_target_pairs={{0,16},{16,0},{8,24},{24,8},{1,17},{17,1},{9,25},{25,9},{2,18},{18... | collective-permute-start | bytes 589832 | tf_op jit(solution)/shard_map/chip0/ppermute | solution.py:300
  12.3 6.1 %collective-permute-start.7 = (f32[384,128]{1,0:T(8,128)S(1)}, f32[384,128]{1,0:T(8,128)S(1)}, u32[]{:S(2)}, u32[]{:S(2)}) collective-permute-start(f32[384,128]{1,0:T(8,128)S(1)} %add.41), channel_id=1, source_target_pairs={{0,16},{16,0},{8,24},{24,8},{1,17},{17,1},{9,25},{25,9},{2,18},{18... | collective-permute-start | bytes 589832 | tf_op jit(solution)/shard_map/chip1/ppermute | solution.py:300
  13.7 5.4 %collective-permute-start.3 = (f32[384,128]{1,0:T(8,128)S(1)}, f32[384,128]{1,0:T(8,128)S(1)}, u32[]{:S(2)}, u32[]{:S(2)}) collective-permute-start(f32[384,128]{1,0:T(8,128)S(1)} %get-tuple-element.107), channel_id=1, source_target_pairs={{0,2},{1,3},{8,10},{9,11},{16,18},{17,19},{24,26},{25,27}} | collective-permute-start | bytes 589832 | tf_op jit(solution)/shard_map/hop0_0/ppermute | solution.py:300
  18.4 1.4 %collective-permute-start.8 = (f32[384,128]{1,0:T(8,128)S(1)}, f32[384,128]{1,0:T(8,128)S(1)}, u32[]{:S(2)}, u32[]{:S(2)}) collective-permute-start(f32[384,128]{1,0:T(8,128)S(1)} %get-tuple-element.105), channel_id=1, source_target_pairs={{0,2},{1,3},{8,10},{9,11},{16,18},{17,19},{24,26},{25,27}} | collective-permute-start | bytes 589832 | tf_op jit(solution)/shard_map/hop0_1/ppermute | solution.py:300
  19.1 5.2 %collective-permute-start.4 = (f32[384,128]{1,0:T(8,128)S(1)}, f32[384,128]{1,0:T(8,128)S(1)}, u32[]{:S(2)}, u32[]{:S(2)}) collective-permute-start(f32[384,128]{1,0:T(8,128)S(1)} %add.39), channel_id=1, source_target_pairs={{2,4},{3,5},{10,12},{11,13},{18,20},{19,21},{26,28},{27,29}} | collective-permute-start | bytes 589832 | tf_op jit(solution)/shard_map/hop1_0/ppermute | solution.py:300
  19.9 5.9 %collective-permute-start.9 = (f32[384,128]{1,0:T(8,128)S(1)}, f32[384,128]{1,0:T(8,128)S(1)}, u32[]{:S(2)}, u32[]{:S(2)}) collective-permute-start(f32[384,128]{1,0:T(8,128)S(1)} %add.43), channel_id=1, source_target_pairs={{2,4},{3,5},{10,12},{11,13},{18,20},{19,21},{26,28},{27,29}} | collective-permute-start | bytes 589832 | tf_op jit(solution)/shard_map/hop1_1/ppermute | solution.py:300
  24.4 20.6 %copy-start = (f32[3072]{0:T(1024)S(1)}, f32[3072]{0:T(1024)}, u32[]{:S(2)}) copy-start(f32[3072]{0:T(1024)} %param.7) | copy-start | bytes 36868
  24.4 6.4 %collective-permute-start.14 = (f32[384,128]{1,0:T(8,128)S(1)}, f32[384,128]{1,0:T(8,128)S(1)}, u32[]{:S(2)}, u32[]{:S(2)}) collective-permute-start(f32[384,128]{1,0:T(8,128)S(1)} %add.45), channel_id=1, source_target_pairs={{4,6},{5,7},{12,14},{13,15},{20,22},{21,23},{28,30},{29,31}} | collective-permute-start | bytes 589832 | tf_op jit(solution)/shard_map/hop2_0/ppermute | solution.py:300
  25.8 9.4 %collective-permute-start.10 = (f32[384,128]{1,0:T(8,128)S(1)}, f32[384,128]{1,0:T(8,128)S(1)}, u32[]{:S(2)}, u32[]{:S(2)}) collective-permute-start(f32[384,128]{1,0:T(8,128)S(1)} %add.44), channel_id=1, source_target_pairs={{4,6},{5,7},{12,14},{13,15},{20,22},{21,23},{28,30},{29,31}} | collective-permute-start | bytes 589832 | tf_op jit(solution)/shard_map/hop2_1/ppermute | solution.py:300
  31.4 8.9 %collective-permute-start.15 = (f32[384,128]{1,0:T(8,128)S(1)}, f32[384,128]{1,0:T(8,128)S(1)}, u32[]{:S(2)}, u32[]{:S(2)}) collective-permute-start(f32[384,128]{1,0:T(8,128)S(1)} %get-tuple-element.104), channel_id=1, source_target_pairs={{0,16},{16,0},{8,24},{24,8},{1,17},{17,1},{9,25},{25,9},{2,18},{18... | collective-permute-start | bytes 589832 | tf_op jit(solution)/shard_map/chipback0/ppermute | solution.py:300
  35.8 6.7 %collective-permute-start.11 = (f32[384,128]{1,0:T(8,128)S(1)}, f32[384,128]{1,0:T(8,128)S(1)}, u32[]{:S(2)}, u32[]{:S(2)}) collective-permute-start(f32[384,128]{1,0:T(8,128)S(1)} %get-tuple-element.95), channel_id=1, source_target_pairs={{0,16},{16,0},{8,24},{24,8},{1,17},{17,1},{9,25},{25,9},{2,18},{18... | collective-permute-start | bytes 589832 | tf_op jit(solution)/shard_map/chipback1/ppermute | solution.py:300
  37.2 7.7 %collective-permute-start.16 = (f32[384,128]{1,0:T(8,128)S(1)}, f32[384,128]{1,0:T(8,128)S(1)}, u32[]{:S(2)}, u32[]{:S(2)}) collective-permute-start(f32[384,128]{1,0:T(8,128)S(1)} %get-tuple-element.103.refs_8_), channel_id=1, source_target_pairs={{0,8},{8,0},{16,24},{24,16},{1,9},{9,1},{17,25},{25,17},{2,10},{10... | collective-permute-start | bytes 589832 | tf_op jit(solution)/shard_map/near0/ppermute | solution.py:300
  40.3 4.6 %collective-permute-start.17 = (f32[384,128]{1,0:T(8,128)S(1)}, f32[384,128]{1,0:T(8,128)S(1)}, u32[]{:S(2)}, u32[]{:S(2)}) collective-permute-start(f32[384,128]{1,0:T(8,128)S(1)} %collective-permute-done.15.refs_9_), channel_id=1, source_target_pairs={{0,8},{8,0},{16,24},{24,16},{1,9},{9,1},{17,25},{25,17},{2,10},{10... | collective-permute-start | bytes 589832 | tf_op jit(solution)/shard_map/far0/ppermute | solution.py:300
  42.5 5.0 %collective-permute-start.12 = (f32[384,128]{1,0:T(8,128)S(1)}, f32[384,128]{1,0:T(8,128)S(1)}, u32[]{:S(2)}, u32[]{:S(2)}) collective-permute-start(f32[384,128]{1,0:T(8,128)S(1)} %get-tuple-element.94.refs_8_), channel_id=1, source_target_pairs={{0,8},{8,0},{16,24},{24,16},{1,9},{9,1},{17,25},{25,17},{2,10},{10... | collective-permute-start | bytes 589832 | tf_op jit(solution)/shard_map/near1/ppermute | solution.py:300
  42.5 5.0 %collective-permute-start.13 = (f32[384,128]{1,0:T(8,128)S(1)}, f32[384,128]{1,0:T(8,128)S(1)}, u32[]{:S(2)}, u32[]{:S(2)}) collective-permute-start(f32[384,128]{1,0:T(8,128)S(1)} %collective-permute-done.11.refs_9_), channel_id=1, source_target_pairs={{0,8},{8,0},{16,24},{24,16},{1,9},{9,1},{17,25},{25,17},{2,10},{10... | collective-permute-start | bytes 589832 | tf_op jit(solution)/shard_map/far1/ppermute | solution.py:300

commit v4 on v3

--- a/solution.py
+++ b/solution.py
@@ -11,7 +11,7 @@
 BLK = 512
 TILE = 256
 CHUNKS = 2
-EARLY = 3
+EARLY = 2
 NO_COST = pl.CostEstimate(flops=0, bytes_accessed=0, transcendentals=0)
 F32 = jnp.float32
 BF16 = jnp.bfloat16
@@ -40,9 +40,14 @@
     return pl.multiple_of((half * 2 + quarter) * width, DH)
 
 
+def place():
+    position = lax.axis_index("seq")
+    return position & 1, position >> 1
+
+
 class Slots:
-    def __init__(self, where_ref, width):
-        self.core, self.chip, self.width = where_ref[0], where_ref[1], width
+    def __init__(self, width):
+        (self.core, self.chip), self.width = place(), width
 
     def column(self, first, slot):
         return pl.multiple_of(first + slot_column(slot, self.width, self.core, self.chip), DH)
@@ -60,17 +65,17 @@
 
 
 SLOT_ORDER = (3, 2, 0, 1)
-KVSUM_OUTS = 6
-
-
-def kvsum_kernel(width, where_ref, k_hbm, v_hbm, q_hbm, *refs):
-    *refs, q_ref, sems = refs
-    slots = Slots(where_ref, width)
+KVSUM_OUTS = 4
+
+
+def kvsum_kernel(width, k_hbm, v_hbm, q_hbm, *refs):
+    *refs, lead, rest, q_ref, sems = refs
+    slots = Slots(width)
     outs = [refs[KVSUM_OUTS * j : KVSUM_OUTS * (j + 1)] for j in range(CHUNKS)]
     loads = []
     for slot in SLOT_ORDER:
         for j in range(CHUNKS):
-            k_ref, v_ref = outs[j][4:]
+            k_ref, v_ref = outs[j][2:]
             first = 4 * width * j
             loads.append(
                 (
@@ -84,7 +89,7 @@
     for slot, j, *copies in loads:
         for copy in copies:
             copy.wait()
-        lead, rest, own, other, k_ref, v_ref = outs[j]
+        own, other, k_ref, v_ref = outs[j]
         for i in range(width // DH):
             c = head_cols(i)
             total = lax.dot_general(
@@ -94,31 +99,32 @@
                 preferred_element_type=F32,
             )
             if slot == 3:
-                lead[c, :] = total
+                lead[j, c, :] = total
             else:
-                rest[(slot + 1) % 3, c, :] = total
+                rest[j, (slot + 1) % 3, c, :] = total
             if slot < 2:
                 (own, other)[slot][c, :] = total
     q_load.wait()
 
 
-def kvsum(where, q, k, v, width):
+def kvsum(q, k, v, width):
     tokens = k.shape[0]
     one = pltpu.VMEM((width, DH), F32)
     part = pltpu.VMEM((4, tokens, width), BF16)
-    outs = [one, pltpu.VMEM((3, width, DH), F32), one, one, part, part] * CHUNKS
+    outs = [one, one, part, part] * CHUNKS
+    outs += [pltpu.VMEM((CHUNKS, width, DH), F32), pltpu.VMEM((CHUNKS, 3, width, DH), F32)]
     outs.append(pltpu.VMEM((tokens, width), BF16))
     results = pl.pallas_call(
         functools.partial(kvsum_kernel, width),
-        in_specs=specs(pltpu.SMEM, *[pltpu.HBM] * 3),
+        in_specs=specs(*[pltpu.HBM] * 3),
         out_specs=specs(*[pltpu.VMEM] * len(outs)),
         out_shape=outs,
         scratch_shapes=[pltpu.SemaphoreType.DMA((3, CHUNKS, 4))],
         compiler_params=params(),
         cost_estimate=NO_COST,
         name="kvsum",
-    )(where, in_hbm(k), in_hbm(v), in_hbm(q))
-    return [results[KVSUM_OUTS * j : KVSUM_OUTS * (j + 1)] for j in range(CHUNKS)], results[-1]
+    )(in_hbm(k), in_hbm(v), in_hbm(q))
+    return [results[KVSUM_OUTS * j : KVSUM_OUTS * (j + 1)] for j in range(CHUNKS)], results[-3:]
 
 
 def local_scores(q_ref, k_ref, c):
@@ -175,7 +181,7 @@
     )(q, k, v)
 
 
-def local_slots_kernel(width, places, where_ref, q_hbm, *refs):
+def local_slots_kernel(width, places, q_hbm, *refs):
     count = len(places)
     if q_hbm is None:
         q_refs, loads = dict(zip(places, refs)), {}
@@ -185,7 +191,7 @@
         *refs, sems = refs
         q_refs = dict(zip(every, [refs[0], *refs[-len(every) + 1 :]]))
         refs = refs[1:]
-        slots = Slots(where_ref, width)
+        slots = Slots(width)
         loads = {
             (j, n): slots.load(4 * width * j, n, q_hbm, q_refs[j, n], sems.at[j, n])
             for j, n in every[1:]
@@ -205,68 +211,70 @@
         copy.wait()
 
 
-def local_slots(where, q, q_lead, q_slots, k_parts, v_parts, width, places):
+def local_slots(q, q_lead, q_slots, k_parts, v_parts, width, places):
     tokens = k_parts[0].shape[1]
     first = q_lead is not None
     every = 4 * CHUNKS
     kernel = functools.partial(local_slots_kernel, width, places)
     if not first:
-        kernel = lambda where_ref, *refs: local_slots_kernel(width, places, where_ref, None, *refs)
+        kernel = lambda *refs: local_slots_kernel(width, places, None, *refs)
     queries = [q_lead] if first else [q_slots[p] for p in places]
     outs = [pltpu.VMEM((tokens, width), F32)] * len(places)
     outs += [pltpu.VMEM((tokens, width), BF16)] * ((every - 1) * first)
     results = pl.pallas_call(
         kernel,
-        in_specs=specs(
-            pltpu.SMEM, *[pltpu.HBM] * first, *[pltpu.VMEM] * (len(queries) + 2 * CHUNKS)
-        ),
+        in_specs=specs(*[pltpu.HBM] * first, *[pltpu.VMEM] * (len(queries) + 2 * CHUNKS)),
         out_specs=specs(*[pltpu.VMEM] * len(outs)),
         out_shape=outs,
         scratch_shapes=[pltpu.SemaphoreType.DMA((CHUNKS, 4))] * first,
         compiler_params=params(),
         cost_estimate=NO_COST,
         name="local_attention",
-    )(where, *([in_hbm(q)] if first else []), *[in_vmem(a) for a in (*queries, *k_parts, *v_parts)])
+    )(*([in_hbm(q)] if first else []), *[in_vmem(a) for a in (*queries, *k_parts, *v_parts)])
     return results[: len(places)], results[len(places) :]
 
 
-def finish_kernel(first, width, where_ref, gain_ref, *refs):
-    q_refs, mixed_refs = refs[:4], refs[4:8]
-    own_near, own_far, lead_ref, rest_ref, far_near, far_far = refs[8:14]
+def finish_kernel(places, width, gain_ref, *refs):
     out_hbm, out_ref, sems = refs[-3:]
-    slots = Slots(where_ref, width)
+    slots = Slots(width)
     second = slots.core.astype(F32)
-    states = (own_near, own_far, far_near, far_far)
-    from_core = (rest_ref.at[0], lead_ref, rest_ref.at[1], rest_ref.at[2])
     stores = []
-    for n in range(4):
-        column = slots.column(first, n)
+    for m, (j, n) in enumerate(places):
+        q_ref, mixed_ref, state_ref, from_core = refs[4 * m : 4 * m + 4]
+        column = slots.column(4 * width * j, n)
         for i in range(width // DH):
             c = head_cols(i)
-            state = states[n][c, :] + second * from_core[n][c, :]
-            mixed = mixed_refs[n][:, c] + jnp.dot(
-                q_refs[n][:, c], state.astype(BF16), preferred_element_type=F32
+            other = from_core[j, c, :] if n == 1 else from_core[j, max(n - 1, 0), c, :]
+            state = state_ref[c, :] + second * other
+            mixed = mixed_ref[:, c] + jnp.dot(
+                q_ref[:, c], state.astype(BF16), preferred_element_type=F32
             )
             meansq = jnp.mean(mixed * mixed, axis=-1, keepdims=True)
             gain = gain_ref[:, pl.ds(pl.multiple_of(column + i * DH, DH), DH)]
-            out_ref[n, :, c] = (mixed * lax.rsqrt(meansq + 1e-05) * gain).astype(BF16)
-        store = pltpu.make_async_copy(out_ref.at[n], out_hbm.at[:, pl.ds(column, width)], sems.at[n])
+            out_ref[m, :, c] = (mixed * lax.rsqrt(meansq + 1e-05) * gain).astype(BF16)
+        store = pltpu.make_async_copy(out_ref.at[m], out_hbm.at[:, pl.ds(column, width)], sems.at[m])
         store.start()
         stores.append(store)
     for store in stores:
         store.wait()
 
 
-def finish(where, gain, queries, mixed, states, out, first, width):
-    tokens = queries[0].shape[0]
+def finish(gain, slots, out, width):
+    places = list(slots)
+    tokens = slots[places[0]][0].shape[0]
     earlier = [] if out is None else [out]
-    operands = [where, gain, *[in_vmem(a) for a in (*queries, *mixed)], *states]
+    operands = [gain]
+    for q, mixed, state, from_core in slots.values():
+        operands += [in_vmem(q), in_vmem(mixed), state, from_core]
     return pl.pallas_call(
-        functools.partial(finish_kernel, first, width),
-        in_specs=specs(pltpu.SMEM, *[pltpu.VMEM] * (len(operands) - 1), *[pltpu.HBM] * len(earlier)),
+        functools.partial(finish_kernel, places, width),
+        in_specs=specs(*[pltpu.VMEM] * len(operands), *[pltpu.HBM] * len(earlier)),
         out_specs=specs(pltpu.HBM)[0],
         out_shape=jax.ShapeDtypeStruct((tokens, gain.shape[1]), BF16),
-        scratch_shapes=[pltpu.VMEM((4, tokens, width), BF16), pltpu.SemaphoreType.DMA((4,))],
+        scratch_shapes=[
+            pltpu.VMEM((len(places), tokens, width), BF16),
+            pltpu.SemaphoreType.DMA((len(places),)),
+        ],
         input_output_aliases={len(operands): 0} if earlier else {},
         compiler_params=params(),
         cost_estimate=NO_COST,
@@ -274,30 +282,36 @@
     )(*operands, *earlier)
 
 
-def combine(compute, count, where, *operands):
+def combine(compute, count, *operands):
     shape = operands[0].shape
 
-    def kernel(where_ref, *refs):
+    def kernel(*refs):
         ins, outs = refs[: len(operands)], refs[len(operands) :]
-        core, chip = where_ref[0].astype(F32), where_ref[1].astype(F32)
+        core, chip = (a.astype(F32) for a in place())
         results = compute(core, chip, *[r[...] for r in ins])
         for ref, value in zip(outs, results):
             ref[...] = value
 
-    return pl.pallas_call(
+    results = pl.pallas_call(
         kernel,
-        in_specs=specs(pltpu.SMEM, *[pltpu.VMEM] * len(operands)),
+        in_specs=specs(*[pltpu.VMEM] * len(operands)),
         out_specs=specs(*[pltpu.VMEM] * count),
         out_shape=[jax.ShapeDtypeStruct(shape, F32)] * count,
         compiler_params=params(),
         cost_estimate=NO_COST,
         name="combine",
-    )(where, *operands)
+    )(*operands)
+    return list(results)
 
 
 def send(name, array, axis, pairs):
     with jax.named_scope(name):
         return lax.ppermute(array, axis, pairs)
+
+
+def add_to(core, chip, *arrays):
+    *arrays, parts = arrays
+    return [a + (parts[j] if parts.ndim == 3 else parts[j, 0]) for j, a in enumerate(arrays)]
 
 
 def tie(*values):
@@ -313,36 +327,34 @@
     other_core = [(0, 1), (1, 0), (2, 3), (3, 2)]
     other_chip = [(0, 2), (2, 0), (1, 3), (3, 1)]
 
-    sums, q_lead = kvsum(where, q, k, v, width)
-    lead = [send(f"lead{j}", s[0], "seq", other_core) for j, s in enumerate(sums)]
-    there = [s[3] + r for s, r in zip(sums, lead)]
-    rest = []
-    for j, s in enumerate(sums):
-        there[0], held = tie(there[0], s[1])
-        rest.append(send(f"rest{j}", held, "seq", other_core))
-    k_parts, v_parts = [s[4] for s in sums], [s[5] for s in sums]
+    sums, (lead, rest, q_lead) = kvsum(q, k, v, width)
+    lead = send("lead", lead, "seq", other_core)
+    there = combine(add_to, CHUNKS, *[s[1] for s in sums], lead)
+    there[0], rest = tie(there[0], rest)
+    rest = send("rest", rest, "seq", other_core)
+    k_parts, v_parts = [s[2] for s in sums], [s[3] for s in sums]
     every = [(j, n) for j in chunks for n in range(4)]
     local, q_slots = [], None
     for j in chunks[:-1]:
-        there[j], held = tie(there[j], where)
+        there[j], k_parts[0] = tie(there[j], k_parts[0])
         places = every[len(local) : len(local) + EARLY]
         if j == 0:
-            part, q_slots = local_slots(held, q, q_lead, None, k_parts, v_parts, width, places)
+            part, q_slots = local_slots(q, q_lead, None, k_parts, v_parts, width, places)
             q_slots = dict(zip(every, [q_lead, *q_slots]))
         else:
-            part, _ = local_slots(held, None, None, q_slots, k_parts, v_parts, width, places)
+            part, _ = local_slots(None, None, q_slots, k_parts, v_parts, width, places)
         there[j + 1], part = tie(there[j + 1], part)
         local += part
     from_chip = [send(f"chip{j}", t, "seq", other_chip) for j, t in enumerate(there)]
-    here = [s[2] + r[0] for s, r in zip(sums, rest)]
+    here = combine(add_to, CHUNKS, *[s[0] for s in sums], rest)
     group_total = [h + r for h, r in zip(here, from_chip)]
 
     arrived = [[] for _ in chunks]
     passing = group_total
     for hop in range(groups - 1):
         if hop == min(1, groups - 2):
-            passing[-1], held = tie(passing[-1], where)
-            late, _ = local_slots(held, None, None, q_slots, k_parts, v_parts, width, every[len(local) :])
+            passing[-1], k_parts[0] = tie(passing[-1], k_parts[0])
+            late, _ = local_slots(None, None, q_slots, k_parts, v_parts, width, every[len(local) :])
         received = [send(f"hop{hop}_{j}", p, "grp", [(hop, hop + 1)]) for j, p in enumerate(passing)]
         if hop == min(1, groups - 2):
             received[0], late = tie(received[0], late)
@@ -356,17 +368,29 @@
         before = sum(arrived[1:], arrived[0])
         return before + (1.0 - chip) * here, before + chip * from_chip
 
-    turned = [combine(turn, 2, where, here[j], from_chip[j], *arrived[j]) for j in chunks]
+    turned = [combine(turn, 2, here[j], from_chip[j], *arrived[j]) for j in chunks]
     from_chip_back = [send(f"chipback{j}", t[0], "seq", other_chip) for j, t in enumerate(turned)]
     near_back = [send(f"near{j}", t[1], "seq", other_core) for j, t in enumerate(turned)]
-    out = None
+    def near_slots(j):
+        return {
+            (j, 0): (q_slots[j, 0], local[j, 0], turned[j][1], rest),
+            (j, 1): (q_slots[j, 1], local[j, 1], from_chip_back[j], lead),
+        }
+
+    def far_slots(j):
+        far_back = send(f"far{j}", from_chip_back[j], "seq", other_core)
+        return {
+            (j, 2): (q_slots[j, 2], local[j, 2], near_back[j], rest),
+            (j, 3): (q_slots[j, 3], local[j, 3], far_back, rest),
+        }
+
+    out, slots = None, {}
     for j in chunks:
-        far_back = send(f"far{j}", from_chip_back[j], "seq", other_core)
-        states = (turned[j][1], from_chip_back[j], lead[j], rest[j], near_back[j], far_back)
-        queries = [q_slots[j, n] for n in range(4)]
-        mixed = [local[j, n] for n in range(4)]
-        out = finish(where, gain, queries, mixed, states, out, j * 4 * width, width)
-    return out
+        out = finish(gain, {**slots, **near_slots(j)}, out, width)
+        slots = far_slots(j)
+        if j + 1 < CHUNKS:
+            from_chip_back[j + 1], out = tie(from_chip_back[j + 1], out)
+    return finish(gain, slots, out, width)
 
 
 def general_states(k, v, heads_here, nblocks, groups):

time: 50.3 us -> 47.4 us (0.942)
  Pallas kernels: 18.2 us -> 15.3 us
  starting transfers between devices: 18.1 us -> 16.6 us
  waiting for transfers between devices: 13.1 us -> 14.5 us
    pallas_call x7 -> x10, Pallas kernels: 18.2 us -> 15.3 us  [the longest x2 6.3 us: local_slots(): pl.pallas_call(kernel, in_specs=specs(*[pltpu.HBM] * first, *[pltpu.VMEM]...]
    ppermute x18 -> x16, starting transfers between devices: 18.1 us -> 16.6 us  [send(): return lax.ppermute(array, axis, pairs)]
    ppermute x18 -> x16, waiting for transfers between devices: 13.1 us -> 14.5 us  [send(): return lax.ppermute(array, axis, pairs)]
  transfers between devices with their start and end apart: 18 -> 16, of which waited for: 5 -> 5; matrix products, arithmetic and copies ran while one was open for 0% -> 0% of each run, Pallas kernels for 23% -> 21%
where the time goes in v4:
time: 47.4 us; the launch traced here: 46.8 us
  starting transfers between devices  16.6 us (35%)
  Pallas kernels  15.3 us (32%)
  waiting for transfers between devices  14.5 us (31%)
    ppermute x16, starting transfers between devices, send(): return lax.ppermute(array, axis, pairs)  16.6 us
    ppermute x16, waiting for transfers between devices, send(): return lax.ppermute(array, axis, pairs)  14.5 us
    pallas_call x2, Pallas kernels, local_slots(): pl.pallas_call(kernel, in_specs=specs(*[pltpu.HBM] * first, *[pltpu.VMEM]...  6.3 us
    pallas_call x3, Pallas kernels, finish(): pl.pallas_call(functools.partial(finish_kernel, places, width), in_specs=...  4.95 us
    pallas_call x1, Pallas kernels, kvsum(): pl.pallas_call(functools.partial(kvsum_kernel, width), in_specs=specs(*[p...  3.84 us
  transfers between devices with their start and end apart: 16, of which 5 were waited for; matrix products, arithmetic and copies ran while one was open for 0% of the time, Pallas kernels for 21%

profile of v4, /device:TPU:25, one launch (start us, length us, event | category | flops | bytes accessed | tf_op | source)
XLA Modules:
  0.0 46.8 jit_solution(11461962540724136153)
XLA Ops:
  0.0 3.8 %kvsum.1 = (f32[384,128]{1,0:T(8,128)S(1)}, f32[384,128]{1,0:T(8,128)S(1)}, bf16[4,512,384]{2,1,0:T(8,128)(2,1)S(1)}, bf16[4,512,384]{2,1,0:T(8,128)(2,1)S(1)}, ...) custom-call(bf16[512,3072]{1,0:T(8,128)(2,1)} %bitcast.10, ...), custom_call_target="tpu_custom_call" | custom-call | tf_op jit(solution)/shard_map/kvsum/pallas_call | solution.py:117
  3.8 0.7 %collective-permute-start = (f32[2,384,128]{2,1,0:T(8,128)S(1)}, f32[2,384,128]{2,1,0:T(8,128)S(1)}, u32[]{:S(2)}, u32[]{:S(2)}) collective-permute-start(f32[2,384,128]{2,1,0:T(8,128)S(1)} %get-tuple-element.60), channel_id=1, source_target_pairs={{0,8},{8,0},{16,24},{24,16},{1,9},{9,1},{17,25},{25,17},{2,10},{10... | collective-permute-start | bytes 1179656 | tf_op jit(solution)/shard_map/lead/ppermute | solution.py:309
  4.6 1.3 %collective-permute-done.refs_2_.refs_7_.refs_15_ = f32[2,384,128]{2,1,0:T(8,128)S(1)} collective-permute-done((f32[2,384,128]{2,1,0:T(8,128)S(1)}, f32[2,384,128]{2,1,0:T(8,128)S(1)}, u32[]{:S(2)}, u32[]{:S(2)}) %collective-permute-start) | collective-permute-done | bytes 393248 | tf_op jit(solution)/shard_map/lead/ppermute | solution.py:309
  6.4 1.2 %collective-permute-start.2 = (f32[384,128]{1,0:T(8,128)S(1)}, f32[384,128]{1,0:T(8,128)S(1)}, u32[]{:S(2)}, u32[]{:S(2)}) collective-permute-start(f32[384,128]{1,0:T(8,128)S(1)} %get-tuple-element.74), channel_id=1, source_target_pairs={{0,16},{16,0},{8,24},{24,8},{1,17},{17,1},{9,25},{25,9},{2,18},{18... | collective-permute-start | bytes 589832 | tf_op jit(solution)/shard_map/chip0/ppermute | solution.py:309
  7.6 2.4 %local_attention.2 = (f32[512,384]{1,0:T(8,128)S(1)}, f32[512,384]{1,0:T(8,128)S(1)}, bf16[512,384]{1,0:T(8,128)(2,1)S(1)}, bf16[512,384]{1,0:T(8,128)(2,1)S(1)}...) custom-call(bf16[512,3072]{1,0:T(8,128)(2,1)} %bitcast.9, ...), custom_call_target="tpu_custom_call" | custom-call | tf_op jit(solution)/shard_map/local_attention/pallas_call | solution.py:224
  10.5 2.3 %collective-permute-done.2.refs_1_ = f32[384,128]{1,0:T(8,128)S(1)} collective-permute-done((f32[384,128]{1,0:T(8,128)S(1)}, f32[384,128]{1,0:T(8,128)S(1)}, u32[]{:S(2)}, u32[]{:S(2)}) %collective-permute-start.2) | collective-permute-done | bytes 196640 | tf_op jit(solution)/shard_map/chip0/ppermute | solution.py:309
  12.8 0.7 %collective-permute-start.3 = (f32[384,128]{1,0:T(8,128)S(1)}, f32[384,128]{1,0:T(8,128)S(1)}, u32[]{:S(2)}, u32[]{:S(2)}) collective-permute-start(f32[384,128]{1,0:T(8,128)S(1)} %add.18), channel_id=1, source_target_pairs={{0,2},{1,3},{8,10},{9,11},{16,18},{17,19},{24,26},{25,27}} | collective-permute-start | bytes 589832 | tf_op jit(solution)/shard_map/hop0_0/ppermute | solution.py:309
  13.5 3.6 %collective-permute-done.5.refs_1_ = f32[384,128]{1,0:T(8,128)S(1)} collective-permute-done((f32[384,128]{1,0:T(8,128)S(1)}, f32[384,128]{1,0:T(8,128)S(1)}, u32[]{:S(2)}, u32[]{:S(2)}) %collective-permute-start.5) | collective-permute-done | bytes 196640 | tf_op jit(solution)/shard_map/chip1/ppermute | solution.py:309
  17.2 0.7 %collective-permute-start.6 = (f32[384,128]{1,0:T(8,128)S(1)}, f32[384,128]{1,0:T(8,128)S(1)}, u32[]{:S(2)}, u32[]{:S(2)}) collective-permute-start(f32[384,128]{1,0:T(8,128)S(1)} %add.20), channel_id=1, source_target_pairs={{0,2},{1,3},{8,10},{9,11},{16,18},{17,19},{24,26},{25,27}} | collective-permute-start | bytes 589832 | tf_op jit(solution)/shard_map/hop0_1/ppermute | solution.py:309
  17.9 0.7 %collective-permute-start.4 = (f32[384,128]{1,0:T(8,128)S(1)}, f32[384,128]{1,0:T(8,128)S(1)}, u32[]{:S(2)}, u32[]{:S(2)}) collective-permute-start(f32[384,128]{1,0:T(8,128)S(1)} %add.19), channel_id=1, source_target_pairs={{2,4},{3,5},{10,12},{11,13},{18,20},{19,21},{26,28},{27,29}} | collective-permute-start | bytes 589832 | tf_op jit(solution)/shard_map/hop1_0/ppermute | solution.py:309
  18.6 0.7 %collective-permute-start.7 = (f32[384,128]{1,0:T(8,128)S(1)}, f32[384,128]{1,0:T(8,128)S(1)}, u32[]{:S(2)}, u32[]{:S(2)}) collective-permute-start(f32[384,128]{1,0:T(8,128)S(1)} %add.21), channel_id=1, source_target_pairs={{2,4},{3,5},{10,12},{11,13},{18,20},{19,21},{26,28},{27,29}} | collective-permute-start | bytes 589832 | tf_op jit(solution)/shard_map/hop1_1/ppermute | solution.py:309
  19.3 3.9 %local_attention.3 = (f32[512,384]{1,0:T(8,128)S(1)}, f32[512,384]{1,0:T(8,128)S(1)}, f32[512,384]{1,0:T(8,128)S(1)}, f32[512,384]{1,0:T(8,128)S(1)}, f32[512,384]{1,0:T(8,128)S(1)}, /*index=5*/f32[512,384]{1,0:T(8,128)S(1)}) custom-call(bf16[512,384]{1,0:T(8,128)(2,1)S(1)} %get-tuple-element.75.refs_0_, ...), custom_call_target="tpu_custom_call" | custom-call | tf_op jit(solution)/shard_map/local_attention/pallas_call | solution.py:224
  23.2 1.3 %collective-permute-start.11 = (f32[384,128]{1,0:T(8,128)S(1)}, f32[384,128]{1,0:T(8,128)S(1)}, u32[]{:S(2)}, u32[]{:S(2)}) collective-permute-start(f32[384,128]{1,0:T(8,128)S(1)} %add.23), channel_id=1, source_target_pairs={{4,6},{5,7},{12,14},{13,15},{20,22},{21,23},{28,30},{29,31}} | collective-permute-start | bytes 589832 | tf_op jit(solution)/shard_map/hop2_0/ppermute | solution.py:309
  24.5 1.3 %collective-permute-start.8 = (f32[384,128]{1,0:T(8,128)S(1)}, f32[384,128]{1,0:T(8,128)S(1)}, u32[]{:S(2)}, u32[]{:S(2)}) collective-permute-start(f32[384,128]{1,0:T(8,128)S(1)} %add.22), channel_id=1, source_target_pairs={{4,6},{5,7},{12,14},{13,15},{20,22},{21,23},{28,30},{29,31}} | collective-permute-start | bytes 589832 | tf_op jit(solution)/shard_map/hop2_1/ppermute | solution.py:309
  25.8 3.8 %collective-permute-done.11.refs_4_ = f32[384,128]{1,0:T(8,128)S(1)} collective-permute-done((f32[384,128]{1,0:T(8,128)S(1)}, f32[384,128]{1,0:T(8,128)S(1)}, u32[]{:S(2)}, u32[]{:S(2)}) %collective-permute-start.11) | collective-permute-done | bytes 196640 | tf_op jit(solution)/shard_map/hop2_0/ppermute | solution.py:309
  29.7 1.1 %collective-permute-start.12 = (f32[384,128]{1,0:T(8,128)S(1)}, f32[384,128]{1,0:T(8,128)S(1)}, u32[]{:S(2)}, u32[]{:S(2)}) collective-permute-start(f32[384,128]{1,0:T(8,128)S(1)} %get-tuple-element.102), channel_id=1, source_target_pairs={{0,16},{16,0},{8,24},{24,8},{1,17},{17,1},{9,25},{25,9},{2,18},{18... | collective-permute-start | bytes 589832 | tf_op jit(solution)/shard_map/chipback0/ppermute | solution.py:309
  30.8 3.4 %collective-permute-done.8.refs_4_ = f32[384,128]{1,0:T(8,128)S(1)} collective-permute-done((f32[384,128]{1,0:T(8,128)S(1)}, f32[384,128]{1,0:T(8,128)S(1)}, u32[]{:S(2)}, u32[]{:S(2)}) %collective-permute-start.8) | collective-permute-done | bytes 196640 | tf_op jit(solution)/shard_map/hop2_1/ppermute | solution.py:309
  34.3 1.3 %collective-permute-start.10 = (f32[384,128]{1,0:T(8,128)S(1)}, f32[384,128]{1,0:T(8,128)S(1)}, u32[]{:S(2)}, u32[]{:S(2)}) collective-permute-start(f32[384,128]{1,0:T(8,128)S(1)} %get-tuple-element.96), channel_id=1, source_target_pairs={{0,16},{16,0},{8,24},{24,8},{1,17},{17,1},{9,25},{25,9},{2,18},{18... | collective-permute-start | bytes 589832 | tf_op jit(solution)/shard_map/chipback1/ppermute | solution.py:309
  35.6 3.1 %collective-permute-start.14 = (f32[384,128]{1,0:T(8,128)S(1)}, f32[384,128]{1,0:T(8,128)S(1)}, u32[]{:S(2)}, u32[]{:S(2)}) collective-permute-start(f32[384,128]{1,0:T(8,128)S(1)} %get-tuple-element.99.refs_2_), channel_id=1, source_target_pairs={{0,8},{8,0},{16,24},{24,16},{1,9},{9,1},{17,25},{25,17},{2,10},{10... | collective-permute-start | bytes 589832 | tf_op jit(solution)/shard_map/near0/ppermute | solution.py:309
  38.7 1.6 %collective-permute-start.15 = (f32[384,128]{1,0:T(8,128)S(1)}, f32[384,128]{1,0:T(8,128)S(1)}, u32[]{:S(2)}, u32[]{:S(2)}) collective-permute-start(f32[384,128]{1,0:T(8,128)S(1)} %collective-permute-done.12.refs_6_), channel_id=1, source_target_pairs={{0,8},{8,0},{16,24},{24,16},{1,9},{9,1},{17,25},{25,17},{2,10},{10... | collective-permute-start | bytes 589832 | tf_op jit(solution)/shard_map/far0/ppermute | solution.py:309
  40.3 1.5 %finish.3.refs_16_ = bf16[512,3072]{1,0:T(8,128)(2,1)} custom-call(f32[1,3072]{1,0:T(1,128)S(1)} %bitcast.5, bf16[512,384]{1,0:T(8,128)(2,1)S(1)} %get-tuple-element.57.refs_0_, f32[512,384]{1,0:T(8,128)S(1)} %get-tuple-element.97.refs_1_, f32[384,128]{1,0:T(8,128)S(1)} %get-tuple-element.99.refs_2_, ...), custom_call_target="tpu_custom_call" | custom-call | tf_op jit(solution)/shard_map/finish/pallas_call | solution.py:269
  41.8 1.4 %collective-permute-start.13 = (f32[384,128]{1,0:T(8,128)S(1)}, f32[384,128]{1,0:T(8,128)S(1)}, u32[]{:S(2)}, u32[]{:S(2)}) collective-permute-start(f32[384,128]{1,0:T(8,128)S(1)} %collective-permute-done.10.refs_14_), channel_id=1, source_target_pairs={{0,8},{8,0},{16,24},{24,16},{1,9},{9,1},{17,25},{25,17},{2,10},{10... | collective-permute-start | bytes 589832 | tf_op jit(solution)/shard_map/far1/ppermute | solution.py:309
  43.3 2.0 %finish.4.refs_8_ = bf16[512,3072]{1,0:T(8,128)(2,1)} custom-call(f32[1,3072]{1,0:T(1,128)S(1)} %bitcast.6, bf16[512,384]{1,0:T(8,128)(2,1)S(1)} %get-tuple-element.75.refs_0_, f32[512,384]{1,0:T(8,128)S(1)} %get-tuple-element.104.refs_1_, f32[384,128]{1,0:T(8,128)S(1)} %collective-permute-done.14.refs_2_, ...), custom_call_target="tpu_custom_call", output_to_operand_aliasing={{}: (17, {})} | custom-call | tf_op jit(solution)/shard_map/finish/pallas_call | solution.py:269
  45.3 1.5 %finish.5 = bf16[512,3072]{1,0:T(8,128)(2,1)} custom-call(f32[1,3072]{1,0:T(1,128)S(1)} %bitcast.7, bf16[512,384]{1,0:T(8,128)(2,1)S(1)} %get-tuple-element.69.refs_4_.refs_0_, f32[512,384]{1,0:T(8,128)S(1)} %get-tuple-element.92.refs_1_, f32[384,128]{1,0:T(8,128)S(1)} %collective-permute-done.9.refs_2_, ...), custom_call_target="tpu_custom_call", output_to_operand_aliasing={{}: (9, {})} | custom-call | tf_op jit(solution)/shard_map/finish/pallas_call | solution.py:269
  (26 shorter events, 1.2 us)
Async XLA Ops:
  3.8 2.1 %collective-permute-start = (f32[2,384,128]{2,1,0:T(8,128)S(1)}, f32[2,384,128]{2,1,0:T(8,128)S(1)}, u32[]{:S(2)}, u32[]{:S(2)}) collective-permute-start(f32[2,384,128]{2,1,0:T(8,128)S(1)} %get-tuple-element.60), channel_id=1, source_target_pairs={{0,8},{8,0},{16,24},{24,16},{1,9},{9,1},{17,25},{25,17},{2,10},{10... | collective-permute-start | bytes 1179656 | tf_op jit(solution)/shard_map/lead/ppermute | solution.py:309
  6.0 4.4 %collective-permute-start.1 = (f32[2,3,384,128]{3,2,1,0:T(8,128)S(1)}, f32[2,3,384,128]{3,2,1,0:T(8,128)S(1)}, u32[]{:S(2)}, u32[]{:S(2)}) collective-permute-start(f32[2,3,384,128]{3,2,1,0:T(8,128)S(1)} %get-tuple-element.72), channel_id=1, source_target_pairs={{0,8},{8,0},{16,24},{24,16},{1,9},{9,1},{17,25},{25,17},{2,10},{10... | collective-permute-start | bytes 3538952 | tf_op jit(solution)/shard_map/rest/ppermute | solution.py:309
  6.4 6.4 %collective-permute-start.2 = (f32[384,128]{1,0:T(8,128)S(1)}, f32[384,128]{1,0:T(8,128)S(1)}, u32[]{:S(2)}, u32[]{:S(2)}) collective-permute-start(f32[384,128]{1,0:T(8,128)S(1)} %get-tuple-element.74), channel_id=1, source_target_pairs={{0,16},{16,0},{8,24},{24,8},{1,17},{17,1},{9,25},{25,9},{2,18},{18... | collective-permute-start | bytes 589832 | tf_op jit(solution)/shard_map/chip0/ppermute | solution.py:309
  10.1 7.1 %collective-permute-start.5 = (f32[384,128]{1,0:T(8,128)S(1)}, f32[384,128]{1,0:T(8,128)S(1)}, u32[]{:S(2)}, u32[]{:S(2)}) collective-permute-start(f32[384,128]{1,0:T(8,128)S(1)} %get-tuple-element.84), channel_id=1, source_target_pairs={{0,16},{16,0},{8,24},{24,8},{1,17},{17,1},{9,25},{25,9},{2,18},{18... | collective-permute-start | bytes 589832 | tf_op jit(solution)/shard_map/chip1/ppermute | solution.py:309
  12.8 5.0 %collective-permute-start.3 = (f32[384,128]{1,0:T(8,128)S(1)}, f32[384,128]{1,0:T(8,128)S(1)}, u32[]{:S(2)}, u32[]{:S(2)}) collective-permute-start(f32[384,128]{1,0:T(8,128)S(1)} %add.18), channel_id=1, source_target_pairs={{0,2},{1,3},{8,10},{9,11},{16,18},{17,19},{24,26},{25,27}} | collective-permute-start | bytes 589832 | tf_op jit(solution)/shard_map/hop0_0/ppermute | solution.py:309
  17.2 1.4 %collective-permute-start.6 = (f32[384,128]{1,0:T(8,128)S(1)}, f32[384,128]{1,0:T(8,128)S(1)}, u32[]{:S(2)}, u32[]{:S(2)}) collective-permute-start(f32[384,128]{1,0:T(8,128)S(1)} %add.20), channel_id=1, source_target_pairs={{0,2},{1,3},{8,10},{9,11},{16,18},{17,19},{24,26},{25,27}} | collective-permute-start | bytes 589832 | tf_op jit(solution)/shard_map/hop0_1/ppermute | solution.py:309
  17.9 5.3 %collective-permute-start.4 = (f32[384,128]{1,0:T(8,128)S(1)}, f32[384,128]{1,0:T(8,128)S(1)}, u32[]{:S(2)}, u32[]{:S(2)}) collective-permute-start(f32[384,128]{1,0:T(8,128)S(1)} %add.19), channel_id=1, source_target_pairs={{2,4},{3,5},{10,12},{11,13},{18,20},{19,21},{26,28},{27,29}} | collective-permute-start | bytes 589832 | tf_op jit(solution)/shard_map/hop1_0/ppermute | solution.py:309
  18.6 5.9 %collective-permute-start.7 = (f32[384,128]{1,0:T(8,128)S(1)}, f32[384,128]{1,0:T(8,128)S(1)}, u32[]{:S(2)}, u32[]{:S(2)}) collective-permute-start(f32[384,128]{1,0:T(8,128)S(1)} %add.21), channel_id=1, source_target_pairs={{2,4},{3,5},{10,12},{11,13},{18,20},{19,21},{26,28},{27,29}} | collective-permute-start | bytes 589832 | tf_op jit(solution)/shard_map/hop1_1/ppermute | solution.py:309
  23.2 17.2 %copy-start = (f32[3072]{0:T(1024)S(1)}, f32[3072]{0:T(1024)}, u32[]{:S(2)}) copy-start(f32[3072]{0:T(1024)} %param.7) | copy-start | bytes 36868
  23.2 6.4 %collective-permute-start.11 = (f32[384,128]{1,0:T(8,128)S(1)}, f32[384,128]{1,0:T(8,128)S(1)}, u32[]{:S(2)}, u32[]{:S(2)}) collective-permute-start(f32[384,128]{1,0:T(8,128)S(1)} %add.23), channel_id=1, source_target_pairs={{4,6},{5,7},{12,14},{13,15},{20,22},{21,23},{28,30},{29,31}} | collective-permute-start | bytes 589832 | tf_op jit(solution)/shard_map/hop2_0/ppermute | solution.py:309
  24.5 9.7 %collective-permute-start.8 = (f32[384,128]{1,0:T(8,128)S(1)}, f32[384,128]{1,0:T(8,128)S(1)}, u32[]{:S(2)}, u32[]{:S(2)}) collective-permute-start(f32[384,128]{1,0:T(8,128)S(1)} %add.22), channel_id=1, source_target_pairs={{4,6},{5,7},{12,14},{13,15},{20,22},{21,23},{28,30},{29,31}} | collective-permute-start | bytes 589832 | tf_op jit(solution)/shard_map/hop2_1/ppermute | solution.py:309
  29.7 9.0 %collective-permute-start.12 = (f32[384,128]{1,0:T(8,128)S(1)}, f32[384,128]{1,0:T(8,128)S(1)}, u32[]{:S(2)}, u32[]{:S(2)}) collective-permute-start(f32[384,128]{1,0:T(8,128)S(1)} %get-tuple-element.102), channel_id=1, source_target_pairs={{0,16},{16,0},{8,24},{24,8},{1,17},{17,1},{9,25},{25,9},{2,18},{18... | collective-permute-start | bytes 589832 | tf_op jit(solution)/shard_map/chipback0/ppermute | solution.py:309
  34.3 7.5 %collective-permute-start.10 = (f32[384,128]{1,0:T(8,128)S(1)}, f32[384,128]{1,0:T(8,128)S(1)}, u32[]{:S(2)}, u32[]{:S(2)}) collective-permute-start(f32[384,128]{1,0:T(8,128)S(1)} %get-tuple-element.96), channel_id=1, source_target_pairs={{0,16},{16,0},{8,24},{24,8},{1,17},{17,1},{9,25},{25,9},{2,18},{18... | collective-permute-start | bytes 589832 | tf_op jit(solution)/shard_map/chipback1/ppermute | solution.py:309
  35.6 7.7 %collective-permute-start.14 = (f32[384,128]{1,0:T(8,128)S(1)}, f32[384,128]{1,0:T(8,128)S(1)}, u32[]{:S(2)}, u32[]{:S(2)}) collective-permute-start(f32[384,128]{1,0:T(8,128)S(1)} %get-tuple-element.99.refs_2_), channel_id=1, source_target_pairs={{0,8},{8,0},{16,24},{24,16},{1,9},{9,1},{17,25},{25,17},{2,10},{10... | collective-permute-start | bytes 589832 | tf_op jit(solution)/shard_map/near0/ppermute | solution.py:309
  38.7 6.5 %collective-permute-start.9 = (f32[384,128]{1,0:T(8,128)S(1)}, f32[384,128]{1,0:T(8,128)S(1)}, u32[]{:S(2)}, u32[]{:S(2)}) collective-permute-start(f32[384,128]{1,0:T(8,128)S(1)} %get-tuple-element.94.refs_10_), channel_id=1, source_target_pairs={{0,8},{8,0},{16,24},{24,16},{1,9},{9,1},{17,25},{25,17},{2,10},{10... | collective-permute-start | bytes 589832 | tf_op jit(solution)/shard_map/near1/ppermute | solution.py:309
  38.7 4.5 %collective-permute-start.15 = (f32[384,128]{1,0:T(8,128)S(1)}, f32[384,128]{1,0:T(8,128)S(1)}, u32[]{:S(2)}, u32[]{:S(2)}) collective-permute-start(f32[384,128]{1,0:T(8,128)S(1)} %collective-permute-done.12.refs_6_), channel_id=1, source_target_pairs={{0,8},{8,0},{16,24},{24,16},{1,9},{9,1},{17,25},{25,17},{2,10},{10... | collective-permute-start | bytes 589832 | tf_op jit(solution)/shard_map/far0/ppermute | solution.py:309
  41.8 3.4 %collective-permute-start.13 = (f32[384,128]{1,0:T(8,128)S(1)}, f32[384,128]{1,0:T(8,128)S(1)}, u32[]{:S(2)}, u32[]{:S(2)}) collective-permute-start(f32[384,128]{1,0:T(8,128)S(1)} %collective-permute-done.10.refs_14_), channel_id=1, source_target_pairs={{0,8},{8,0},{16,24},{24,16},{1,9},{9,1},{17,25},{25,17},{2,10},{10... | collective-permute-start | bytes 589832 | tf_op jit(solution)/shard_map/far1/ppermute | solution.py:309

commit v5 on v4

--- a/solution.py
+++ b/solution.py
@@ -11,7 +11,7 @@
 BLK = 512
 TILE = 256
 CHUNKS = 2
-EARLY = 2
+EARLY = 4
 NO_COST = pl.CostEstimate(flops=0, bytes_accessed=0, transcendentals=0)
 F32 = jnp.float32
 BF16 = jnp.bfloat16
@@ -335,17 +335,11 @@
     k_parts, v_parts = [s[2] for s in sums], [s[3] for s in sums]
     every = [(j, n) for j in chunks for n in range(4)]
     local, q_slots = [], None
-    for j in chunks[:-1]:
-        there[j], k_parts[0] = tie(there[j], k_parts[0])
-        places = every[len(local) : len(local) + EARLY]
-        if j == 0:
-            part, q_slots = local_slots(q, q_lead, None, k_parts, v_parts, width, places)
-            q_slots = dict(zip(every, [q_lead, *q_slots]))
-        else:
-            part, _ = local_slots(None, None, q_slots, k_parts, v_parts, width, places)
-        there[j + 1], part = tie(there[j + 1], part)
-        local += part
+    there[0], k_parts[0] = tie(there[0], k_parts[0])
+    local, q_slots = local_slots(q, q_lead, None, k_parts, v_parts, width, every[:EARLY])
+    q_slots = dict(zip(every, [q_lead, *q_slots]))
     from_chip = [send(f"chip{j}", t, "seq", other_chip) for j, t in enumerate(there)]
+    from_chip[0], local = tie(from_chip[0], list(local))
     here = combine(add_to, CHUNKS, *[s[0] for s in sums], rest)
     group_total = [h + r for h, r in zip(here, from_chip)]
 
@@ -371,23 +365,21 @@
     turned = [combine(turn, 2, here[j], from_chip[j], *arrived[j]) for j in chunks]
     from_chip_back = [send(f"chipback{j}", t[0], "seq", other_chip) for j, t in enumerate(turned)]
     near_back = [send(f"near{j}", t[1], "seq", other_core) for j, t in enumerate(turned)]
-    def near_slots(j):
+    def early_slots(j):
         return {
             (j, 0): (q_slots[j, 0], local[j, 0], turned[j][1], rest),
             (j, 1): (q_slots[j, 1], local[j, 1], from_chip_back[j], lead),
+            (j, 2): (q_slots[j, 2], local[j, 2], near_back[j], rest),
         }
 
-    def far_slots(j):
+    def last_slot(j):
         far_back = send(f"far{j}", from_chip_back[j], "seq", other_core)
-        return {
-            (j, 2): (q_slots[j, 2], local[j, 2], near_back[j], rest),
-            (j, 3): (q_slots[j, 3], local[j, 3], far_back, rest),
-        }
+        return {(j, 3): (q_slots[j, 3], local[j, 3], far_back, rest)}
 
     out, slots = None, {}
     for j in chunks:
-        out = finish(gain, {**slots, **near_slots(j)}, out, width)
-        slots = far_slots(j)
+        out = finish(gain, {**slots, **early_slots(j)}, out, width)
+        slots = last_slot(j)
         if j + 1 < CHUNKS:
             from_chip_back[j + 1], out = tie(from_chip_back[j + 1], out)
     return finish(gain, slots, out, width)

time: 47.4 us -> 46.7 us (0.985)
  waiting for transfers between devices: 14.5 us -> 9.93 us
  starting transfers between devices: 16.6 us -> 20.5 us
    ppermute x16, waiting for transfers between devices: 14.5 us -> 9.93 us  [send(): return lax.ppermute(array, axis, pairs)]
    ppermute x16, starting transfers between devices: 16.6 us -> 20.5 us  [send(): return lax.ppermute(array, axis, pairs)]
  transfers between devices with their start and end apart: 16 -> 16, of which waited for: 5 -> 4; matrix products, arithmetic and copies ran while one was open for 0% -> 0% of each run, Pallas kernels for 21% -> 23%
where the time goes in v5:
time: 46.7 us; the launch traced here: 46.4 us
  starting transfers between devices  20.5 us (44%)
  Pallas kernels  15.6 us (33%)
  waiting for transfers between devices  9.93 us (21%)
    ppermute x16, starting transfers between devices, send(): return lax.ppermute(array, axis, pairs)  20.5 us
    ppermute x16, waiting for transfers between devices, send(): return lax.ppermute(array, axis, pairs)  9.93 us
    pallas_call x2, Pallas kernels, local_slots(): pl.pallas_call(kernel, in_specs=specs(*[pltpu.HBM] * first, *[pltpu.VMEM]...  6.65 us
    pallas_call x3, Pallas kernels, finish(): pl.pallas_call(functools.partial(finish_kernel, places, width), in_specs=...  4.88 us
    pallas_call x1, Pallas kernels, kvsum(): pl.pallas_call(functools.partial(kvsum_kernel, width), in_specs=specs(*[p...  3.84 us
  transfers between devices with their start and end apart: 16, of which 4 were waited for; matrix products, arithmetic and copies ran while one was open for 0% of the time, Pallas kernels for 23%

profile of v5, /device:TPU:25, one launch (start us, length us, event | category | flops | bytes accessed | tf_op | source)
XLA Modules:
  0.0 46.4 jit_solution(3504238291528641586)
XLA Ops:
  0.0 3.8 %kvsum.1 = (f32[384,128]{1,0:T(8,128)S(1)}, f32[384,128]{1,0:T(8,128)S(1)}, bf16[4,512,384]{2,1,0:T(8,128)(2,1)S(1)}, bf16[4,512,384]{2,1,0:T(8,128)(2,1)S(1)}, ...) custom-call(bf16[512,3072]{1,0:T(8,128)(2,1)} %bitcast.10, ...), custom_call_target="tpu_custom_call" | custom-call | tf_op jit(solution)/shard_map/kvsum/pallas_call | solution.py:117
  3.8 0.7 %collective-permute-start = (f32[2,384,128]{2,1,0:T(8,128)S(1)}, f32[2,384,128]{2,1,0:T(8,128)S(1)}, u32[]{:S(2)}, u32[]{:S(2)}) collective-permute-start(f32[2,384,128]{2,1,0:T(8,128)S(1)} %get-tuple-element.60), channel_id=1, source_target_pairs={{0,8},{8,0},{16,24},{24,16},{1,9},{9,1},{17,25},{25,17},{2,10},{10... | collective-permute-start | bytes 1179656 | tf_op jit(solution)/shard_map/lead/ppermute | solution.py:309
  4.6 1.3 %collective-permute-done.refs_2_.refs_7_.refs_11_ = f32[2,384,128]{2,1,0:T(8,128)S(1)} collective-permute-done((f32[2,384,128]{2,1,0:T(8,128)S(1)}, f32[2,384,128]{2,1,0:T(8,128)S(1)}, u32[]{:S(2)}, u32[]{:S(2)}) %collective-permute-start) | collective-permute-done | bytes 393248 | tf_op jit(solution)/shard_map/lead/ppermute | solution.py:309
  6.4 1.2 %collective-permute-start.2 = (f32[384,128]{1,0:T(8,128)S(1)}, f32[384,128]{1,0:T(8,128)S(1)}, u32[]{:S(2)}, u32[]{:S(2)}) collective-permute-start(f32[384,128]{1,0:T(8,128)S(1)} %get-tuple-element.74), channel_id=1, source_target_pairs={{0,16},{16,0},{8,24},{24,8},{1,17},{17,1},{9,25},{25,9},{2,18},{18... | collective-permute-start | bytes 589832 | tf_op jit(solution)/shard_map/chip0/ppermute | solution.py:309
  7.9 4.0 %local_attention.2 = (f32[512,384]{1,0:T(8,128)S(1)}, f32[512,384]{1,0:T(8,128)S(1)}, f32[512,384]{1,0:T(8,128)S(1)}, f32[512,384]{1,0:T(8,128)S(1)}, bf16[512,3...) custom-call(bf16[512,3072]{1,0:T(8,128)(2,1)} %bitcast.9, ...), custom_call_target="tpu_custom_call" | custom-call | tf_op jit(solution)/shard_map/local_attention/pallas_call | solution.py:224
  11.9 0.9 %collective-permute-done.2.refs_1_ = f32[384,128]{1,0:T(8,128)S(1)} collective-permute-done((f32[384,128]{1,0:T(8,128)S(1)}, f32[384,128]{1,0:T(8,128)S(1)}, u32[]{:S(2)}, u32[]{:S(2)}) %collective-permute-start.2) | collective-permute-done | bytes 196640 | tf_op jit(solution)/shard_map/chip0/ppermute | solution.py:309
  12.9 0.7 %collective-permute-start.3 = (f32[384,128]{1,0:T(8,128)S(1)}, f32[384,128]{1,0:T(8,128)S(1)}, u32[]{:S(2)}, u32[]{:S(2)}) collective-permute-start(f32[384,128]{1,0:T(8,128)S(1)} %add.18), channel_id=1, source_target_pairs={{0,2},{1,3},{8,10},{9,11},{16,18},{17,19},{24,26},{25,27}} | collective-permute-start | bytes 589832 | tf_op jit(solution)/shard_map/hop0_0/ppermute | solution.py:309
  13.6 3.4 %collective-permute-done.5.refs_1_ = f32[384,128]{1,0:T(8,128)S(1)} collective-permute-done((f32[384,128]{1,0:T(8,128)S(1)}, f32[384,128]{1,0:T(8,128)S(1)}, u32[]{:S(2)}, u32[]{:S(2)}) %collective-permute-start.5) | collective-permute-done | bytes 196640 | tf_op jit(solution)/shard_map/chip1/ppermute | solution.py:309
  17.0 0.7 %collective-permute-start.6 = (f32[384,128]{1,0:T(8,128)S(1)}, f32[384,128]{1,0:T(8,128)S(1)}, u32[]{:S(2)}, u32[]{:S(2)}) collective-permute-start(f32[384,128]{1,0:T(8,128)S(1)} %add.20), channel_id=1, source_target_pairs={{0,2},{1,3},{8,10},{9,11},{16,18},{17,19},{24,26},{25,27}} | collective-permute-start | bytes 589832 | tf_op jit(solution)/shard_map/hop0_1/ppermute | solution.py:309
  17.8 0.7 %collective-permute-start.4 = (f32[384,128]{1,0:T(8,128)S(1)}, f32[384,128]{1,0:T(8,128)S(1)}, u32[]{:S(2)}, u32[]{:S(2)}) collective-permute-start(f32[384,128]{1,0:T(8,128)S(1)} %add.19), channel_id=1, source_target_pairs={{2,4},{3,5},{10,12},{11,13},{18,20},{19,21},{26,28},{27,29}} | collective-permute-start | bytes 589832 | tf_op jit(solution)/shard_map/hop1_0/ppermute | solution.py:309
  18.5 0.7 %collective-permute-start.7 = (f32[384,128]{1,0:T(8,128)S(1)}, f32[384,128]{1,0:T(8,128)S(1)}, u32[]{:S(2)}, u32[]{:S(2)}) collective-permute-start(f32[384,128]{1,0:T(8,128)S(1)} %add.21), channel_id=1, source_target_pairs={{2,4},{3,5},{10,12},{11,13},{18,20},{19,21},{26,28},{27,29}} | collective-permute-start | bytes 589832 | tf_op jit(solution)/shard_map/hop1_1/ppermute | solution.py:309
  19.2 2.6 %local_attention.3 = (f32[512,384]{1,0:T(8,128)S(1)}, f32[512,384]{1,0:T(8,128)S(1)}, f32[512,384]{1,0:T(8,128)S(1)}, f32[512,384]{1,0:T(8,128)S(1)}) custom-call(bf16[512,384]{1,0:T(8,128)(2,1)S(1)} %get-tuple-element.80.refs_0_.refs_4_, bf16[512,384]{1,0:T(8,128)(2,1)S(1)} %get-tuple-element.81.refs_1_.refs_8_, ...), custom_call_target="tpu_custom_call" | custom-call | tf_op jit(solution)/shard_map/local_attention/pallas_call | solution.py:224
  21.8 1.3 %collective-permute-start.10 = (f32[384,128]{1,0:T(8,128)S(1)}, f32[384,128]{1,0:T(8,128)S(1)}, u32[]{:S(2)}, u32[]{:S(2)}) collective-permute-start(f32[384,128]{1,0:T(8,128)S(1)} %add.23), channel_id=1, source_target_pairs={{4,6},{5,7},{12,14},{13,15},{20,22},{21,23},{28,30},{29,31}} | collective-permute-start | bytes 589832 | tf_op jit(solution)/shard_map/hop2_0/ppermute | solution.py:309
  23.2 1.3 %collective-permute-start.8 = (f32[384,128]{1,0:T(8,128)S(1)}, f32[384,128]{1,0:T(8,128)S(1)}, u32[]{:S(2)}, u32[]{:S(2)}) collective-permute-start(f32[384,128]{1,0:T(8,128)S(1)} %add.22), channel_id=1, source_target_pairs={{4,6},{5,7},{12,14},{13,15},{20,22},{21,23},{28,30},{29,31}} | collective-permute-start | bytes 589832 | tf_op jit(solution)/shard_map/hop2_1/ppermute | solution.py:309
  24.5 4.2 %collective-permute-done.10.refs_4_ = f32[384,128]{1,0:T(8,128)S(1)} collective-permute-done((f32[384,128]{1,0:T(8,128)S(1)}, f32[384,128]{1,0:T(8,128)S(1)}, u32[]{:S(2)}, u32[]{:S(2)}) %collective-permute-start.10) | collective-permute-done | bytes 196640 | tf_op jit(solution)/shard_map/hop2_0/ppermute | solution.py:309
  28.8 1.3 %collective-permute-start.11 = (f32[384,128]{1,0:T(8,128)S(1)}, f32[384,128]{1,0:T(8,128)S(1)}, u32[]{:S(2)}, u32[]{:S(2)}) collective-permute-start(f32[384,128]{1,0:T(8,128)S(1)} %get-tuple-element.98), channel_id=1, source_target_pairs={{0,16},{16,0},{8,24},{24,8},{1,17},{17,1},{9,25},{25,9},{2,18},{18... | collective-permute-start | bytes 589832 | tf_op jit(solution)/shard_map/chipback0/ppermute | solution.py:309
  30.1 4.8 %collective-permute-start.12 = (f32[384,128]{1,0:T(8,128)S(1)}, f32[384,128]{1,0:T(8,128)S(1)}, u32[]{:S(2)}, u32[]{:S(2)}) collective-permute-start(f32[384,128]{1,0:T(8,128)S(1)} %get-tuple-element.95.refs_2_), channel_id=1, source_target_pairs={{0,8},{8,0},{16,24},{24,16},{1,9},{9,1},{17,25},{25,17},{2,10},{10... | collective-permute-start | bytes 589832 | tf_op jit(solution)/shard_map/near0/ppermute | solution.py:309
  34.9 0.7 %collective-permute-start.9 = (f32[384,128]{1,0:T(8,128)S(1)}, f32[384,128]{1,0:T(8,128)S(1)}, u32[]{:S(2)}, u32[]{:S(2)}) collective-permute-start(f32[384,128]{1,0:T(8,128)S(1)} %get-tuple-element.92), channel_id=1, source_target_pairs={{0,16},{16,0},{8,24},{24,8},{1,17},{17,1},{9,25},{25,9},{2,18},{18... | collective-permute-start | bytes 589832 | tf_op jit(solution)/shard_map/chipback1/ppermute | solution.py:309
  35.7 3.2 %collective-permute-start.15 = (f32[384,128]{1,0:T(8,128)S(1)}, f32[384,128]{1,0:T(8,128)S(1)}, u32[]{:S(2)}, u32[]{:S(2)}) collective-permute-start(f32[384,128]{1,0:T(8,128)S(1)} %get-tuple-element.105.refs_6_), channel_id=1, source_target_pairs={{0,8},{8,0},{16,24},{24,16},{1,9},{9,1},{17,25},{25,17},{2,10},{10... | collective-permute-start | bytes 589832 | tf_op jit(solution)/shard_map/near1/ppermute | solution.py:309
  38.9 1.0 %collective-permute-start.14 = (f32[384,128]{1,0:T(8,128)S(1)}, f32[384,128]{1,0:T(8,128)S(1)}, u32[]{:S(2)}, u32[]{:S(2)}) collective-permute-start(f32[384,128]{1,0:T(8,128)S(1)} %collective-permute-done.11.refs_6_), channel_id=1, source_target_pairs={{0,8},{8,0},{16,24},{24,16},{1,9},{9,1},{17,25},{25,17},{2,10},{10... | collective-permute-start | bytes 589832 | tf_op jit(solution)/shard_map/far0/ppermute | solution.py:309
  39.9 1.7 %finish.3.refs_16_ = bf16[512,3072]{1,0:T(8,128)(2,1)} custom-call(f32[1,3072]{1,0:T(1,128)S(1)} %bitcast.5, bf16[512,384]{1,0:T(8,128)(2,1)S(1)} %get-tuple-element.57.refs_0_, f32[512,384]{1,0:T(8,128)S(1)} %get-tuple-element.93.refs_1_, f32[384,128]{1,0:T(8,128)S(1)} %get-tuple-element.95.refs_2_, ...), custom_call_target="tpu_custom_call" | custom-call | tf_op jit(solution)/shard_map/finish/pallas_call | solution.py:269
  41.7 1.6 %collective-permute-start.13 = (f32[384,128]{1,0:T(8,128)S(1)}, f32[384,128]{1,0:T(8,128)S(1)}, u32[]{:S(2)}, u32[]{:S(2)}) collective-permute-start(f32[384,128]{1,0:T(8,128)S(1)} %collective-permute-done.9.refs_10_), channel_id=1, source_target_pairs={{0,8},{8,0},{16,24},{24,16},{1,9},{9,1},{17,25},{25,17},{2,10},{10... | collective-permute-start | bytes 589832 | tf_op jit(solution)/shard_map/far1/ppermute | solution.py:309
  43.2 2.0 %finish.4.refs_4_ = bf16[512,3072]{1,0:T(8,128)(2,1)} custom-call(f32[1,3072]{1,0:T(1,128)S(1)} %bitcast.6, bf16[512,384]{1,0:T(8,128)(2,1)S(1)} %get-tuple-element.102.refs_0_, f32[512,384]{1,0:T(8,128)S(1)} %get-tuple-element.103.refs_1_, f32[384,128]{1,0:T(8,128)S(1)} %collective-permute-done.14.refs_2_, ...), custom_call_target="tpu_custom_call", output_to_operand_aliasing={{}: (17, {})} | custom-call | tf_op jit(solution)/shard_map/finish/pallas_call | solution.py:269
  45.2 1.2 %finish.5 = bf16[512,3072]{1,0:T(8,128)(2,1)} custom-call(f32[1,3072]{1,0:T(1,128)S(1)} %bitcast.7, bf16[512,384]{1,0:T(8,128)(2,1)S(1)} %get-tuple-element.69.refs_3_.refs_0_, f32[512,384]{1,0:T(8,128)S(1)} %get-tuple-element.90.refs_1_, f32[384,128]{1,0:T(8,128)S(1)} %collective-permute-done.13.refs_2_, ...), custom_call_target="tpu_custom_call", output_to_operand_aliasing={{}: (5, {})} | custom-call | tf_op jit(solution)/shard_map/finish/pallas_call | solution.py:269
  (26 shorter events, 1.1 us)
Async XLA Ops:
  3.8 2.1 %collective-permute-start = (f32[2,384,128]{2,1,0:T(8,128)S(1)}, f32[2,384,128]{2,1,0:T(8,128)S(1)}, u32[]{:S(2)}, u32[]{:S(2)}) collective-permute-start(f32[2,384,128]{2,1,0:T(8,128)S(1)} %get-tuple-element.60), channel_id=1, source_target_pairs={{0,8},{8,0},{16,24},{24,16},{1,9},{9,1},{17,25},{25,17},{2,10},{10... | collective-permute-start | bytes 1179656 | tf_op jit(solution)/shard_map/lead/ppermute | solution.py:309
  6.0 6.8 %collective-permute-start.1 = (f32[2,3,384,128]{3,2,1,0:T(8,128)S(1)}, f32[2,3,384,128]{3,2,1,0:T(8,128)S(1)}, u32[]{:S(2)}, u32[]{:S(2)}) collective-permute-start(f32[2,3,384,128]{3,2,1,0:T(8,128)S(1)} %get-tuple-element.72), channel_id=1, source_target_pairs={{0,8},{8,0},{16,24},{24,16},{1,9},{9,1},{17,25},{25,17},{2,10},{10... | collective-permute-start | bytes 3538952 | tf_op jit(solution)/shard_map/rest/ppermute | solution.py:309
  6.4 6.4 %collective-permute-start.2 = (f32[384,128]{1,0:T(8,128)S(1)}, f32[384,128]{1,0:T(8,128)S(1)}, u32[]{:S(2)}, u32[]{:S(2)}) collective-permute-start(f32[384,128]{1,0:T(8,128)S(1)} %get-tuple-element.74), channel_id=1, source_target_pairs={{0,16},{16,0},{8,24},{24,8},{1,17},{17,1},{9,25},{25,9},{2,18},{18... | collective-permute-start | bytes 589832 | tf_op jit(solution)/shard_map/chip0/ppermute | solution.py:309
  7.6 9.4 %collective-permute-start.5 = (f32[384,128]{1,0:T(8,128)S(1)}, f32[384,128]{1,0:T(8,128)S(1)}, u32[]{:S(2)}, u32[]{:S(2)}) collective-permute-start(f32[384,128]{1,0:T(8,128)S(1)} %get-tuple-element.84), channel_id=1, source_target_pairs={{0,16},{16,0},{8,24},{24,8},{1,17},{17,1},{9,25},{25,9},{2,18},{18... | collective-permute-start | bytes 589832 | tf_op jit(solution)/shard_map/chip1/ppermute | solution.py:309
  12.9 4.8 %collective-permute-start.3 = (f32[384,128]{1,0:T(8,128)S(1)}, f32[384,128]{1,0:T(8,128)S(1)}, u32[]{:S(2)}, u32[]{:S(2)}) collective-permute-start(f32[384,128]{1,0:T(8,128)S(1)} %add.18), channel_id=1, source_target_pairs={{0,2},{1,3},{8,10},{9,11},{16,18},{17,19},{24,26},{25,27}} | collective-permute-start | bytes 589832 | tf_op jit(solution)/shard_map/hop0_0/ppermute | solution.py:309
  17.0 1.4 %collective-permute-start.6 = (f32[384,128]{1,0:T(8,128)S(1)}, f32[384,128]{1,0:T(8,128)S(1)}, u32[]{:S(2)}, u32[]{:S(2)}) collective-permute-start(f32[384,128]{1,0:T(8,128)S(1)} %add.20), channel_id=1, source_target_pairs={{0,2},{1,3},{8,10},{9,11},{16,18},{17,19},{24,26},{25,27}} | collective-permute-start | bytes 589832 | tf_op jit(solution)/shard_map/hop0_1/ppermute | solution.py:309
  17.8 4.1 %collective-permute-start.4 = (f32[384,128]{1,0:T(8,128)S(1)}, f32[384,128]{1,0:T(8,128)S(1)}, u32[]{:S(2)}, u32[]{:S(2)}) collective-permute-start(f32[384,128]{1,0:T(8,128)S(1)} %add.19), channel_id=1, source_target_pairs={{2,4},{3,5},{10,12},{11,13},{18,20},{19,21},{26,28},{27,29}} | collective-permute-start | bytes 589832 | tf_op jit(solution)/shard_map/hop1_0/ppermute | solution.py:309
  18.5 4.7 %collective-permute-start.7 = (f32[384,128]{1,0:T(8,128)S(1)}, f32[384,128]{1,0:T(8,128)S(1)}, u32[]{:S(2)}, u32[]{:S(2)}) collective-permute-start(f32[384,128]{1,0:T(8,128)S(1)} %add.21), channel_id=1, source_target_pairs={{2,4},{3,5},{10,12},{11,13},{18,20},{19,21},{26,28},{27,29}} | collective-permute-start | bytes 589832 | tf_op jit(solution)/shard_map/hop1_1/ppermute | solution.py:309
  21.8 18.1 %copy-start = (f32[3072]{0:T(1024)S(1)}, f32[3072]{0:T(1024)}, u32[]{:S(2)}) copy-start(f32[3072]{0:T(1024)} %param.7) | copy-start | bytes 36868
  21.8 6.9 %collective-permute-start.10 = (f32[384,128]{1,0:T(8,128)S(1)}, f32[384,128]{1,0:T(8,128)S(1)}, u32[]{:S(2)}, u32[]{:S(2)}) collective-permute-start(f32[384,128]{1,0:T(8,128)S(1)} %add.23), channel_id=1, source_target_pairs={{4,6},{5,7},{12,14},{13,15},{20,22},{21,23},{28,30},{29,31}} | collective-permute-start | bytes 589832 | tf_op jit(solution)/shard_map/hop2_0/ppermute | solution.py:309
  23.2 11.7 %collective-permute-start.8 = (f32[384,128]{1,0:T(8,128)S(1)}, f32[384,128]{1,0:T(8,128)S(1)}, u32[]{:S(2)}, u32[]{:S(2)}) collective-permute-start(f32[384,128]{1,0:T(8,128)S(1)} %add.22), channel_id=1, source_target_pairs={{4,6},{5,7},{12,14},{13,15},{20,22},{21,23},{28,30},{29,31}} | collective-permute-start | bytes 589832 | tf_op jit(solution)/shard_map/hop2_1/ppermute | solution.py:309
  28.8 10.1 %collective-permute-start.11 = (f32[384,128]{1,0:T(8,128)S(1)}, f32[384,128]{1,0:T(8,128)S(1)}, u32[]{:S(2)}, u32[]{:S(2)}) collective-permute-start(f32[384,128]{1,0:T(8,128)S(1)} %get-tuple-element.98), channel_id=1, source_target_pairs={{0,16},{16,0},{8,24},{24,8},{1,17},{17,1},{9,25},{25,9},{2,18},{18... | collective-permute-start | bytes 589832 | tf_op jit(solution)/shard_map/chipback0/ppermute | solution.py:309
  30.1 9.8 %collective-permute-start.12 = (f32[384,128]{1,0:T(8,128)S(1)}, f32[384,128]{1,0:T(8,128)S(1)}, u32[]{:S(2)}, u32[]{:S(2)}) collective-permute-start(f32[384,128]{1,0:T(8,128)S(1)} %get-tuple-element.95.refs_2_), channel_id=1, source_target_pairs={{0,8},{8,0},{16,24},{24,16},{1,9},{9,1},{17,25},{25,17},{2,10},{10... | collective-permute-start | bytes 589832 | tf_op jit(solution)/shard_map/near0/ppermute | solution.py:309
  34.9 6.7 %collective-permute-start.9 = (f32[384,128]{1,0:T(8,128)S(1)}, f32[384,128]{1,0:T(8,128)S(1)}, u32[]{:S(2)}, u32[]{:S(2)}) collective-permute-start(f32[384,128]{1,0:T(8,128)S(1)} %get-tuple-element.92), channel_id=1, source_target_pairs={{0,16},{16,0},{8,24},{24,8},{1,17},{17,1},{9,25},{25,9},{2,18},{18... | collective-permute-start | bytes 589832 | tf_op jit(solution)/shard_map/chipback1/ppermute | solution.py:309
  35.7 7.6 %collective-permute-start.15 = (f32[384,128]{1,0:T(8,128)S(1)}, f32[384,128]{1,0:T(8,128)S(1)}, u32[]{:S(2)}, u32[]{:S(2)}) collective-permute-start(f32[384,128]{1,0:T(8,128)S(1)} %get-tuple-element.105.refs_6_), channel_id=1, source_target_pairs={{0,8},{8,0},{16,24},{24,16},{1,9},{9,1},{17,25},{25,17},{2,10},{10... | collective-permute-start | bytes 589832 | tf_op jit(solution)/shard_map/near1/ppermute | solution.py:309
  38.9 4.4 %collective-permute-start.14 = (f32[384,128]{1,0:T(8,128)S(1)}, f32[384,128]{1,0:T(8,128)S(1)}, u32[]{:S(2)}, u32[]{:S(2)}) collective-permute-start(f32[384,128]{1,0:T(8,128)S(1)} %collective-permute-done.11.refs_6_), channel_id=1, source_target_pairs={{0,8},{8,0},{16,24},{24,16},{1,9},{9,1},{17,25},{25,17},{2,10},{10... | collective-permute-start | bytes 589832 | tf_op jit(solution)/shard_map/far0/ppermute | solution.py:309
  41.7 3.6 %collective-permute-start.13 = (f32[384,128]{1,0:T(8,128)S(1)}, f32[384,128]{1,0:T(8,128)S(1)}, u32[]{:S(2)}, u32[]{:S(2)}) collective-permute-start(f32[384,128]{1,0:T(8,128)S(1)} %collective-permute-done.9.refs_10_), channel_id=1, source_target_pairs={{0,8},{8,0},{16,24},{24,16},{1,9},{9,1},{17,25},{25,17},{2,10},{10... | collective-permute-start | bytes 589832 | tf_op jit(solution)/shard_map/far1/ppermute | solution.py:309

commit v6 on v5

--- a/solution.py
+++ b/solution.py
@@ -11,7 +11,7 @@
 BLK = 512
 TILE = 256
 CHUNKS = 2
-EARLY = 4
+EARLY = 3
 NO_COST = pl.CostEstimate(flops=0, bytes_accessed=0, transcendentals=0)
 F32 = jnp.float32
 BF16 = jnp.bfloat16
@@ -68,8 +68,8 @@
 KVSUM_OUTS = 4
 
 
-def kvsum_kernel(width, k_hbm, v_hbm, q_hbm, *refs):
-    *refs, lead, rest, q_ref, sems = refs
+def kvsum_kernel(width, k_hbm, v_hbm, *refs):
+    *refs, lead, rest, sems = refs
     slots = Slots(width)
     outs = [refs[KVSUM_OUTS * j : KVSUM_OUTS * (j + 1)] for j in range(CHUNKS)]
     loads = []
@@ -85,7 +85,6 @@
                     slots.load(first, slot, v_hbm, v_ref.at[slot], sems.at[1, j, slot]),
                 )
             )
-    q_load = slots.load(0, 0, q_hbm, q_ref, sems.at[2, 0, 0])
     for slot, j, *copies in loads:
         for copy in copies:
             copy.wait()
@@ -104,27 +103,25 @@
                 rest[j, (slot + 1) % 3, c, :] = total
             if slot < 2:
                 (own, other)[slot][c, :] = total
-    q_load.wait()
-
-
-def kvsum(q, k, v, width):
+
+
+def kvsum(k, v, width):
     tokens = k.shape[0]
     one = pltpu.VMEM((width, DH), F32)
     part = pltpu.VMEM((4, tokens, width), BF16)
     outs = [one, one, part, part] * CHUNKS
     outs += [pltpu.VMEM((CHUNKS, width, DH), F32), pltpu.VMEM((CHUNKS, 3, width, DH), F32)]
-    outs.append(pltpu.VMEM((tokens, width), BF16))
     results = pl.pallas_call(
         functools.partial(kvsum_kernel, width),
-        in_specs=specs(*[pltpu.HBM] * 3),
+        in_specs=specs(pltpu.HBM, pltpu.HBM),
         out_specs=specs(*[pltpu.VMEM] * len(outs)),
         out_shape=outs,
-        scratch_shapes=[pltpu.SemaphoreType.DMA((3, CHUNKS, 4))],
+        scratch_shapes=[pltpu.SemaphoreType.DMA((2, CHUNKS, 4))],
         compiler_params=params(),
         cost_estimate=NO_COST,
         name="kvsum",
-    )(in_hbm(k), in_hbm(v), in_hbm(q))
-    return [results[KVSUM_OUTS * j : KVSUM_OUTS * (j + 1)] for j in range(CHUNKS)], results[-3:]
+    )(in_hbm(k), in_hbm(v))
+    return [results[KVSUM_OUTS * j : KVSUM_OUTS * (j + 1)] for j in range(CHUNKS)], results[-2:]
 
 
 def local_scores(q_ref, k_ref, c):
@@ -181,21 +178,18 @@
     )(q, k, v)
 
 
-def local_slots_kernel(width, places, q_hbm, *refs):
+def local_slots_kernel(width, places, load, *refs):
     count = len(places)
-    if q_hbm is None:
-        q_refs, loads = dict(zip(places, refs)), {}
-        refs = refs[count:]
-    else:
+    if load:
         every = [(j, n) for j in range(CHUNKS) for n in range(4)]
-        *refs, sems = refs
-        q_refs = dict(zip(every, [refs[0], *refs[-len(every) + 1 :]]))
-        refs = refs[1:]
+        q_hbm, *refs, sems = refs
+        q_refs, refs = dict(zip(every, refs[-len(every) :])), refs[: -len(every)]
         slots = Slots(width)
         loads = {
-            (j, n): slots.load(4 * width * j, n, q_hbm, q_refs[j, n], sems.at[j, n])
-            for j, n in every[1:]
+            (j, n): slots.load(4 * width * j, n, q_hbm, q_refs[j, n], sems.at[j, n]) for j, n in every
         }
+    else:
+        q_refs, loads, refs = dict(zip(places, refs)), {}, refs[count:]
     k_refs, v_refs, out_refs = refs[:CHUNKS], refs[CHUNKS : 2 * CHUNKS], refs[2 * CHUNKS :]
 
     def items():
@@ -211,26 +205,23 @@
         copy.wait()
 
 
-def local_slots(q, q_lead, q_slots, k_parts, v_parts, width, places):
+def local_slots(q, q_slots, k_parts, v_parts, width, places):
     tokens = k_parts[0].shape[1]
-    first = q_lead is not None
+    load = q_slots is None
     every = 4 * CHUNKS
-    kernel = functools.partial(local_slots_kernel, width, places)
-    if not first:
-        kernel = lambda *refs: local_slots_kernel(width, places, None, *refs)
-    queries = [q_lead] if first else [q_slots[p] for p in places]
+    queries = [] if load else [q_slots[p] for p in places]
     outs = [pltpu.VMEM((tokens, width), F32)] * len(places)
-    outs += [pltpu.VMEM((tokens, width), BF16)] * ((every - 1) * first)
+    outs += [pltpu.VMEM((tokens, width), BF16)] * (every * load)
     results = pl.pallas_call(
-        kernel,
-        in_specs=specs(*[pltpu.HBM] * first, *[pltpu.VMEM] * (len(queries) + 2 * CHUNKS)),
+        functools.partial(local_slots_kernel, width, places, load),
+        in_specs=specs(*[pltpu.HBM] * load, *[pltpu.VMEM] * (len(queries) + 2 * CHUNKS)),
         out_specs=specs(*[pltpu.VMEM] * len(outs)),
         out_shape=outs,
-        scratch_shapes=[pltpu.SemaphoreType.DMA((CHUNKS, 4))] * first,
+        scratch_shapes=[pltpu.SemaphoreType.DMA((CHUNKS, 4))] * load,
         compiler_params=params(),
         cost_estimate=NO_COST,
         name="local_attention",
-    )(*([in_hbm(q)] if first else []), *[in_vmem(a) for a in (*queries, *k_parts, *v_parts)])
+    )(*([in_hbm(q)] if load else []), *[in_vmem(a) for a in (*queries, *k_parts, *v_parts)])
     return results[: len(places)], results[len(places) :]
 
 
@@ -327,7 +318,7 @@
     other_core = [(0, 1), (1, 0), (2, 3), (3, 2)]
     other_chip = [(0, 2), (2, 0), (1, 3), (3, 1)]
 
-    sums, (lead, rest, q_lead) = kvsum(q, k, v, width)
+    sums, (lead, rest) = kvsum(k, v, width)
     lead = send("lead", lead, "seq", other_core)
     there = combine(add_to, CHUNKS, *[s[1] for s in sums], lead)
     there[0], rest = tie(there[0], rest)
@@ -336,8 +327,8 @@
     every = [(j, n) for j in chunks for n in range(4)]
     local, q_slots = [], None
     there[0], k_parts[0] = tie(there[0], k_parts[0])
-    local, q_slots = local_slots(q, q_lead, None, k_parts, v_parts, width, every[:EARLY])
-    q_slots = dict(zip(every, [q_lead, *q_slots]))
+    local, q_slots = local_slots(q, None, k_parts, v_parts, width, every[:EARLY])
+    q_slots = dict(zip(every, q_slots))
     from_chip = [send(f"chip{j}", t, "seq", other_chip) for j, t in enumerate(there)]
     from_chip[0], local = tie(from_chip[0], list(local))
     here = combine(add_to, CHUNKS, *[s[0] for s in sums], rest)
@@ -348,7 +339,7 @@
     for hop in range(groups - 1):
         if hop == min(1, groups - 2):
             passing[-1], k_parts[0] = tie(passing[-1], k_parts[0])
-            late, _ = local_slots(None, None, q_slots, k_parts, v_parts, width, every[len(local) :])
+            late, _ = local_slots(None, q_slots, k_parts, v_parts, width, every[len(local) :])
         received = [send(f"hop{hop}_{j}", p, "grp", [(hop, hop + 1)]) for j, p in enumerate(passing)]
         if hop == min(1, groups - 2):
             received[0], late = tie(received[0], late)

time: 46.7 us -> 46.6 us (level)
  no operation moved by 1% of the time
where the time goes in v6:
time: 46.6 us; the launch traced here: 46.4 us
  starting transfers between devices  20.4 us (44%)
  Pallas kernels  15.7 us (34%)
  waiting for transfers between devices  10 us (21%)
    ppermute x16, starting transfers between devices, send(): return lax.ppermute(array, axis, pairs)  20.4 us
    ppermute x16, waiting for transfers between devices, send(): return lax.ppermute(array, axis, pairs)  10 us
    pallas_call x2, Pallas kernels, local_slots(): pl.pallas_call(functools.partial(local_slots_kernel, width, places, load)...  6.74 us
    pallas_call x3, Pallas kernels, finish(): pl.pallas_call(functools.partial(finish_kernel, places, width), in_specs=...  4.92 us
    pallas_call x1, Pallas kernels, kvsum(): pl.pallas_call(functools.partial(kvsum_kernel, width), in_specs=specs(plt...  3.77 us
  transfers between devices with their start and end apart: 16, of which 4 were waited for; matrix products, arithmetic and copies ran while one was open for 0% of the time, Pallas kernels for 23%

profile of v6, /device:TPU:25, one launch (start us, length us, event | category | flops | bytes accessed | tf_op | source)
XLA Modules:
  0.0 46.4 jit_solution(9801044735324788962)
XLA Ops:
  0.0 3.8 %kvsum.1 = (f32[384,128]{1,0:T(8,128)S(1)}, f32[384,128]{1,0:T(8,128)S(1)}, bf16[4,512,384]{2,1,0:T(8,128)(2,1)S(1)}, bf16[4,512,384]{2,1,0:T(8,128)(2,1)S(1)}, ...) custom-call(bf16[512,3072]{1,0:T(8,128)(2,1)} %bitcast.8, ...), custom_call_target="tpu_custom_call" | custom-call | tf_op jit(solution)/shard_map/kvsum/pallas_call | solution.py:114
  3.8 0.7 %collective-permute-start = (f32[2,384,128]{2,1,0:T(8,128)S(1)}, f32[2,384,128]{2,1,0:T(8,128)S(1)}, u32[]{:S(2)}, u32[]{:S(2)}) collective-permute-start(f32[2,384,128]{2,1,0:T(8,128)S(1)} %get-tuple-element.59), channel_id=1, source_target_pairs={{0,8},{8,0},{16,24},{24,16},{1,9},{9,1},{17,25},{25,17},{2,10},{10... | collective-permute-start | bytes 1179656 | tf_op jit(solution)/shard_map/lead/ppermute | solution.py:300
  4.5 1.3 %collective-permute-done.refs_2_.refs_7_.refs_11_ = f32[2,384,128]{2,1,0:T(8,128)S(1)} collective-permute-done((f32[2,384,128]{2,1,0:T(8,128)S(1)}, f32[2,384,128]{2,1,0:T(8,128)S(1)}, u32[]{:S(2)}, u32[]{:S(2)}) %collective-permute-start) | collective-permute-done | bytes 393248 | tf_op jit(solution)/shard_map/lead/ppermute | solution.py:300
  6.3 1.2 %collective-permute-start.2 = (f32[384,128]{1,0:T(8,128)S(1)}, f32[384,128]{1,0:T(8,128)S(1)}, u32[]{:S(2)}, u32[]{:S(2)}) collective-permute-start(f32[384,128]{1,0:T(8,128)S(1)} %get-tuple-element.73), channel_id=1, source_target_pairs={{0,16},{16,0},{8,24},{24,8},{1,17},{17,1},{9,25},{25,9},{2,18},{18... | collective-permute-start | bytes 589832 | tf_op jit(solution)/shard_map/chip0/ppermute | solution.py:300
  7.8 3.5 %local_attention.2 = (f32[512,384]{1,0:T(8,128)S(1)}, f32[512,384]{1,0:T(8,128)S(1)}, f32[512,384]{1,0:T(8,128)S(1)}, bf16[512,384]{1,0:T(8,128)(2,1)S(1)}, bf16...) custom-call(bf16[512,3072]{1,0:T(8,128)(2,1)} %bitcast.10, ...), custom_call_target="tpu_custom_call" | custom-call | tf_op jit(solution)/shard_map/local_attention/pallas_call | solution.py:215
  11.3 1.4 %collective-permute-done.2.refs_1_ = f32[384,128]{1,0:T(8,128)S(1)} collective-permute-done((f32[384,128]{1,0:T(8,128)S(1)}, f32[384,128]{1,0:T(8,128)S(1)}, u32[]{:S(2)}, u32[]{:S(2)}) %collective-permute-start.2) | collective-permute-done | bytes 196640 | tf_op jit(solution)/shard_map/chip0/ppermute | solution.py:300
  12.8 0.7 %collective-permute-start.3 = (f32[384,128]{1,0:T(8,128)S(1)}, f32[384,128]{1,0:T(8,128)S(1)}, u32[]{:S(2)}, u32[]{:S(2)}) collective-permute-start(f32[384,128]{1,0:T(8,128)S(1)} %add.18), channel_id=1, source_target_pairs={{0,2},{1,3},{8,10},{9,11},{16,18},{17,19},{24,26},{25,27}} | collective-permute-start | bytes 589832 | tf_op jit(solution)/shard_map/hop0_0/ppermute | solution.py:300
  13.5 3.4 %collective-permute-done.5.refs_1_ = f32[384,128]{1,0:T(8,128)S(1)} collective-permute-done((f32[384,128]{1,0:T(8,128)S(1)}, f32[384,128]{1,0:T(8,128)S(1)}, u32[]{:S(2)}, u32[]{:S(2)}) %collective-permute-start.5) | collective-permute-done | bytes 196640 | tf_op jit(solution)/shard_map/chip1/ppermute | solution.py:300
  17.0 0.7 %collective-permute-start.6 = (f32[384,128]{1,0:T(8,128)S(1)}, f32[384,128]{1,0:T(8,128)S(1)}, u32[]{:S(2)}, u32[]{:S(2)}) collective-permute-start(f32[384,128]{1,0:T(8,128)S(1)} %add.20), channel_id=1, source_target_pairs={{0,2},{1,3},{8,10},{9,11},{16,18},{17,19},{24,26},{25,27}} | collective-permute-start | bytes 589832 | tf_op jit(solution)/shard_map/hop0_1/ppermute | solution.py:300
  17.7 0.7 %collective-permute-start.4 = (f32[384,128]{1,0:T(8,128)S(1)}, f32[384,128]{1,0:T(8,128)S(1)}, u32[]{:S(2)}, u32[]{:S(2)}) collective-permute-start(f32[384,128]{1,0:T(8,128)S(1)} %add.19), channel_id=1, source_target_pairs={{2,4},{3,5},{10,12},{11,13},{18,20},{19,21},{26,28},{27,29}} | collective-permute-start | bytes 589832 | tf_op jit(solution)/shard_map/hop1_0/ppermute | solution.py:300
  18.4 0.7 %collective-permute-start.7 = (f32[384,128]{1,0:T(8,128)S(1)}, f32[384,128]{1,0:T(8,128)S(1)}, u32[]{:S(2)}, u32[]{:S(2)}) collective-permute-start(f32[384,128]{1,0:T(8,128)S(1)} %add.21), channel_id=1, source_target_pairs={{2,4},{3,5},{10,12},{11,13},{18,20},{19,21},{26,28},{27,29}} | collective-permute-start | bytes 589832 | tf_op jit(solution)/shard_map/hop1_1/ppermute | solution.py:300
  19.1 3.3 %local_attention.3 = (f32[512,384]{1,0:T(8,128)S(1)}, f32[512,384]{1,0:T(8,128)S(1)}, f32[512,384]{1,0:T(8,128)S(1)}, f32[512,384]{1,0:T(8,128)S(1)}, f32[512,384]{1,0:T(8,128)S(1)}) custom-call(bf16[512,384]{1,0:T(8,128)(2,1)S(1)} %get-tuple-element.78.refs_0_, bf16[512,384]{1,0:T(8,128)(2,1)S(1)} %get-tuple-element.79.refs_1_.refs_4_, ...), custom_call_target="tpu_custom_call" | custom-call | tf_op jit(solution)/shard_map/local_attention/pallas_call | solution.py:215
  22.4 1.3 %collective-permute-start.10 = (f32[384,128]{1,0:T(8,128)S(1)}, f32[384,128]{1,0:T(8,128)S(1)}, u32[]{:S(2)}, u32[]{:S(2)}) collective-permute-start(f32[384,128]{1,0:T(8,128)S(1)} %add.23), channel_id=1, source_target_pairs={{4,6},{5,7},{12,14},{13,15},{20,22},{21,23},{28,30},{29,31}} | collective-permute-start | bytes 589832 | tf_op jit(solution)/shard_map/hop2_0/ppermute | solution.py:300
  23.7 1.3 %collective-permute-start.8 = (f32[384,128]{1,0:T(8,128)S(1)}, f32[384,128]{1,0:T(8,128)S(1)}, u32[]{:S(2)}, u32[]{:S(2)}) collective-permute-start(f32[384,128]{1,0:T(8,128)S(1)} %add.22), channel_id=1, source_target_pairs={{4,6},{5,7},{12,14},{13,15},{20,22},{21,23},{28,30},{29,31}} | collective-permute-start | bytes 589832 | tf_op jit(solution)/shard_map/hop2_1/ppermute | solution.py:300
  25.0 3.8 %collective-permute-done.10.refs_4_ = f32[384,128]{1,0:T(8,128)S(1)} collective-permute-done((f32[384,128]{1,0:T(8,128)S(1)}, f32[384,128]{1,0:T(8,128)S(1)}, u32[]{:S(2)}, u32[]{:S(2)}) %collective-permute-start.10) | collective-permute-done | bytes 196640 | tf_op jit(solution)/shard_map/hop2_0/ppermute | solution.py:300
  28.9 1.3 %collective-permute-start.11 = (f32[384,128]{1,0:T(8,128)S(1)}, f32[384,128]{1,0:T(8,128)S(1)}, u32[]{:S(2)}, u32[]{:S(2)}) collective-permute-start(f32[384,128]{1,0:T(8,128)S(1)} %get-tuple-element.99), channel_id=1, source_target_pairs={{0,16},{16,0},{8,24},{24,8},{1,17},{17,1},{9,25},{25,9},{2,18},{18... | collective-permute-start | bytes 589832 | tf_op jit(solution)/shard_map/chipback0/ppermute | solution.py:300
  30.1 4.6 %collective-permute-start.12 = (f32[384,128]{1,0:T(8,128)S(1)}, f32[384,128]{1,0:T(8,128)S(1)}, u32[]{:S(2)}, u32[]{:S(2)}) collective-permute-start(f32[384,128]{1,0:T(8,128)S(1)} %get-tuple-element.96.refs_2_), channel_id=1, source_target_pairs={{0,8},{8,0},{16,24},{24,16},{1,9},{9,1},{17,25},{25,17},{2,10},{10... | collective-permute-start | bytes 589832 | tf_op jit(solution)/shard_map/near0/ppermute | solution.py:300
  34.8 0.7 %collective-permute-start.9 = (f32[384,128]{1,0:T(8,128)S(1)}, f32[384,128]{1,0:T(8,128)S(1)}, u32[]{:S(2)}, u32[]{:S(2)}) collective-permute-start(f32[384,128]{1,0:T(8,128)S(1)} %get-tuple-element.92), channel_id=1, source_target_pairs={{0,16},{16,0},{8,24},{24,8},{1,17},{17,1},{9,25},{25,9},{2,18},{18... | collective-permute-start | bytes 589832 | tf_op jit(solution)/shard_map/chipback1/ppermute | solution.py:300
  35.6 3.2 %collective-permute-start.15 = (f32[384,128]{1,0:T(8,128)S(1)}, f32[384,128]{1,0:T(8,128)S(1)}, u32[]{:S(2)}, u32[]{:S(2)}) collective-permute-start(f32[384,128]{1,0:T(8,128)S(1)} %get-tuple-element.105.refs_6_), channel_id=1, source_target_pairs={{0,8},{8,0},{16,24},{24,16},{1,9},{9,1},{17,25},{25,17},{2,10},{10... | collective-permute-start | bytes 589832 | tf_op jit(solution)/shard_map/near1/ppermute | solution.py:300
  38.8 1.1 %collective-permute-start.14 = (f32[384,128]{1,0:T(8,128)S(1)}, f32[384,128]{1,0:T(8,128)S(1)}, u32[]{:S(2)}, u32[]{:S(2)}) collective-permute-start(f32[384,128]{1,0:T(8,128)S(1)} %collective-permute-done.11.refs_6_), channel_id=1, source_target_pairs={{0,8},{8,0},{16,24},{24,16},{1,9},{9,1},{17,25},{25,17},{2,10},{10... | collective-permute-start | bytes 589832 | tf_op jit(solution)/shard_map/far0/ppermute | solution.py:300
  39.9 1.7 %finish.3.refs_16_ = bf16[512,3072]{1,0:T(8,128)(2,1)} custom-call(f32[1,3072]{1,0:T(1,128)S(1)} %bitcast.5, bf16[512,384]{1,0:T(8,128)(2,1)S(1)} %get-tuple-element.93.refs_0_, f32[512,384]{1,0:T(8,128)S(1)} %get-tuple-element.94.refs_1_, f32[384,128]{1,0:T(8,128)S(1)} %get-tuple-element.96.refs_2_, ...), custom_call_target="tpu_custom_call" | custom-call | tf_op jit(solution)/shard_map/finish/pallas_call | solution.py:260
  41.6 1.6 %collective-permute-start.13 = (f32[384,128]{1,0:T(8,128)S(1)}, f32[384,128]{1,0:T(8,128)S(1)}, u32[]{:S(2)}, u32[]{:S(2)}) collective-permute-start(f32[384,128]{1,0:T(8,128)S(1)} %collective-permute-done.9.refs_10_), channel_id=1, source_target_pairs={{0,8},{8,0},{16,24},{24,16},{1,9},{9,1},{17,25},{25,17},{2,10},{10... | collective-permute-start | bytes 589832 | tf_op jit(solution)/shard_map/far1/ppermute | solution.py:300
  43.2 2.0 %finish.4.refs_4_ = bf16[512,3072]{1,0:T(8,128)(2,1)} custom-call(f32[1,3072]{1,0:T(1,128)S(1)} %bitcast.6, bf16[512,384]{1,0:T(8,128)(2,1)S(1)} %get-tuple-element.78.refs_0_, f32[512,384]{1,0:T(8,128)S(1)} %get-tuple-element.103.refs_1_, f32[384,128]{1,0:T(8,128)S(1)} %collective-permute-done.14.refs_2_, ...), custom_call_target="tpu_custom_call", output_to_operand_aliasing={{}: (17, {})} | custom-call | tf_op jit(solution)/shard_map/finish/pallas_call | solution.py:260
  45.2 1.2 %finish.5 = bf16[512,3072]{1,0:T(8,128)(2,1)} custom-call(f32[1,3072]{1,0:T(1,128)S(1)} %bitcast.7, bf16[512,384]{1,0:T(8,128)(2,1)S(1)} %get-tuple-element.68.refs_4_.refs_0_, f32[512,384]{1,0:T(8,128)S(1)} %get-tuple-element.90.refs_1_, f32[384,128]{1,0:T(8,128)S(1)} %collective-permute-done.13.refs_2_, ...), custom_call_target="tpu_custom_call", output_to_operand_aliasing={{}: (5, {})} | custom-call | tf_op jit(solution)/shard_map/finish/pallas_call | solution.py:260
  (26 shorter events, 1.1 us)
Async XLA Ops:
  3.8 2.1 %collective-permute-start = (f32[2,384,128]{2,1,0:T(8,128)S(1)}, f32[2,384,128]{2,1,0:T(8,128)S(1)}, u32[]{:S(2)}, u32[]{:S(2)}) collective-permute-start(f32[2,384,128]{2,1,0:T(8,128)S(1)} %get-tuple-element.59), channel_id=1, source_target_pairs={{0,8},{8,0},{16,24},{24,16},{1,9},{9,1},{17,25},{25,17},{2,10},{10... | collective-permute-start | bytes 1179656 | tf_op jit(solution)/shard_map/lead/ppermute | solution.py:300
  5.9 6.8 %collective-permute-start.1 = (f32[2,3,384,128]{3,2,1,0:T(8,128)S(1)}, f32[2,3,384,128]{3,2,1,0:T(8,128)S(1)}, u32[]{:S(2)}, u32[]{:S(2)}) collective-permute-start(f32[2,3,384,128]{3,2,1,0:T(8,128)S(1)} %get-tuple-element.71), channel_id=1, source_target_pairs={{0,8},{8,0},{16,24},{24,16},{1,9},{9,1},{17,25},{25,17},{2,10},{10... | collective-permute-start | bytes 3538952 | tf_op jit(solution)/shard_map/rest/ppermute | solution.py:300
  6.3 6.4 %collective-permute-start.2 = (f32[384,128]{1,0:T(8,128)S(1)}, f32[384,128]{1,0:T(8,128)S(1)}, u32[]{:S(2)}, u32[]{:S(2)}) collective-permute-start(f32[384,128]{1,0:T(8,128)S(1)} %get-tuple-element.73), channel_id=1, source_target_pairs={{0,16},{16,0},{8,24},{24,8},{1,17},{17,1},{9,25},{25,9},{2,18},{18... | collective-permute-start | bytes 589832 | tf_op jit(solution)/shard_map/chip0/ppermute | solution.py:300
  7.6 9.4 %collective-permute-start.5 = (f32[384,128]{1,0:T(8,128)S(1)}, f32[384,128]{1,0:T(8,128)S(1)}, u32[]{:S(2)}, u32[]{:S(2)}) collective-permute-start(f32[384,128]{1,0:T(8,128)S(1)} %get-tuple-element.83), channel_id=1, source_target_pairs={{0,16},{16,0},{8,24},{24,8},{1,17},{17,1},{9,25},{25,9},{2,18},{18... | collective-permute-start | bytes 589832 | tf_op jit(solution)/shard_map/chip1/ppermute | solution.py:300
  12.8 4.8 %collective-permute-start.3 = (f32[384,128]{1,0:T(8,128)S(1)}, f32[384,128]{1,0:T(8,128)S(1)}, u32[]{:S(2)}, u32[]{:S(2)}) collective-permute-start(f32[384,128]{1,0:T(8,128)S(1)} %add.18), channel_id=1, source_target_pairs={{0,2},{1,3},{8,10},{9,11},{16,18},{17,19},{24,26},{25,27}} | collective-permute-start | bytes 589832 | tf_op jit(solution)/shard_map/hop0_0/ppermute | solution.py:300
  17.0 1.4 %collective-permute-start.6 = (f32[384,128]{1,0:T(8,128)S(1)}, f32[384,128]{1,0:T(8,128)S(1)}, u32[]{:S(2)}, u32[]{:S(2)}) collective-permute-start(f32[384,128]{1,0:T(8,128)S(1)} %add.20), channel_id=1, source_target_pairs={{0,2},{1,3},{8,10},{9,11},{16,18},{17,19},{24,26},{25,27}} | collective-permute-start | bytes 589832 | tf_op jit(solution)/shard_map/hop0_1/ppermute | solution.py:300
  17.7 4.7 %collective-permute-start.4 = (f32[384,128]{1,0:T(8,128)S(1)}, f32[384,128]{1,0:T(8,128)S(1)}, u32[]{:S(2)}, u32[]{:S(2)}) collective-permute-start(f32[384,128]{1,0:T(8,128)S(1)} %add.19), channel_id=1, source_target_pairs={{2,4},{3,5},{10,12},{11,13},{18,20},{19,21},{26,28},{27,29}} | collective-permute-start | bytes 589832 | tf_op jit(solution)/shard_map/hop1_0/ppermute | solution.py:300
  18.4 5.3 %collective-permute-start.7 = (f32[384,128]{1,0:T(8,128)S(1)}, f32[384,128]{1,0:T(8,128)S(1)}, u32[]{:S(2)}, u32[]{:S(2)}) collective-permute-start(f32[384,128]{1,0:T(8,128)S(1)} %add.21), channel_id=1, source_target_pairs={{2,4},{3,5},{10,12},{11,13},{18,20},{19,21},{26,28},{27,29}} | collective-permute-start | bytes 589832 | tf_op jit(solution)/shard_map/hop1_1/ppermute | solution.py:300
  22.3 17.5 %copy-start = (f32[3072]{0:T(1024)S(1)}, f32[3072]{0:T(1024)}, u32[]{:S(2)}) copy-start(f32[3072]{0:T(1024)} %param.7) | copy-start | bytes 36868
  22.4 6.4 %collective-permute-start.10 = (f32[384,128]{1,0:T(8,128)S(1)}, f32[384,128]{1,0:T(8,128)S(1)}, u32[]{:S(2)}, u32[]{:S(2)}) collective-permute-start(f32[384,128]{1,0:T(8,128)S(1)} %add.23), channel_id=1, source_target_pairs={{4,6},{5,7},{12,14},{13,15},{20,22},{21,23},{28,30},{29,31}} | collective-permute-start | bytes 589832 | tf_op jit(solution)/shard_map/hop2_0/ppermute | solution.py:300
  23.7 11.0 %collective-permute-start.8 = (f32[384,128]{1,0:T(8,128)S(1)}, f32[384,128]{1,0:T(8,128)S(1)}, u32[]{:S(2)}, u32[]{:S(2)}) collective-permute-start(f32[384,128]{1,0:T(8,128)S(1)} %add.22), channel_id=1, source_target_pairs={{4,6},{5,7},{12,14},{13,15},{20,22},{21,23},{28,30},{29,31}} | collective-permute-start | bytes 589832 | tf_op jit(solution)/shard_map/hop2_1/ppermute | solution.py:300
  28.9 9.9 %collective-permute-start.11 = (f32[384,128]{1,0:T(8,128)S(1)}, f32[384,128]{1,0:T(8,128)S(1)}, u32[]{:S(2)}, u32[]{:S(2)}) collective-permute-start(f32[384,128]{1,0:T(8,128)S(1)} %get-tuple-element.99), channel_id=1, source_target_pairs={{0,16},{16,0},{8,24},{24,8},{1,17},{17,1},{9,25},{25,9},{2,18},{18... | collective-permute-start | bytes 589832 | tf_op jit(solution)/shard_map/chipback0/ppermute | solution.py:300
  30.1 9.7 %collective-permute-start.12 = (f32[384,128]{1,0:T(8,128)S(1)}, f32[384,128]{1,0:T(8,128)S(1)}, u32[]{:S(2)}, u32[]{:S(2)}) collective-permute-start(f32[384,128]{1,0:T(8,128)S(1)} %get-tuple-element.96.refs_2_), channel_id=1, source_target_pairs={{0,8},{8,0},{16,24},{24,16},{1,9},{9,1},{17,25},{25,17},{2,10},{10... | collective-permute-start | bytes 589832 | tf_op jit(solution)/shard_map/near0/ppermute | solution.py:300
  34.8 6.7 %collective-permute-start.9 = (f32[384,128]{1,0:T(8,128)S(1)}, f32[384,128]{1,0:T(8,128)S(1)}, u32[]{:S(2)}, u32[]{:S(2)}) collective-permute-start(f32[384,128]{1,0:T(8,128)S(1)} %get-tuple-element.92), channel_id=1, source_target_pairs={{0,16},{16,0},{8,24},{24,8},{1,17},{17,1},{9,25},{25,9},{2,18},{18... | collective-permute-start | bytes 589832 | tf_op jit(solution)/shard_map/chipback1/ppermute | solution.py:300
  35.6 7.6 %collective-permute-start.15 = (f32[384,128]{1,0:T(8,128)S(1)}, f32[384,128]{1,0:T(8,128)S(1)}, u32[]{:S(2)}, u32[]{:S(2)}) collective-permute-start(f32[384,128]{1,0:T(8,128)S(1)} %get-tuple-element.105.refs_6_), channel_id=1, source_target_pairs={{0,8},{8,0},{16,24},{24,16},{1,9},{9,1},{17,25},{25,17},{2,10},{10... | collective-permute-start | bytes 589832 | tf_op jit(solution)/shard_map/near1/ppermute | solution.py:300
  38.8 4.4 %collective-permute-start.14 = (f32[384,128]{1,0:T(8,128)S(1)}, f32[384,128]{1,0:T(8,128)S(1)}, u32[]{:S(2)}, u32[]{:S(2)}) collective-permute-start(f32[384,128]{1,0:T(8,128)S(1)} %collective-permute-done.11.refs_6_), channel_id=1, source_target_pairs={{0,8},{8,0},{16,24},{24,16},{1,9},{9,1},{17,25},{25,17},{2,10},{10... | collective-permute-start | bytes 589832 | tf_op jit(solution)/shard_map/far0/ppermute | solution.py:300
  41.6 3.6 %collective-permute-start.13 = (f32[384,128]{1,0:T(8,128)S(1)}, f32[384,128]{1,0:T(8,128)S(1)}, u32[]{:S(2)}, u32[]{:S(2)}) collective-permute-start(f32[384,128]{1,0:T(8,128)S(1)} %collective-permute-done.9.refs_10_), channel_id=1, source_target_pairs={{0,8},{8,0},{16,24},{24,16},{1,9},{9,1},{17,25},{25,17},{2,10},{10... | collective-permute-start | bytes 589832 | tf_op jit(solution)/shard_map/far1/ppermute | solution.py:300

commit v7 on v6

--- a/solution.py
+++ b/solution.py
@@ -338,7 +338,7 @@
     passing = group_total
     for hop in range(groups - 1):
         if hop == min(1, groups - 2):
-            passing[-1], k_parts[0] = tie(passing[-1], k_parts[0])
+            passing[0], k_parts[0] = tie(passing[0], k_parts[0])
             late, _ = local_slots(None, q_slots, k_parts, v_parts, width, every[len(local) :])
         received = [send(f"hop{hop}_{j}", p, "grp", [(hop, hop + 1)]) for j, p in enumerate(passing)]
         if hop == min(1, groups - 2):

time: 46.6 us -> 46.6 us (level)
  no operation moved by 1% of the time
where the time goes in v7:
time: 46.6 us; the launch traced here: 46.4 us
  starting transfers between devices  20.4 us (44%)
  Pallas kernels  15.7 us (34%)
  waiting for transfers between devices  10 us (21%)
    ppermute x16, starting transfers between devices, send(): return lax.ppermute(array, axis, pairs)  20.4 us
    ppermute x16, waiting for transfers between devices, send(): return lax.ppermute(array, axis, pairs)  10 us
    pallas_call x2, Pallas kernels, local_slots(): pl.pallas_call(functools.partial(local_slots_kernel, width, places, load)...  6.74 us
    pallas_call x3, Pallas kernels, finish(): pl.pallas_call(functools.partial(finish_kernel, places, width), in_specs=...  4.92 us
    pallas_call x1, Pallas kernels, kvsum(): pl.pallas_call(functools.partial(kvsum_kernel, width), in_specs=specs(plt...  3.77 us
  transfers between devices with their start and end apart: 16, of which 4 were waited for; matrix products, arithmetic and copies ran while one was open for 0% of the time, Pallas kernels for 23%

profile of v7, /device:TPU:25, one launch (start us, length us, event | category | flops | bytes accessed | tf_op | source)
XLA Modules:
  0.0 46.4 jit_solution(9801044735324788962)
XLA Ops:
  0.0 3.8 %kvsum.1 = (f32[384,128]{1,0:T(8,128)S(1)}, f32[384,128]{1,0:T(8,128)S(1)}, bf16[4,512,384]{2,1,0:T(8,128)(2,1)S(1)}, bf16[4,512,384]{2,1,0:T(8,128)(2,1)S(1)}, ...) custom-call(bf16[512,3072]{1,0:T(8,128)(2,1)} %bitcast.8, ...), custom_call_target="tpu_custom_call" | custom-call | tf_op jit(solution)/shard_map/kvsum/pallas_call | solution.py:114
  3.8 0.7 %collective-permute-start = (f32[2,384,128]{2,1,0:T(8,128)S(1)}, f32[2,384,128]{2,1,0:T(8,128)S(1)}, u32[]{:S(2)}, u32[]{:S(2)}) collective-permute-start(f32[2,384,128]{2,1,0:T(8,128)S(1)} %get-tuple-element.59), channel_id=1, source_target_pairs={{0,8},{8,0},{16,24},{24,16},{1,9},{9,1},{17,25},{25,17},{2,10},{10... | collective-permute-start | bytes 1179656 | tf_op jit(solution)/shard_map/lead/ppermute | solution.py:300
  4.5 1.3 %collective-permute-done.refs_2_.refs_7_.refs_11_ = f32[2,384,128]{2,1,0:T(8,128)S(1)} collective-permute-done((f32[2,384,128]{2,1,0:T(8,128)S(1)}, f32[2,384,128]{2,1,0:T(8,128)S(1)}, u32[]{:S(2)}, u32[]{:S(2)}) %collective-permute-start) | collective-permute-done | bytes 393248 | tf_op jit(solution)/shard_map/lead/ppermute | solution.py:300
  6.3 1.2 %collective-permute-start.2 = (f32[384,128]{1,0:T(8,128)S(1)}, f32[384,128]{1,0:T(8,128)S(1)}, u32[]{:S(2)}, u32[]{:S(2)}) collective-permute-start(f32[384,128]{1,0:T(8,128)S(1)} %get-tuple-element.73), channel_id=1, source_target_pairs={{0,16},{16,0},{8,24},{24,8},{1,17},{17,1},{9,25},{25,9},{2,18},{18... | collective-permute-start | bytes 589832 | tf_op jit(solution)/shard_map/chip0/ppermute | solution.py:300
  7.8 3.5 %local_attention.2 = (f32[512,384]{1,0:T(8,128)S(1)}, f32[512,384]{1,0:T(8,128)S(1)}, f32[512,384]{1,0:T(8,128)S(1)}, bf16[512,384]{1,0:T(8,128)(2,1)S(1)}, bf16...) custom-call(bf16[512,3072]{1,0:T(8,128)(2,1)} %bitcast.10, ...), custom_call_target="tpu_custom_call" | custom-call | tf_op jit(solution)/shard_map/local_attention/pallas_call | solution.py:215
  11.3 1.4 %collective-permute-done.2.refs_1_ = f32[384,128]{1,0:T(8,128)S(1)} collective-permute-done((f32[384,128]{1,0:T(8,128)S(1)}, f32[384,128]{1,0:T(8,128)S(1)}, u32[]{:S(2)}, u32[]{:S(2)}) %collective-permute-start.2) | collective-permute-done | bytes 196640 | tf_op jit(solution)/shard_map/chip0/ppermute | solution.py:300
  12.8 0.7 %collective-permute-start.3 = (f32[384,128]{1,0:T(8,128)S(1)}, f32[384,128]{1,0:T(8,128)S(1)}, u32[]{:S(2)}, u32[]{:S(2)}) collective-permute-start(f32[384,128]{1,0:T(8,128)S(1)} %add.18), channel_id=1, source_target_pairs={{0,2},{1,3},{8,10},{9,11},{16,18},{17,19},{24,26},{25,27}} | collective-permute-start | bytes 589832 | tf_op jit(solution)/shard_map/hop0_0/ppermute | solution.py:300
  13.5 3.4 %collective-permute-done.5.refs_1_ = f32[384,128]{1,0:T(8,128)S(1)} collective-permute-done((f32[384,128]{1,0:T(8,128)S(1)}, f32[384,128]{1,0:T(8,128)S(1)}, u32[]{:S(2)}, u32[]{:S(2)}) %collective-permute-start.5) | collective-permute-done | bytes 196640 | tf_op jit(solution)/shard_map/chip1/ppermute | solution.py:300
  17.0 0.7 %collective-permute-start.6 = (f32[384,128]{1,0:T(8,128)S(1)}, f32[384,128]{1,0:T(8,128)S(1)}, u32[]{:S(2)}, u32[]{:S(2)}) collective-permute-start(f32[384,128]{1,0:T(8,128)S(1)} %add.20), channel_id=1, source_target_pairs={{0,2},{1,3},{8,10},{9,11},{16,18},{17,19},{24,26},{25,27}} | collective-permute-start | bytes 589832 | tf_op jit(solution)/shard_map/hop0_1/ppermute | solution.py:300
  17.7 0.7 %collective-permute-start.4 = (f32[384,128]{1,0:T(8,128)S(1)}, f32[384,128]{1,0:T(8,128)S(1)}, u32[]{:S(2)}, u32[]{:S(2)}) collective-permute-start(f32[384,128]{1,0:T(8,128)S(1)} %add.19), channel_id=1, source_target_pairs={{2,4},{3,5},{10,12},{11,13},{18,20},{19,21},{26,28},{27,29}} | collective-permute-start | bytes 589832 | tf_op jit(solution)/shard_map/hop1_0/ppermute | solution.py:300
  18.4 0.7 %collective-permute-start.7 = (f32[384,128]{1,0:T(8,128)S(1)}, f32[384,128]{1,0:T(8,128)S(1)}, u32[]{:S(2)}, u32[]{:S(2)}) collective-permute-start(f32[384,128]{1,0:T(8,128)S(1)} %add.21), channel_id=1, source_target_pairs={{2,4},{3,5},{10,12},{11,13},{18,20},{19,21},{26,28},{27,29}} | collective-permute-start | bytes 589832 | tf_op jit(solution)/shard_map/hop1_1/ppermute | solution.py:300
  19.1 3.3 %local_attention.3 = (f32[512,384]{1,0:T(8,128)S(1)}, f32[512,384]{1,0:T(8,128)S(1)}, f32[512,384]{1,0:T(8,128)S(1)}, f32[512,384]{1,0:T(8,128)S(1)}, f32[512,384]{1,0:T(8,128)S(1)}) custom-call(bf16[512,384]{1,0:T(8,128)(2,1)S(1)} %get-tuple-element.79.refs_0_, bf16[512,384]{1,0:T(8,128)(2,1)S(1)} %get-tuple-element.80.refs_1_.refs_4_, ...), custom_call_target="tpu_custom_call" | custom-call | tf_op jit(solution)/shard_map/local_attention/pallas_call | solution.py:215
  22.4 1.3 %collective-permute-start.10 = (f32[384,128]{1,0:T(8,128)S(1)}, f32[384,128]{1,0:T(8,128)S(1)}, u32[]{:S(2)}, u32[]{:S(2)}) collective-permute-start(f32[384,128]{1,0:T(8,128)S(1)} %add.23), channel_id=1, source_target_pairs={{4,6},{5,7},{12,14},{13,15},{20,22},{21,23},{28,30},{29,31}} | collective-permute-start | bytes 589832 | tf_op jit(solution)/shard_map/hop2_0/ppermute | solution.py:300
  23.7 1.3 %collective-permute-start.8 = (f32[384,128]{1,0:T(8,128)S(1)}, f32[384,128]{1,0:T(8,128)S(1)}, u32[]{:S(2)}, u32[]{:S(2)}) collective-permute-start(f32[384,128]{1,0:T(8,128)S(1)} %add.22), channel_id=1, source_target_pairs={{4,6},{5,7},{12,14},{13,15},{20,22},{21,23},{28,30},{29,31}} | collective-permute-start | bytes 589832 | tf_op jit(solution)/shard_map/hop2_1/ppermute | solution.py:300
  25.0 3.8 %collective-permute-done.10.refs_4_ = f32[384,128]{1,0:T(8,128)S(1)} collective-permute-done((f32[384,128]{1,0:T(8,128)S(1)}, f32[384,128]{1,0:T(8,128)S(1)}, u32[]{:S(2)}, u32[]{:S(2)}) %collective-permute-start.10) | collective-permute-done | bytes 196640 | tf_op jit(solution)/shard_map/hop2_0/ppermute | solution.py:300
  28.9 1.3 %collective-permute-start.11 = (f32[384,128]{1,0:T(8,128)S(1)}, f32[384,128]{1,0:T(8,128)S(1)}, u32[]{:S(2)}, u32[]{:S(2)}) collective-permute-start(f32[384,128]{1,0:T(8,128)S(1)} %get-tuple-element.99), channel_id=1, source_target_pairs={{0,16},{16,0},{8,24},{24,8},{1,17},{17,1},{9,25},{25,9},{2,18},{18... | collective-permute-start | bytes 589832 | tf_op jit(solution)/shard_map/chipback0/ppermute | solution.py:300
  30.1 4.6 %collective-permute-start.12 = (f32[384,128]{1,0:T(8,128)S(1)}, f32[384,128]{1,0:T(8,128)S(1)}, u32[]{:S(2)}, u32[]{:S(2)}) collective-permute-start(f32[384,128]{1,0:T(8,128)S(1)} %get-tuple-element.96.refs_2_), channel_id=1, source_target_pairs={{0,8},{8,0},{16,24},{24,16},{1,9},{9,1},{17,25},{25,17},{2,10},{10... | collective-permute-start | bytes 589832 | tf_op jit(solution)/shard_map/near0/ppermute | solution.py:300
  34.8 0.7 %collective-permute-start.9 = (f32[384,128]{1,0:T(8,128)S(1)}, f32[384,128]{1,0:T(8,128)S(1)}, u32[]{:S(2)}, u32[]{:S(2)}) collective-permute-start(f32[384,128]{1,0:T(8,128)S(1)} %get-tuple-element.92), channel_id=1, source_target_pairs={{0,16},{16,0},{8,24},{24,8},{1,17},{17,1},{9,25},{25,9},{2,18},{18... | collective-permute-start | bytes 589832 | tf_op jit(solution)/shard_map/chipback1/ppermute | solution.py:300
  35.6 3.2 %collective-permute-start.15 = (f32[384,128]{1,0:T(8,128)S(1)}, f32[384,128]{1,0:T(8,128)S(1)}, u32[]{:S(2)}, u32[]{:S(2)}) collective-permute-start(f32[384,128]{1,0:T(8,128)S(1)} %get-tuple-element.105.refs_6_), channel_id=1, source_target_pairs={{0,8},{8,0},{16,24},{24,16},{1,9},{9,1},{17,25},{25,17},{2,10},{10... | collective-permute-start | bytes 589832 | tf_op jit(solution)/shard_map/near1/ppermute | solution.py:300
  38.8 1.1 %collective-permute-start.14 = (f32[384,128]{1,0:T(8,128)S(1)}, f32[384,128]{1,0:T(8,128)S(1)}, u32[]{:S(2)}, u32[]{:S(2)}) collective-permute-start(f32[384,128]{1,0:T(8,128)S(1)} %collective-permute-done.11.refs_6_), channel_id=1, source_target_pairs={{0,8},{8,0},{16,24},{24,16},{1,9},{9,1},{17,25},{25,17},{2,10},{10... | collective-permute-start | bytes 589832 | tf_op jit(solution)/shard_map/far0/ppermute | solution.py:300
  39.9 1.7 %finish.3.refs_16_ = bf16[512,3072]{1,0:T(8,128)(2,1)} custom-call(f32[1,3072]{1,0:T(1,128)S(1)} %bitcast.5, bf16[512,384]{1,0:T(8,128)(2,1)S(1)} %get-tuple-element.93.refs_0_, f32[512,384]{1,0:T(8,128)S(1)} %get-tuple-element.94.refs_1_, f32[384,128]{1,0:T(8,128)S(1)} %get-tuple-element.96.refs_2_, ...), custom_call_target="tpu_custom_call" | custom-call | tf_op jit(solution)/shard_map/finish/pallas_call | solution.py:260
  41.6 1.6 %collective-permute-start.13 = (f32[384,128]{1,0:T(8,128)S(1)}, f32[384,128]{1,0:T(8,128)S(1)}, u32[]{:S(2)}, u32[]{:S(2)}) collective-permute-start(f32[384,128]{1,0:T(8,128)S(1)} %collective-permute-done.9.refs_10_), channel_id=1, source_target_pairs={{0,8},{8,0},{16,24},{24,16},{1,9},{9,1},{17,25},{25,17},{2,10},{10... | collective-permute-start | bytes 589832 | tf_op jit(solution)/shard_map/far1/ppermute | solution.py:300
  43.2 2.0 %finish.4.refs_4_ = bf16[512,3072]{1,0:T(8,128)(2,1)} custom-call(f32[1,3072]{1,0:T(1,128)S(1)} %bitcast.6, bf16[512,384]{1,0:T(8,128)(2,1)S(1)} %get-tuple-element.79.refs_0_, f32[512,384]{1,0:T(8,128)S(1)} %get-tuple-element.103.refs_1_, f32[384,128]{1,0:T(8,128)S(1)} %collective-permute-done.14.refs_2_, ...), custom_call_target="tpu_custom_call", output_to_operand_aliasing={{}: (17, {})} | custom-call | tf_op jit(solution)/shard_map/finish/pallas_call | solution.py:260
  45.2 1.2 %finish.5 = bf16[512,3072]{1,0:T(8,128)(2,1)} custom-call(f32[1,3072]{1,0:T(1,128)S(1)} %bitcast.7, bf16[512,384]{1,0:T(8,128)(2,1)S(1)} %get-tuple-element.68.refs_4_.refs_0_, f32[512,384]{1,0:T(8,128)S(1)} %get-tuple-element.89.refs_1_, f32[384,128]{1,0:T(8,128)S(1)} %collective-permute-done.13.refs_2_, ...), custom_call_target="tpu_custom_call", output_to_operand_aliasing={{}: (5, {})} | custom-call | tf_op jit(solution)/shard_map/finish/pallas_call | solution.py:260
  (26 shorter events, 1.1 us)
Async XLA Ops:
  3.8 2.1 %collective-permute-start = (f32[2,384,128]{2,1,0:T(8,128)S(1)}, f32[2,384,128]{2,1,0:T(8,128)S(1)}, u32[]{:S(2)}, u32[]{:S(2)}) collective-permute-start(f32[2,384,128]{2,1,0:T(8,128)S(1)} %get-tuple-element.59), channel_id=1, source_target_pairs={{0,8},{8,0},{16,24},{24,16},{1,9},{9,1},{17,25},{25,17},{2,10},{10... | collective-permute-start | bytes 1179656 | tf_op jit(solution)/shard_map/lead/ppermute | solution.py:300
  5.9 6.8 %collective-permute-start.1 = (f32[2,3,384,128]{3,2,1,0:T(8,128)S(1)}, f32[2,3,384,128]{3,2,1,0:T(8,128)S(1)}, u32[]{:S(2)}, u32[]{:S(2)}) collective-permute-start(f32[2,3,384,128]{3,2,1,0:T(8,128)S(1)} %get-tuple-element.71), channel_id=1, source_target_pairs={{0,8},{8,0},{16,24},{24,16},{1,9},{9,1},{17,25},{25,17},{2,10},{10... | collective-permute-start | bytes 3538952 | tf_op jit(solution)/shard_map/rest/ppermute | solution.py:300
  6.3 6.4 %collective-permute-start.2 = (f32[384,128]{1,0:T(8,128)S(1)}, f32[384,128]{1,0:T(8,128)S(1)}, u32[]{:S(2)}, u32[]{:S(2)}) collective-permute-start(f32[384,128]{1,0:T(8,128)S(1)} %get-tuple-element.73), channel_id=1, source_target_pairs={{0,16},{16,0},{8,24},{24,8},{1,17},{17,1},{9,25},{25,9},{2,18},{18... | collective-permute-start | bytes 589832 | tf_op jit(solution)/shard_map/chip0/ppermute | solution.py:300
  7.6 9.4 %collective-permute-start.5 = (f32[384,128]{1,0:T(8,128)S(1)}, f32[384,128]{1,0:T(8,128)S(1)}, u32[]{:S(2)}, u32[]{:S(2)}) collective-permute-start(f32[384,128]{1,0:T(8,128)S(1)} %get-tuple-element.91), channel_id=1, source_target_pairs={{0,16},{16,0},{8,24},{24,8},{1,17},{17,1},{9,25},{25,9},{2,18},{18... | collective-permute-start | bytes 589832 | tf_op jit(solution)/shard_map/chip1/ppermute | solution.py:300
  12.8 4.8 %collective-permute-start.3 = (f32[384,128]{1,0:T(8,128)S(1)}, f32[384,128]{1,0:T(8,128)S(1)}, u32[]{:S(2)}, u32[]{:S(2)}) collective-permute-start(f32[384,128]{1,0:T(8,128)S(1)} %add.18), channel_id=1, source_target_pairs={{0,2},{1,3},{8,10},{9,11},{16,18},{17,19},{24,26},{25,27}} | collective-permute-start | bytes 589832 | tf_op jit(solution)/shard_map/hop0_0/ppermute | solution.py:300
  17.0 1.4 %collective-permute-start.6 = (f32[384,128]{1,0:T(8,128)S(1)}, f32[384,128]{1,0:T(8,128)S(1)}, u32[]{:S(2)}, u32[]{:S(2)}) collective-permute-start(f32[384,128]{1,0:T(8,128)S(1)} %add.20), channel_id=1, source_target_pairs={{0,2},{1,3},{8,10},{9,11},{16,18},{17,19},{24,26},{25,27}} | collective-permute-start | bytes 589832 | tf_op jit(solution)/shard_map/hop0_1/ppermute | solution.py:300
  17.7 4.7 %collective-permute-start.4 = (f32[384,128]{1,0:T(8,128)S(1)}, f32[384,128]{1,0:T(8,128)S(1)}, u32[]{:S(2)}, u32[]{:S(2)}) collective-permute-start(f32[384,128]{1,0:T(8,128)S(1)} %add.19), channel_id=1, source_target_pairs={{2,4},{3,5},{10,12},{11,13},{18,20},{19,21},{26,28},{27,29}} | collective-permute-start | bytes 589832 | tf_op jit(solution)/shard_map/hop1_0/ppermute | solution.py:300
  18.4 5.3 %collective-permute-start.7 = (f32[384,128]{1,0:T(8,128)S(1)}, f32[384,128]{1,0:T(8,128)S(1)}, u32[]{:S(2)}, u32[]{:S(2)}) collective-permute-start(f32[384,128]{1,0:T(8,128)S(1)} %add.21), channel_id=1, source_target_pairs={{2,4},{3,5},{10,12},{11,13},{18,20},{19,21},{26,28},{27,29}} | collective-permute-start | bytes 589832 | tf_op jit(solution)/shard_map/hop1_1/ppermute | solution.py:300
  22.3 17.5 %copy-start = (f32[3072]{0:T(1024)S(1)}, f32[3072]{0:T(1024)}, u32[]{:S(2)}) copy-start(f32[3072]{0:T(1024)} %param.7) | copy-start | bytes 36868
  22.4 6.4 %collective-permute-start.10 = (f32[384,128]{1,0:T(8,128)S(1)}, f32[384,128]{1,0:T(8,128)S(1)}, u32[]{:S(2)}, u32[]{:S(2)}) collective-permute-start(f32[384,128]{1,0:T(8,128)S(1)} %add.23), channel_id=1, source_target_pairs={{4,6},{5,7},{12,14},{13,15},{20,22},{21,23},{28,30},{29,31}} | collective-permute-start | bytes 589832 | tf_op jit(solution)/shard_map/hop2_0/ppermute | solution.py:300
  23.7 11.0 %collective-permute-start.8 = (f32[384,128]{1,0:T(8,128)S(1)}, f32[384,128]{1,0:T(8,128)S(1)}, u32[]{:S(2)}, u32[]{:S(2)}) collective-permute-start(f32[384,128]{1,0:T(8,128)S(1)} %add.22), channel_id=1, source_target_pairs={{4,6},{5,7},{12,14},{13,15},{20,22},{21,23},{28,30},{29,31}} | collective-permute-start | bytes 589832 | tf_op jit(solution)/shard_map/hop2_1/ppermute | solution.py:300
  28.9 9.9 %collective-permute-start.11 = (f32[384,128]{1,0:T(8,128)S(1)}, f32[384,128]{1,0:T(8,128)S(1)}, u32[]{:S(2)}, u32[]{:S(2)}) collective-permute-start(f32[384,128]{1,0:T(8,128)S(1)} %get-tuple-element.99), channel_id=1, source_target_pairs={{0,16},{16,0},{8,24},{24,8},{1,17},{17,1},{9,25},{25,9},{2,18},{18... | collective-permute-start | bytes 589832 | tf_op jit(solution)/shard_map/chipback0/ppermute | solution.py:300
  30.1 9.7 %collective-permute-start.12 = (f32[384,128]{1,0:T(8,128)S(1)}, f32[384,128]{1,0:T(8,128)S(1)}, u32[]{:S(2)}, u32[]{:S(2)}) collective-permute-start(f32[384,128]{1,0:T(8,128)S(1)} %get-tuple-element.96.refs_2_), channel_id=1, source_target_pairs={{0,8},{8,0},{16,24},{24,16},{1,9},{9,1},{17,25},{25,17},{2,10},{10... | collective-permute-start | bytes 589832 | tf_op jit(solution)/shard_map/near0/ppermute | solution.py:300
  34.8 6.7 %collective-permute-start.9 = (f32[384,128]{1,0:T(8,128)S(1)}, f32[384,128]{1,0:T(8,128)S(1)}, u32[]{:S(2)}, u32[]{:S(2)}) collective-permute-start(f32[384,128]{1,0:T(8,128)S(1)} %get-tuple-element.92), channel_id=1, source_target_pairs={{0,16},{16,0},{8,24},{24,8},{1,17},{17,1},{9,25},{25,9},{2,18},{18... | collective-permute-start | bytes 589832 | tf_op jit(solution)/shard_map/chipback1/ppermute | solution.py:300
  35.6 7.6 %collective-permute-start.15 = (f32[384,128]{1,0:T(8,128)S(1)}, f32[384,128]{1,0:T(8,128)S(1)}, u32[]{:S(2)}, u32[]{:S(2)}) collective-permute-start(f32[384,128]{1,0:T(8,128)S(1)} %get-tuple-element.105.refs_6_), channel_id=1, source_target_pairs={{0,8},{8,0},{16,24},{24,16},{1,9},{9,1},{17,25},{25,17},{2,10},{10... | collective-permute-start | bytes 589832 | tf_op jit(solution)/shard_map/near1/ppermute | solution.py:300
  38.8 4.4 %collective-permute-start.14 = (f32[384,128]{1,0:T(8,128)S(1)}, f32[384,128]{1,0:T(8,128)S(1)}, u32[]{:S(2)}, u32[]{:S(2)}) collective-permute-start(f32[384,128]{1,0:T(8,128)S(1)} %collective-permute-done.11.refs_6_), channel_id=1, source_target_pairs={{0,8},{8,0},{16,24},{24,16},{1,9},{9,1},{17,25},{25,17},{2,10},{10... | collective-permute-start | bytes 589832 | tf_op jit(solution)/shard_map/far0/ppermute | solution.py:300
  41.6 3.6 %collective-permute-start.13 = (f32[384,128]{1,0:T(8,128)S(1)}, f32[384,128]{1,0:T(8,128)S(1)}, u32[]{:S(2)}, u32[]{:S(2)}) collective-permute-start(f32[384,128]{1,0:T(8,128)S(1)} %collective-permute-done.9.refs_10_), channel_id=1, source_target_pairs={{0,8},{8,0},{16,24},{24,16},{1,9},{9,1},{17,25},{25,17},{2,10},{10... | collective-permute-start | bytes 589832 | tf_op jit(solution)/shard_map/far1/ppermute | solution.py:300
